TPU v7x, 256 devices: a whole 4x4x8 slice. The times are simulated.
256 devices in a mesh: dp: 16 (over x_hi, y, core), tensor: 16 (over x_lo, z).
Axes of the slice: x: 4 (x_hi: 2, x_lo: 2; x = x_hi * 2 + x_lo), y: 4, z: 8, core: 2. Of those that a mesh axis runs over, the one named last changes fastest.
Arguments:
- stored_layer_input: bfloat16 [8192, 4096], P('dp', 'tensor'), may hold values from -6 to 6
- saved_up_output: bfloat16 [8192, 14336], P('dp', 'tensor'), may hold values from -6 to 6
- hidden_gradient: bfloat16 [8192, 14336], P('dp', 'tensor'), may hold values from -6 to 6
- frozen_gate_weight: bfloat16 [4096, 14336], P(None, 'tensor'), may hold values from -1 to 1, as said below
- lowrank_down: bfloat16 [4096, 64], replicated, may hold values from -0.09375 to 0.09375
- lowrank_up: bfloat16 [64, 14336], P(None, 'tensor'), may hold values from -0.75 to 0.75
- magnitude: float32 [14336], P('tensor'), may hold values from 0.5 to 4
Outputs:
- layer_input_gradient: bfloat16 [8192, 4096], P('dp', 'tensor')
- up_output_gradient: bfloat16 [8192, 14336], P('dp', 'tensor')
- lowrank_down_gradient: float32 [4096, 64], P('tensor')
- lowrank_up_gradient: float32 [64, 14336], P(None, 'tensor')
- magnitude_gradient: float32 [14336], P('tensor')
Inputs may be any that keep to these rules, and one draw needn't show every extreme that they name: `frozen_gate_weight`: frozen base weights.
All inputs are finite; a program needn't handle non-finite values.
Results may differ from a plain program's by a relative error of at most 0.007.
Values may be sent and summed in bfloat16 or wider, within the bound.
No kernel may reach another device: no remote copies, remote signals or barrier semaphores. Data moves between devices by JAX's collectives and lax.ppermute only.
A program may use at most 128 MiB of HBM per device.

v0:
```python
import math

import jax
import jax.numpy as jnp
from jax import lax
from jax.sharding import PartitionSpec as P

epsilon = 1e-06


def contract(left, right, left_dim, right_dim):
    return lax.dot_general(
        left, right, (((left_dim,), (right_dim,)), ((), ())), preferred_element_type=jnp.float32
    )


def split_product(left, right):
    high_part = right.astype(jnp.bfloat16)
    low_part = (right - high_part.astype(jnp.float32)).astype(jnp.bfloat16)
    return contract(left, high_part, 0, 0) + contract(left, low_part, 0, 0)


def per_device(
    stored_layer_input,
    saved_up_output,
    hidden_gradient,
    frozen_gate_weight,
    lowrank_down,
    lowrank_up,
    magnitude,
):
    tensor_rank = lax.axis_index("tensor")
    own_width = stored_layer_input.shape[1]
    tok_rows = stored_layer_input.shape[0]
    scaling_factor = 1.0 / math.sqrt(tok_rows * lax.axis_size("dp"))
    combined_weight_matrix = frozen_gate_weight.astype(jnp.float32) + contract(
        lowrank_down, lowrank_up, 1, 0
    )
    col_norms = jnp.sqrt(jnp.sum(combined_weight_matrix * combined_weight_matrix, axis=0) + epsilon)
    scales = magnitude / col_norms
    merged = combined_weight_matrix.astype(jnp.bfloat16)
    input_features = lax.all_gather(stored_layer_input, "tensor", axis=1, tiled=True)
    gate_pre = contract(input_features, merged, 1, 0)
    gate_out = gate_pre * scales
    gate_sig = jax.nn.sigmoid(gate_out)
    cotangent = hidden_gradient.astype(jnp.float32)
    up_output_gradient = (cotangent * gate_out * gate_sig).astype(jnp.bfloat16)
    gate_grad = (
        cotangent
        * saved_up_output.astype(jnp.float32)
        * gate_sig
        * (1.0 + gate_out * (1.0 - gate_sig))
    )
    magnitude_piece = jnp.sum(gate_grad * gate_pre, axis=0) / col_norms * scaling_factor
    scaled_gradient = (gate_grad * scales).astype(jnp.bfloat16)
    offset = tensor_rank * own_width
    feature_part = lax.psum_scatter(
        contract(merged, scaled_gradient, 1, 1), "tensor", scatter_dimension=0, tiled=True
    )
    partial_value = jnp.transpose(feature_part)
    layer_input_gradient = partial_value.astype(jnp.bfloat16)
    lowrank_latent = contract(input_features, lowrank_down, 1, 0)
    lowrank_query = contract(scaled_gradient, lowrank_up, 1, 1)
    latent_high = lowrank_latent.astype(jnp.bfloat16)
    latent_rest = (lowrank_latent - latent_high.astype(jnp.float32)).astype(jnp.bfloat16)
    up_piece = contract(latent_high, scaled_gradient, 0, 0)
    up_piece = (up_piece + contract(latent_rest, scaled_gradient, 0, 0)) * scaling_factor
    down_whole = split_product(input_features, lowrank_query) * scaling_factor
    down_summed = lax.psum(down_whole, ("dp", "tensor"))
    lowrank_down_gradient = lax.dynamic_slice_in_dim(down_summed, offset, own_width, 0)
    lowrank_up_gradient, magnitude_gradient = lax.psum((up_piece, magnitude_piece), "dp")
    return (
        layer_input_gradient,
        up_output_gradient,
        lowrank_down_gradient,
        lowrank_up_gradient,
        magnitude_gradient,
    )


def solution(mesh):
    return jax.shard_map(
        per_device,
        mesh=mesh,
        in_specs=(
            P("dp", "tensor"),
            P("dp", "tensor"),
            P("dp", "tensor"),
            P(None, "tensor"),
            P(),
            P(None, "tensor"),
            P("tensor"),
        ),
        out_specs=(
            P("dp", "tensor"),
            P("dp", "tensor"),
            P("tensor", None),
            P(None, "tensor"),
            P("tensor"),
        ),
        check_vma=False,
    )
```

profile of v0, /device:TPU:1, one launch (start us, length us, event | category | flops | bytes accessed | tf_op | source)
XLA Modules:
  0.0 627.5 jit_solution(3921881000895234386)
XLA Ops:
  7.2 0.0 all-gather.2.cloned.1.call-start
  7.2 0.7 all-gather.2.cloned.1.call-update
  7.9 0.0 all-reduce.3.cloned.1.call-start
  8.0 0.2 copy-done
  8.2 8.6 %multiply_reduce_fusion = (f32[896]{0:T(1024)S(1)}, f32[4096,896]{1,0:T(8,128)}) fusion(bf16[4096,896]{1,0:T(8,128)(2,1)} %param.10, bf16[4096,64]{0,1:T(8,128)(2,1)S(1)} %copy-done, bf16[64,896]{1,0:T(8,128)(2,1)} %param.12), kind=kOutput, calls=%fused_computation | convolution fusion | flops 484441216 | bytes 22662656 | tf_op jit(solution)/shard_map/dot_general | solution.py:12
  16.8 76.5 %all-gather.2.cloned.1.call-done = bf16[512,4096]{1,0:T(8,128)(2,1)} async-done(((bf16[512,256]{1,0:T(8,128)(2,1)}), bf16[512,4096]{1,0:T(8,128)(2,1)}) %all-gather.2.cloned.1.call-update) | async-done | bytes 4194320 | tf_op jit(solution)/shard_map/all_gather | solution.py:42
  93.3 15.0 %fusion.7 = (f32[896]{0:T(1024)S(1)}, bf16[512,896]{1,0:T(8,128)(2,1)S(1)}, bf16[512,896]{1,0:T(8,128)(2,1)}) fusion(f32[896]{0:T(1024)S(1)} %fusion.15, bf16[512,896]{1,0:T(8,128)(2,1)S(1)} %copy-done.4, bf16[512,896]{1,0:T(8,128)(2,1)S(1)} %copy-done.5, bf16[512,4096]{1,0:T(8,128)(2,1)} %all-gather.2.cloned.1.call-done, ...), kind=kOutput, calls=%fused_computation.14 | convolution fusion | flops 3777821696 | bytes 29891584 | tf_op jit(solution)/shard_map/dot_general | solution.py:12
  108.3 0.4 fusion.20
  108.7 0.8 fusion.13
  109.6 1.8 fusion.2
  111.4 0.0 reduce-scatter.2.cloned.1.call-start
  111.5 14.2 %fusion.16 = f32[4096,512]{1,0:T(8,128)} fusion(bf16[512,896]{1,0:T(8,128)(2,1)S(1)} %get-tuple-element.11, f32[4096,896]{1,0:T(8,128)} %get-tuple-element.14, bf16[4096,896]{1,0:T(8,128)(2,1)} %param.10), kind=kOutput, calls=%fused_computation.32 | convolution fusion | flops 3769106432 | bytes 31326208 | tf_op jit(solution)/shard_map/dot_general | solution.py:12
  125.7 0.0 all-reduce.5.cloned.1.call-start
  125.7 43.0 %psum.23 = f32[896]{0:T(1024)} all-reduce(f32[896]{0:T(1024)S(1)} %divide_multiply_fusion), channel_id=1, replica_groups=mesh['dp'=16,'tensor'=16] {'dp'}, use_global_device_ids=true, to_apply=%region_5.0 | all-reduce | flops 896 | bytes 7168 | tf_op jit(solution)/shard_map/psum | solution.py:71
  168.7 3.6 fusion.21
  172.3 0.3 fusion.10
  172.6 1.0 fusion.8
  173.6 201.5 %all-reduce.3.cloned.1.call-done = f32[4096,64]{0,1:T(8,128)} async-done(((f32[4096,64]{0,1:T(8,128)}), f32[4096,64]{0,1:T(8,128)}) %all-reduce.3.cloned.1.call-update) | async-done | bytes 1048592 | tf_op jit(solution)/shard_map/psum | solution.py:69
  375.1 1.5 constant_dynamic-slice_fusion
  376.6 102.7 %reduce-scatter.2.cloned.1.call-done = f32[256,512]{1,0:T(8,128)} async-done(((f32[4096,512]{1,0:T(8,128)}), f32[256,512]{1,0:T(8,128)}) %reduce-scatter.2.cloned.1.call-update) | async-done | bytes 524304 | tf_op jit(solution)/shard_map/reduce_scatter | solution.py:57
  479.3 1.1 convert_bitcast_fusion
  480.3 0.8 copy.12
  481.2 138.1 %all-reduce.5.cloned.1.call-done = f32[64,896]{1,0:T(8,128)} async-done(((f32[64,896]{1,0:T(8,128)}), f32[64,896]{1,0:T(8,128)}) %all-reduce.5.cloned.1.call-update) | async-done | bytes 229392 | tf_op jit(solution)/shard_map/psum | solution.py:71
  619.3 1.6 copy.15
  (16 shorter events, 0.1 us)
Async XLA Ops:
  7.2 1.0 copy-start
  7.2 86.1 %all-gather.2.cloned.1.call-start = ((), (), s32[]{:S(2)}) async-start(), calls=%async_computation.1 | async-start | bytes 4456448 | tf_op jit(solution)/shard_map/all_gather | solution.py:42
  7.9 8.9 %copy-start.3 = (f32[896]{0:T(1024)S(1)}, f32[896]{0:T(1024)}, u32[]{:S(2)}) copy-start(f32[896]{0:T(1024)} %param.13) | copy-start | bytes 10756
  7.9 85.4 %copy-start.4 = (bf16[512,896]{1,0:T(8,128)(2,1)S(1)}, bf16[512,896]{1,0:T(8,128)(2,1)}, u32[]{:S(2)}) copy-start(bf16[512,896]{1,0:T(8,128)(2,1)} %param.8) | copy-start | bytes 2752516
  7.9 85.4 %copy-start.5 = (bf16[512,896]{1,0:T(8,128)(2,1)S(1)}, bf16[512,896]{1,0:T(8,128)(2,1)}, u32[]{:S(2)}) copy-start(bf16[512,896]{1,0:T(8,128)(2,1)} %param.9) | copy-start | bytes 2752516
  7.9 367.2 %all-reduce.3.cloned.1.call-start = ((), (), s32[]{:S(2)}) async-start(), calls=%async_computation.3 | async-start | bytes 2097152 | tf_op jit(solution)/shard_map/psum | solution.py:69
  93.3 15.0 %copy-start.2 = (bf16[64,896]{1,0:T(8,128)(2,1)S(1)}, bf16[64,896]{1,0:T(8,128)(2,1)}, u32[]{:S(2)}) copy-start(bf16[64,896]{1,0:T(8,128)(2,1)} %param.12) | copy-start | bytes 344068
  93.3 15.4 %copy-start.1 = (bf16[512,4096]{1,0:T(8,128)(2,1)S(1)}, bf16[512,4096]{1,0:T(8,128)(2,1)}, u32[]{:S(2)}) copy-start(bf16[512,4096]{1,0:T(8,128)(2,1)} %all-gather.2.cloned.1.call-done) | copy-start | bytes 12582916
  111.4 367.8 %reduce-scatter.2.cloned.1.call-start = ((), (), s32[]{:S(2)}) async-start(), calls=%async_computation.2 | async-start | bytes 8912896 | tf_op jit(solution)/shard_map/reduce_scatter | solution.py:57
  125.7 493.7 %all-reduce.5.cloned.1.call-start = ((), (), s32[]{:S(2)}) async-start(), calls=%async_computation.4 | async-start | bytes 458752 | tf_op jit(solution)/shard_map/psum | solution.py:71
Sparse Core Ops, SparseCore 0:
  9.7 83.5 all-gather.1
  111.6 263.5 all-reduce.2
  377.9 101.3 reduce-scatter.1
  482.5 136.7 all-reduce.4
where the time goes:
time: 629 us; the launch traced here: 627 us
  waiting for transfers between devices  520 us (83%)
  matrix products  45.7 us (7%)
  blocking collectives  43 us (7%)
  between operations  13.8 us (2%)
    psum x1, waiting for transfers between devices, per_device(): down_summed = lax.psum(down_whole, ('dp', 'tensor'))  202 us
    psum x1, waiting for transfers between devices, per_device(): lax.psum((up_piece, magnitude_piece), 'dp')  138 us
    reduce_scatter x1, waiting for transfers between devices, per_device(): lax.psum_scatter(contract(merged, scaled_gradient, 1, 1), 'tensor', scatt...  103 us
    all_gather x1, waiting for transfers between devices, per_device(): lax.all_gather(stored_layer_input, 'tensor', axis=1, tiled=True)  76.5 us
    dot_general x9, matrix products, contract(): lax.dot_general(left, right, (((left_dim,), (right_dim,)), ((), ())), pre...  45.7 us
    psum x1, blocking collectives, per_device(): lax.psum((up_piece, magnitude_piece), 'dp')  43 us
  transfers between devices with their start and end apart: 4, of which 4 were waited for; matrix products, arithmetic and copies ran while one was open for 5% of the time, Pallas kernels for 0%

commit v1 on v0

v1 whole, which is shorter than its diff:
```python
import functools
import math

import jax
import jax.numpy as jnp
from jax import lax
from jax.experimental import pallas as pl
from jax.experimental.pallas import tpu as pltpu
from jax.sharding import PartitionSpec as P

EPSILON = 1e-06
RING = 8
PAIR = 2

EARLY = (
    (0, 0),
    (0, -1), (0, 1), (1, 0),
    (0, -2), (0, 2), (1, -1),
    (0, -3), (0, 3), (1, 1),
    (0, 4), (1, 2), (1, -2),
)
LATE = ((1, -3), (1, 3), (1, 4))
FIRST_OUT = ((1, 4), (1, -3), (1, 3))
REST_OUT = (
    (0, 4), (1, 2), (1, -2), (0, -3), (0, 3), (1, 1), (0, -2), (0, 2), (1, -1),
    (0, -1), (0, 1), (1, 0), (0, 0),
)

ANY = pl.BlockSpec(memory_space=pl.ANY)
VMEM = pl.BlockSpec(memory_space=pltpu.VMEM)
SMEM = pl.BlockSpec(memory_space=pltpu.SMEM)


def ring_perm(step):
    return [
        (pair * RING + at, pair * RING + (at + step) % RING)
        for pair in range(PAIR)
        for at in range(RING)
    ]


def ring_xor(bit):
    return [
        (pair * RING + at, pair * RING + (at ^ bit)) for pair in range(PAIR) for at in range(RING)
    ]


def flip_perm(bit):
    return [(at, at ^ bit) for at in range(16)]


def up_ring(array):
    return lax.ppermute(array, "tensor", ring_perm(1))


def down_ring(array):
    return lax.ppermute(array, "tensor", ring_perm(-1))


def across(array):
    return lax.ppermute(array, "tensor", flip_perm(RING))


def dot(left, right, left_dim, right_dim):
    return lax.dot_general(
        left, right, (((left_dim,), (right_dim,)), ((), ())), preferred_element_type=jnp.float32
    )


def row_of(rank, offset, height):
    pair, ring = offset
    own_pair, own_ring = rank // RING, rank % RING
    other = own_pair if pair == 0 else 1 - own_pair
    block = other * RING + (own_ring + ring + RING) % RING
    return pl.multiple_of(block * height, height)


def merge_kernel(weight_ref, down_ref, up_ref, merged_ref, square_ref):
    wide = weight_ref[...].astype(jnp.float32) + dot(down_ref[...], up_ref[...], 1, 0)
    width = wide.shape[1]
    merged_ref[:, :width] = wide.astype(jnp.bfloat16)
    merged_ref[:, width:] = jnp.concatenate(
        [down_ref[...], jnp.zeros_like(down_ref)], axis=1
    )
    part = jnp.sum(wide * wide, axis=0, keepdims=True)

    @pl.when(pl.program_id(0) == 0)
    def _():
        square_ref[...] = part

    @pl.when(pl.program_id(0) != 0)
    def _():
        square_ref[...] += part


def merge(weight, lowrank_down, lowrank_up):
    depth, width = weight.shape
    rank = lowrank_down.shape[1]
    rows = 512
    return pl.pallas_call(
        merge_kernel,
        grid=(depth // rows,),
        in_specs=[
            pl.BlockSpec((rows, width), lambda i: (i, 0)),
            pl.BlockSpec((rows, rank), lambda i: (i, 0)),
            pl.BlockSpec((rank, width), lambda i: (0, 0)),
        ],
        out_specs=[
            pl.BlockSpec((rows, width + 2 * rank), lambda i: (i, 0)),
            pl.BlockSpec((1, width), lambda i: (0, 0)),
        ],
        out_shape=[
            jax.ShapeDtypeStruct((depth, width + 2 * rank), jnp.bfloat16),
            jax.ShapeDtypeStruct((1, width), jnp.float32),
        ],
        compiler_params=pltpu.CompilerParams(vmem_limit_bytes=32 * 2**20),
        cost_estimate=pl.CostEstimate(
            flops=2 * depth * width * rank, bytes_accessed=4 * depth * width, transcendentals=0
        ),
        name="merge",
    )(weight, lowrank_down, lowrank_up)


def gate_early_kernel(count, rank_ref, *refs):
    blocks, merged_ref, total_ref, held, rows, sems = (
        refs[:count], refs[count], refs[count + 1], refs[count + 2], refs[count + 3], refs[count + 4]
    )
    rank = rank_ref[0]
    height = held.shape[2]
    copies = []
    for at, offset in enumerate(EARLY):
        pair = (
            pltpu.make_async_copy(blocks[at], held.at[at], sems.at[at, 0]),
            pltpu.make_async_copy(
                merged_ref.at[pl.ds(row_of(rank, offset, height), height)],
                rows.at[at],
                sems.at[at, 1],
            ),
        )
        for copy in pair:
            copy.start()
        copies.append(pair)
    for at in range(count):
        for copy in copies[at]:
            copy.wait()
        part = dot(held[at], rows[at], 1, 0)
        if at == 0:
            total_ref[...] = part
        else:
            total_ref[...] += part


def gate_early(rank, blocks, merged):
    tokens, height = blocks[0].shape
    wide = merged.shape[1]
    count = len(blocks)
    return pl.pallas_call(
        functools.partial(gate_early_kernel, count),
        in_specs=[SMEM] + [ANY] * (count + 1),
        out_specs=VMEM,
        out_shape=jax.ShapeDtypeStruct((tokens, wide), jnp.float32),
        scratch_shapes=[
            pltpu.VMEM((count, tokens, height), jnp.bfloat16),
            pltpu.VMEM((count, height, wide), jnp.bfloat16),
            pltpu.SemaphoreType.DMA((count, 2)),
        ],
        compiler_params=pltpu.CompilerParams(vmem_limit_bytes=40 * 2**20),
        cost_estimate=pl.CostEstimate(
            flops=2 * tokens * height * wide * count,
            bytes_accessed=count * height * (wide + tokens) * 2 + tokens * wide * 4,
            transcendentals=0,
        ),
        name="gate_early",
    )(rank, *blocks, merged)


def gate_late_kernel(
    factor,
    rank_ref,
    late_a,
    late_b,
    late_c,
    merged_ref,
    total_ref,
    square_ref,
    magnitude_ref,
    hidden_ref,
    saved_ref,
    lowrank_up_ref,
    up_out_ref,
    scaled_ref,
    query_ref,
    up_piece_ref,
    magnitude_piece_ref,
    first_a,
    first_b,
    first_c,
    held,
    rows,
    out_rows,
    sems,
):
    rank = rank_ref[0]
    height = held.shape[2]
    width = hidden_ref.shape[1]
    low = lowrank_up_ref.shape[0]
    copies = []
    for at, (block, offset) in enumerate(zip((late_a, late_b, late_c), LATE)):
        pair = (
            pltpu.make_async_copy(block, held.at[at], sems.at[at, 0]),
            pltpu.make_async_copy(
                merged_ref.at[pl.ds(row_of(rank, offset, height), height)],
                rows.at[at],
                sems.at[at, 1],
            ),
        )
        for copy in pair:
            copy.start()
        copies.append(pair)
    out_copies = []
    for at, offset in enumerate(FIRST_OUT):
        copy = pltpu.make_async_copy(
            merged_ref.at[pl.ds(row_of(rank, offset, height), height)],
            out_rows.at[at],
            sems.at[at, 2],
        )
        copy.start()
        out_copies.append(copy)
    for at in range(len(LATE)):
        for copy in copies[at]:
            copy.wait()
    norms = jnp.sqrt(square_ref[...] + EPSILON)
    scales = magnitude_ref[...] / norms
    tokens = hidden_ref.shape[0]
    tile = 128

    magnitude_piece_ref[...] = jnp.zeros_like(magnitude_piece_ref)
    up_piece_ref[...] = jnp.zeros_like(up_piece_ref)

    @pl.loop(0, tokens // tile)
    def _(step):
        here = pl.ds(pl.multiple_of(step * tile, tile), tile)
        total = total_ref[here, :]
        for at in range(len(LATE)):
            total += dot(held[at, here, :], rows[at], 1, 0)
        gate_pre = total[:, :width]
        latent = total[:, width : width + low]
        gate_out = gate_pre * scales
        gate_sig = 1.0 / (1.0 + jnp.exp(-gate_out))
        cotangent = hidden_ref[here, :].astype(jnp.float32)
        up_out_ref[here, :] = (cotangent * gate_out * gate_sig).astype(jnp.bfloat16)
        gate_grad = (
            cotangent
            * saved_ref[here, :].astype(jnp.float32)
            * gate_sig
            * (1.0 + gate_out * (1.0 - gate_sig))
        )
        magnitude_piece_ref[...] += jnp.sum(gate_grad * gate_pre, axis=0, keepdims=True)
        scaled = (gate_grad * scales).astype(jnp.bfloat16)
        scaled_ref[here, :] = scaled
        latent_high = latent.astype(jnp.bfloat16)
        latent_rest = (latent - latent_high.astype(jnp.float32)).astype(jnp.bfloat16)
        up_piece_ref[...] += dot(latent_high, scaled, 0, 0) + dot(latent_rest, scaled, 0, 0)

    magnitude_piece_ref[...] = magnitude_piece_ref[...] / norms * factor
    up_piece_ref[...] = up_piece_ref[...] * factor
    for at, out in enumerate((first_a, first_b, first_c)):
        out_copies[at].wait()
        out[...] = dot(scaled_ref[...], out_rows[at][:, :width], 1, 1).astype(jnp.bfloat16)
    query_ref[...] = dot(lowrank_up_ref[...], scaled_ref[...], 1, 1).astype(jnp.bfloat16)


def gate_late(factor, rank, late, merged, total, square, magnitude, hidden, saved, lowrank_up):
    tokens, height = late[0].shape
    wide = merged.shape[1]
    width = hidden.shape[1]
    low = lowrank_up.shape[0]
    block = jax.ShapeDtypeStruct((tokens, height), jnp.bfloat16)
    return pl.pallas_call(
        functools.partial(gate_late_kernel, factor),
        in_specs=[SMEM] + [ANY] * 4 + [VMEM] * 6,
        out_specs=[VMEM] * 8,
        out_shape=[
            jax.ShapeDtypeStruct((tokens, width), jnp.bfloat16),
            jax.ShapeDtypeStruct((tokens, width), jnp.bfloat16),
            jax.ShapeDtypeStruct((low, tokens), jnp.bfloat16),
            jax.ShapeDtypeStruct((low, width), jnp.float32),
            jax.ShapeDtypeStruct((1, width), jnp.float32),
            block,
            block,
            block,
        ],
        scratch_shapes=[
            pltpu.VMEM((len(LATE), tokens, height), jnp.bfloat16),
            pltpu.VMEM((len(LATE), height, wide), jnp.bfloat16),
            pltpu.VMEM((len(LATE), height, wide), jnp.bfloat16),
            pltpu.SemaphoreType.DMA((len(LATE), 3)),
        ],
        compiler_params=pltpu.CompilerParams(vmem_limit_bytes=40 * 2**20),
        cost_estimate=pl.CostEstimate(
            flops=2 * tokens * height * wide * 7,
            bytes_accessed=16 * 2**20,
            transcendentals=2 * tokens * width,
        ),
        name="gate_late",
    )(rank, *late, merged, total, square, magnitude, hidden, saved, lowrank_up)


def rest_kernel(count, rank_ref, merged_ref, scaled_ref, *refs):
    outs, rows, sems = refs[:count], refs[count], refs[count + 1]
    rank = rank_ref[0]
    height = rows.shape[1]
    width = scaled_ref.shape[1]
    copies = []
    for at, offset in enumerate(REST_OUT):
        copy = pltpu.make_async_copy(
            merged_ref.at[pl.ds(row_of(rank, offset, height), height)], rows.at[at], sems.at[at]
        )
        copy.start()
        copies.append(copy)
    for at in range(count):
        copies[at].wait()
        outs[at][...] = dot(scaled_ref[...], rows[at][:, :width], 1, 1).astype(jnp.bfloat16)


def rest(rank, merged, scaled, height):
    tokens, width = scaled.shape
    wide = merged.shape[1]
    count = len(REST_OUT)
    return pl.pallas_call(
        functools.partial(rest_kernel, count),
        in_specs=[SMEM, ANY, VMEM],
        out_specs=[VMEM] * count,
        out_shape=[jax.ShapeDtypeStruct((tokens, height), jnp.bfloat16)] * count,
        scratch_shapes=[
            pltpu.VMEM((count, height, wide), jnp.bfloat16),
            pltpu.SemaphoreType.DMA((count,)),
        ],
        compiler_params=pltpu.CompilerParams(vmem_limit_bytes=40 * 2**20),
        cost_estimate=pl.CostEstimate(
            flops=2 * tokens * height * width * count,
            bytes_accessed=count * height * (wide + tokens) * 2,
            transcendentals=0,
        ),
        name="rest",
    )(rank, merged, scaled)


def payload_kernel(factor, query_ref, input_ref, up_ref, magnitude_ref, out_ref):
    query = query_ref[...]
    high = query.astype(jnp.bfloat16)
    rest_part = (query - high.astype(jnp.float32)).astype(jnp.bfloat16)
    low, width = up_ref.shape
    down = (dot(high, input_ref[...], 1, 0) + dot(rest_part, input_ref[...], 1, 0)) * factor
    out_ref[...] = jnp.zeros_like(out_ref)
    out_ref[:low, :width] = up_ref[...]
    out_ref[:low, width:] = down
    out_ref[low : low + 1, :width] = magnitude_ref[...]


def payload(factor, query, own, up_piece, magnitude_piece):
    low, width = up_piece.shape
    return pl.pallas_call(
        functools.partial(payload_kernel, factor),
        in_specs=[VMEM] * 4,
        out_specs=VMEM,
        out_shape=jax.ShapeDtypeStruct((low + 8, width + own.shape[1]), jnp.float32),
        cost_estimate=pl.CostEstimate(
            flops=4 * low * own.shape[0] * own.shape[1], bytes_accessed=2**20, transcendentals=0
        ),
        name="payload",
    )(query, own, up_piece, magnitude_piece)


def f32(array):
    return array.astype(jnp.float32)


def narrow(*arrays):
    total = f32(arrays[0])
    for array in arrays[1:]:
        total = total + f32(array)
    return total.astype(jnp.bfloat16)


def sum_small(array, perms, axis):
    for perm in perms:
        sent = lax.optimization_barrier(array.astype(jnp.bfloat16))
        array = f32(sent) + f32(lax.ppermute(sent, axis, perm))
    return array


def sum_payload(array, perms, low):
    array = array + lax.ppermute(array, "dp", flip_perm(1))
    for perm in perms:
        row = array[low : low + 1]
        high = lax.reduce_precision(row, 8, 7)
        pad = jnp.zeros((14, array.shape[1]), jnp.float32)
        sent = jnp.concatenate([array[:low], high, row - high, pad], axis=0).astype(jnp.bfloat16)
        sent = lax.optimization_barrier(sent)
        both = f32(sent) + f32(lax.ppermute(sent, "dp", perm))
        array = jnp.concatenate([both[:low], both[low : low + 1] + both[low + 1 : low + 2]], axis=0)
    return array


def per_device(
    stored_layer_input,
    saved_up_output,
    hidden_gradient,
    frozen_gate_weight,
    lowrank_down,
    lowrank_up,
    magnitude,
):
    own = stored_layer_input
    tokens, height = own.shape
    width = frozen_gate_weight.shape[1]
    low = lowrank_up.shape[0]
    factor = 1.0 / math.sqrt(tokens * lax.axis_size("dp"))
    rank = lax.axis_index("tensor").astype(jnp.int32).reshape(1)

    merged, square = merge(frozen_gate_weight, lowrank_down, lowrank_up)

    got = {(0, 0): own}
    got[0, -1], got[0, 1], got[1, 0] = up_ring(own), down_ring(own), across(own)
    got[0, -2], got[0, 2], got[1, -1] = (
        up_ring(got[0, -1]), down_ring(got[0, 1]), across(got[0, -1])
    )
    got[0, -3], got[0, 3], got[1, 1] = (
        up_ring(got[0, -2]), down_ring(got[0, 2]), across(got[0, 1])
    )
    got[0, 4], got[1, 2], got[1, -2] = (
        up_ring(got[0, -3]), down_ring(got[1, 1]), across(got[0, -2])
    )
    got[1, -3], got[1, 3], got[1, 4] = (
        up_ring(got[1, -2]), down_ring(got[1, 2]), across(got[0, 4])
    )

    total = gate_early(rank, [got[offset] for offset in EARLY], merged)
    up_output_gradient, scaled, query, up_piece, magnitude_piece, *first = gate_late(
        factor,
        rank,
        [got[offset] for offset in LATE],
        merged,
        total,
        square,
        magnitude.reshape(1, width),
        hidden_gradient,
        saved_up_output,
        lowrank_up,
    )
    part = dict(zip(FIRST_OUT, first))
    into_far, into_down, into_up = (
        across(part[1, 4]), down_ring(part[1, -3]), up_ring(part[1, 3])
    )
    part.update(zip(REST_OUT, rest(rank, merged, scaled, height)))
    in_a = down_ring(narrow(part[0, 4], into_far))
    in_b = up_ring(narrow(part[1, 2], into_up))
    in_c = across(narrow(part[1, -2], into_down))
    in_d = down_ring(narrow(part[0, -3], in_a))
    in_e = up_ring(part[0, 3])
    in_f = across(narrow(part[1, 1], in_b))
    in_g = down_ring(narrow(part[0, -2], in_c, in_d))
    in_h = up_ring(narrow(part[0, 2], in_e))
    in_i = across(part[1, -1])
    in_j = down_ring(narrow(part[0, -1], in_g, in_i))
    in_k = up_ring(narrow(part[0, 1], in_f, in_h))
    in_l = across(part[1, 0])
    layer_input_gradient = narrow(part[0, 0], in_j, in_k, in_l)

    query = sum_small(query, (flip_perm(RING), ring_xor(1), ring_xor(2), ring_xor(4)), "tensor")
    pieces = payload(factor, query, own, up_piece, magnitude_piece)
    summed = sum_payload(pieces, (flip_perm(2), flip_perm(4), flip_perm(8)), low)
    return (
        layer_input_gradient,
        up_output_gradient,
        jnp.transpose(summed[:low, width:]),
        summed[:low, :width],
        summed[low, :width],
    )


def solution(mesh):
    return jax.shard_map(
        per_device,
        mesh=mesh,
        in_specs=(
            P("dp", "tensor"),
            P("dp", "tensor"),
            P("dp", "tensor"),
            P(None, "tensor"),
            P(),
            P(None, "tensor"),
            P("tensor"),
        ),
        out_specs=(
            P("dp", "tensor"),
            P("dp", "tensor"),
            P("tensor", None),
            P(None, "tensor"),
            P("tensor"),
        ),
        check_vma=False,
    )
```

time: 629 us -> 148 us (0.24)
  the two profiles are of different devices: /device:TPU:1 before, /device:TPU:18 now
where the time goes in v1:
time: 148 us
  waiting for transfers between devices  52 us (35%)
  starting transfers between devices  45.8 us (31%)
  Pallas kernels  28.3 us (19%)
  local copies, waits for them, and re-layouts  11.9 us (8%)
  other arithmetic  8.64 us (6%)
    ppermute x10, waiting for transfers between devices, up_ring(): return lax.ppermute(array, 'tensor', ring_perm(1))  24.8 us
    ppermute x10, starting transfers between devices, down_ring(): return lax.ppermute(array, 'tensor', ring_perm(-1))  19.1 us
    ppermute x10, waiting for transfers between devices, down_ring(): return lax.ppermute(array, 'tensor', ring_perm(-1))  13.7 us
    pallas_call x1, Pallas kernels, rest(): pl.pallas_call(functools.partial(rest_kernel, count), in_specs=[SMEM, ANY...  9.84 us
    unnamed x23, local copies, waits for them, and re-layouts  9.71 us
    ppermute x10, starting transfers between devices, across(): return lax.ppermute(array, 'tensor', flip_perm(RING))  9.6 us
    pallas_call x1, Pallas kernels, gate_late(): pl.pallas_call(functools.partial(gate_late_kernel, factor), in_specs=[SME...  7.43 us
    ppermute x10, starting transfers between devices, up_ring(): return lax.ppermute(array, 'tensor', ring_perm(1))  7.38 us
  transfers between devices with their start and end apart: 38, of which 16 were waited for; matrix products, arithmetic and copies ran while one was open for 8% of the time, Pallas kernels for 14%

profile of v1, /device:TPU:18, one launch (start us, length us, event | category | flops | bytes accessed | tf_op | source)
XLA Modules:
  0.0 147.7 jit_solution(5553985006497005503)
XLA Ops:
  2.6 4.0 %collective-permute-start.4 = (bf16[512,256]{1,0:T(8,128)(2,1)}, bf16[512,256]{1,0:T(8,128)(2,1)S(1)}, u32[]{:S(2)}, u32[]{:S(2)}) collective-permute-start(bf16[512,256]{1,0:T(8,128)(2,1)} %input_ref.1), channel_id=1, source_target_pairs={{0,7},{1,0},{2,1},{3,2},{4,3},{5,4},{6,5},{7,6},{8,15},{9,8},{10,9... | collective-permute-start | bytes 786440 | tf_op jit(solution)/shard_map/ppermute | solution.py:57
  6.7 6.4 %collective-permute-done.refs_1_ = bf16[512,256]{1,0:T(8,128)(2,1)S(1)} collective-permute-done((bf16[512,256]{1,0:T(8,128)(2,1)}, bf16[512,256]{1,0:T(8,128)(2,1)S(1)}, u32[]{:S(2)}, u32[]{:S(2)}) %collective-permute-start) | collective-permute-done | bytes 262176 | tf_op jit(solution)/shard_map/ppermute | solution.py:53
  13.6 8.2 %collective-permute-done.1.refs_4_ = bf16[512,256]{1,0:T(8,128)(2,1)S(1)} collective-permute-done((bf16[512,256]{1,0:T(8,128)(2,1)S(1)}, bf16[512,256]{1,0:T(8,128)(2,1)S(1)}, u32[]{:S(2)}, u32[]{:S(2)}) %collective-permute-start.1) | collective-permute-done | bytes 262176 | tf_op jit(solution)/shard_map/ppermute | solution.py:53
  22.3 3.2 %collective-permute-start.12 = (bf16[512,256]{1,0:T(8,128)(2,1)S(1)}, bf16[512,256]{1,0:T(8,128)(2,1)}, u32[]{:S(2)}, u32[]{:S(2)}) collective-permute-start(bf16[512,256]{1,0:T(8,128)(2,1)S(1)} %collective-permute-done.4.refs_2_), channel_id=1, source_target_pairs={{0,7},{1,0},{2,1},{3,2},{4,3},{5,4},{6,5},{7,6},{8,15},{9,8},{10,9... | collective-permute-start | bytes 786440 | tf_op jit(solution)/shard_map/ppermute | solution.py:57
  27.1 2.5 %collective-permute-done.8.refs_7_ = bf16[512,256]{1,0:T(8,128)(2,1)S(1)} collective-permute-done((bf16[512,256]{1,0:T(8,128)(2,1)S(1)}, bf16[512,256]{1,0:T(8,128)(2,1)S(1)}, u32[]{:S(2)}, u32[]{:S(2)}) %collective-permute-start.8) | collective-permute-done | bytes 262176 | tf_op jit(solution)/shard_map/ppermute | solution.py:53
  32.3 3.8 %collective-permute-start.14 = (bf16[512,256]{1,0:T(8,128)(2,1)}, bf16[512,256]{1,0:T(8,128)(2,1)}, u32[]{:S(2)}, u32[]{:S(2)}) collective-permute-start(bf16[512,256]{1,0:T(8,128)(2,1)} %collective-permute-done.12.refs_5_), channel_id=1, source_target_pairs={{0,7},{1,0},{2,1},{3,2},{4,3},{5,4},{6,5},{7,6},{8,15},{9,8},{10,9... | collective-permute-start | bytes 786440 | tf_op jit(solution)/shard_map/ppermute | solution.py:57
  38.4 3.1 %copy-done.2 = bf16[4096,896]{1,0:T(8,128)(2,1)S(1)} copy-done((bf16[4096,896]{1,0:T(8,128)(2,1)S(1)}, bf16[4096,896]{1,0:T(8,128)(2,1)}, u32[]{:S(2)}) %copy-start.2) | copy-done | bytes 7340056
  42.4 3.8 %merge.1 = (bf16[4096,1024]{1,0:T(8,128)(2,1)S(1)}, f32[1,896]{1,0:T(1,128)S(1)}) custom-call(bf16[4096,896]{1,0:T(8,128)(2,1)S(1)} %copy-done.2, bf16[4096,64]{1,0:T(8,128)(2,1)S(1)} %copy.12.down_ref, bf16[64,896]{1,0:T(8,128)(2,1)S(1)} %copy-done.6), custom_call_target="tpu_custom_call" | custom-call | flops 469762048 | bytes 14680064 | tf_op jit(solution)/shard_map/merge/pallas_call | solution.py:100
  46.4 3.2 %collective-permute-start.7 = (bf16[512,256]{1,0:T(8,128)(2,1)}, bf16[512,256]{1,0:T(8,128)(2,1)S(1)}, u32[]{:S(2)}, u32[]{:S(2)}) collective-permute-start(bf16[512,256]{1,0:T(8,128)(2,1)} %collective-permute-done.6.refs_11_), channel_id=1, source_target_pairs={{0,7},{1,0},{2,1},{3,2},{4,3},{5,4},{6,5},{7,6},{8,15},{9,8},{10,9... | collective-permute-start | bytes 786440 | tf_op jit(solution)/shard_map/ppermute | solution.py:57
  51.1 5.2 %gate_early.1.total_ref = f32[512,1024]{1,0:T(8,128)S(1)} custom-call(s32[1]{0:T(128)} %bitcast.rank_ref, bf16[512,256]{1,0:T(8,128)(2,1)S(1)} %copy-done.3, bf16[512,256]{1,0:T(8,128)(2,1)S(1)} %collective-permute-done.refs_1_, bf16[512,256]{1,0:T(8,128)(2,1)S(1)} %collective-permute-done.4.refs_2_, bf16[512,256]{1,0:T(8,128)(2,1)S(1)} %copy-done.8, ...), custom_call_target="tpu_custom_call" | custom-call | flops 3489660928 | bytes 12320768 | tf_op jit(solution)/shard_map/gate_early/pallas_call | solution.py:157
  56.4 7.4 %gate_late.1 = (bf16[512,896]{1,0:T(8,128)(2,1)}, bf16[512,896]{1,0:T(8,128)(2,1)S(1)}, bf16[64,512]{1,0:T(8,128)(2,1)S(1)}, f32[64,896]{1,0:T(8,128)S(1)}, f32[...) custom-call(s32[1]{0:T(128)} %bitcast.rank_ref, ...), custom_call_target="tpu_custom_call" | custom-call | flops 1879048192 | bytes 16777216 | tf_op jit(solution)/shard_map/gate_late/pallas_call | solution.py:279
  65.3 2.9 %collective-permute-done.30 = bf16[64,512]{1,0:T(8,128)(2,1)S(1)} collective-permute-done((bf16[64,512]{1,0:T(8,128)(2,1)S(1)}, bf16[64,512]{1,0:T(8,128)(2,1)S(1)}, u32[]{:S(2)}, u32[]{:S(2)}) %collective-permute-start.30) | collective-permute-done | bytes 65568 | tf_op jit(solution)/shard_map/ppermute | solution.py:389
  68.4 4.3 %collective-permute-done.31 = bf16[64,512]{1,0:T(8,128)(2,1)S(1)} collective-permute-done((bf16[64,512]{1,0:T(8,128)(2,1)S(1)}, bf16[64,512]{1,0:T(8,128)(2,1)S(1)}, u32[]{:S(2)}, u32[]{:S(2)}) %collective-permute-start.31) | collective-permute-done | bytes 65568 | tf_op jit(solution)/shard_map/ppermute | solution.py:389
  73.7 3.4 %copy-done.1 = bf16[4096,1024]{1,0:T(8,128)(2,1)S(1)} copy-done((bf16[4096,1024]{1,0:T(8,128)(2,1)S(1)}, bf16[4096,1024]{1,0:T(8,128)(2,1)}, u32[]{:S(2)}) %copy-start.1) | copy-done | bytes 8388632
  77.1 9.8 %rest.1 = (bf16[512,256]{1,0:T(8,128)(2,1)S(1)}, bf16[512,256]{1,0:T(8,128)(2,1)S(1)}, bf16[512,256]{1,0:T(8,128)(2,1)S(1)}, bf16[512,256]{1,0:T(8,128)(2,1)S(1)...) custom-call(s32[1]{0:T(128)} %bitcast.rank_ref, ...), custom_call_target="tpu_custom_call" | custom-call | flops 3053453312 | bytes 10223616 | tf_op jit(solution)/shard_map/rest/pallas_call | solution.py:330
  91.7 2.7 %collective-permute-start.15 = (bf16[512,256]{1,0:T(8,128)(2,1)S(1)}, bf16[512,256]{1,0:T(8,128)(2,1)S(1)}, u32[]{:S(2)}, u32[]{:S(2)}) collective-permute-start(bf16[512,256]{1,0:T(8,128)(2,1)S(1)} %get-tuple-element.35), channel_id=1, source_target_pairs={{0,7},{1,0},{2,1},{3,2},{4,3},{5,4},{6,5},{7,6},{8,15},{9,8},{10,9... | collective-permute-start | bytes 786440 | tf_op jit(solution)/shard_map/ppermute | solution.py:57
  94.4 2.9 %collective-permute-done.26 = bf16[512,256]{1,0:T(8,128)(2,1)S(1)} collective-permute-done((bf16[512,256]{1,0:T(8,128)(2,1)S(1)}, bf16[512,256]{1,0:T(8,128)(2,1)S(1)}, u32[]{:S(2)}, u32[]{:S(2)}) %collective-permute-start.26) | collective-permute-done | bytes 262176 | tf_op jit(solution)/shard_map/ppermute | solution.py:53
  97.3 3.2 %collective-permute-start.33 = (bf16[64,512]{1,0:T(8,128)(2,1)S(1)}, bf16[64,512]{1,0:T(8,128)(2,1)S(1)}, u32[]{:S(2)}, u32[]{:S(2)}) collective-permute-start(bf16[64,512]{1,0:T(8,128)(2,1)S(1)} %add_convert_fusion.10), channel_id=1, source_target_pairs={{0,4},{1,5},{2,6},{3,7},{4,0},{5,1},{6,2},{7,3},{8,12},{9,13},{10,... | collective-permute-start | bytes 196616 | tf_op jit(solution)/shard_map/ppermute | solution.py:389
  110.0 2.9 %collective-permute-done.24 = bf16[512,256]{1,0:T(8,128)(2,1)} collective-permute-done((bf16[512,256]{1,0:T(8,128)(2,1)}, bf16[512,256]{1,0:T(8,128)(2,1)}, u32[]{:S(2)}, u32[]{:S(2)}) %collective-permute-start.24) | collective-permute-done | bytes 262176 | tf_op jit(solution)/shard_map/ppermute | solution.py:53
  119.7 3.2 %collective-permute-done.35 = bf16[80,1152]{1,0:T(8,128)(2,1)S(1)} collective-permute-done((bf16[80,1152]{1,0:T(8,128)(2,1)S(1)}, bf16[80,1152]{1,0:T(8,128)(2,1)S(1)}, u32[]{:S(2)}, u32[]{:S(2)}) %collective-permute-start.35) | collective-permute-done | bytes 184352 | tf_op jit(solution)/shard_map/ppermute | solution.py:401
  127.8 3.2 %collective-permute-done.19 = bf16[512,256]{1,0:T(8,128)(2,1)S(1)} collective-permute-done((bf16[512,256]{1,0:T(8,128)(2,1)S(1)}, bf16[512,256]{1,0:T(8,128)(2,1)S(1)}, u32[]{:S(2)}, u32[]{:S(2)}) %collective-permute-start.19) | collective-permute-done | bytes 262176 | tf_op jit(solution)/shard_map/ppermute | solution.py:57
  132.3 2.2 %collective-permute-start.37 = (bf16[80,1152]{1,0:T(8,128)(2,1)S(1)}, bf16[80,1152]{1,0:T(8,128)(2,1)S(1)}, u32[]{:S(2)}, u32[]{:S(2)}) collective-permute-start(bf16[80,1152]{1,0:T(8,128)(2,1)S(1)} %maximum_maximum_fusion.2), channel_id=1, source_target_pairs={{0,128},{16,144},{32,160},{48,176},{64,192},{80,208},{96,224},{112... | collective-permute-start | bytes 552968 | tf_op jit(solution)/shard_map/ppermute | solution.py:401
  134.6 5.7 %collective-permute-done.20 = bf16[512,256]{1,0:T(8,128)(2,1)S(1)} collective-permute-done((bf16[512,256]{1,0:T(8,128)(2,1)S(1)}, bf16[512,256]{1,0:T(8,128)(2,1)S(1)}, u32[]{:S(2)}, u32[]{:S(2)}) %collective-permute-start.20) | collective-permute-done | bytes 262176 | tf_op jit(solution)/shard_map/ppermute | solution.py:57
  142.5 4.3 %collective-permute-done.22 = bf16[512,256]{1,0:T(8,128)(2,1)S(1)} collective-permute-done((bf16[512,256]{1,0:T(8,128)(2,1)S(1)}, bf16[512,256]{1,0:T(8,128)(2,1)S(1)}, u32[]{:S(2)}, u32[]{:S(2)}) %collective-permute-start.22) | collective-permute-done | bytes 262176 | tf_op jit(solution)/shard_map/ppermute | solution.py:57
  (116 shorter events, 44.8 us)
Async XLA Ops:
  0.6 12.5 %collective-permute-start = (bf16[512,256]{1,0:T(8,128)(2,1)}, bf16[512,256]{1,0:T(8,128)(2,1)S(1)}, u32[]{:S(2)}, u32[]{:S(2)}) collective-permute-start(bf16[512,256]{1,0:T(8,128)(2,1)} %input_ref.1), channel_id=1, source_target_pairs={{0,1},{1,2},{2,3},{3,4},{4,5},{5,6},{6,7},{7,0},{8,9},{9,10},{10,1... | collective-permute-start | bytes 786440 | tf_op jit(solution)/shard_map/ppermute | solution.py:53
  2.6 10.5 %collective-permute-start.4 = (bf16[512,256]{1,0:T(8,128)(2,1)}, bf16[512,256]{1,0:T(8,128)(2,1)S(1)}, u32[]{:S(2)}, u32[]{:S(2)}) collective-permute-start(bf16[512,256]{1,0:T(8,128)(2,1)} %input_ref.1), channel_id=1, source_target_pairs={{0,7},{1,0},{2,1},{3,2},{4,3},{5,4},{6,5},{7,6},{8,15},{9,8},{10,9... | collective-permute-start | bytes 786440 | tf_op jit(solution)/shard_map/ppermute | solution.py:57
  13.1 14.0 %collective-permute-start.5 = (bf16[512,256]{1,0:T(8,128)(2,1)S(1)}, bf16[512,256]{1,0:T(8,128)(2,1)S(1)}, u32[]{:S(2)}, u32[]{:S(2)}) collective-permute-start(bf16[512,256]{1,0:T(8,128)(2,1)S(1)} %collective-permute-done.4.refs_2_), channel_id=1, source_target_pairs={{0,8},{1,9},{2,10},{3,11},{4,12},{5,13},{6,14},{7,15},{8,0},{9,1},... | collective-permute-start | bytes 786440 | tf_op jit(solution)/shard_map/ppermute | solution.py:61
  22.3 10.0 %collective-permute-start.12 = (bf16[512,256]{1,0:T(8,128)(2,1)S(1)}, bf16[512,256]{1,0:T(8,128)(2,1)}, u32[]{:S(2)}, u32[]{:S(2)}) collective-permute-start(bf16[512,256]{1,0:T(8,128)(2,1)S(1)} %collective-permute-done.4.refs_2_), channel_id=1, source_target_pairs={{0,7},{1,0},{2,1},{3,2},{4,3},{5,4},{6,5},{7,6},{8,15},{9,8},{10,9... | collective-permute-start | bytes 786440 | tf_op jit(solution)/shard_map/ppermute | solution.py:57
  25.6 20.7 %collective-permute-start.2 = (bf16[512,256]{1,0:T(8,128)(2,1)S(1)}, bf16[512,256]{1,0:T(8,128)(2,1)}, u32[]{:S(2)}, u32[]{:S(2)}) collective-permute-start(bf16[512,256]{1,0:T(8,128)(2,1)S(1)} %collective-permute-done.1.refs_4_), channel_id=1, source_target_pairs={{0,8},{1,9},{2,10},{3,11},{4,12},{5,13},{6,14},{7,15},{8,0},{9,1},... | collective-permute-start | bytes 786440 | tf_op jit(solution)/shard_map/ppermute | solution.py:61
  27.1 19.3 %collective-permute-start.6 = (bf16[512,256]{1,0:T(8,128)(2,1)S(1)}, bf16[512,256]{1,0:T(8,128)(2,1)}, u32[]{:S(2)}, u32[]{:S(2)}) collective-permute-start(bf16[512,256]{1,0:T(8,128)(2,1)S(1)} %collective-permute-done.5.refs_9_), channel_id=1, source_target_pairs={{0,7},{1,0},{2,1},{3,2},{4,3},{5,4},{6,5},{7,6},{8,15},{9,8},{10,9... | collective-permute-start | bytes 786440 | tf_op jit(solution)/shard_map/ppermute | solution.py:57
  29.6 20.0 %collective-permute-start.9 = (bf16[512,256]{1,0:T(8,128)(2,1)S(1)}, bf16[512,256]{1,0:T(8,128)(2,1)}, u32[]{:S(2)}, u32[]{:S(2)}) collective-permute-start(bf16[512,256]{1,0:T(8,128)(2,1)S(1)} %collective-permute-done.8.refs_7_), channel_id=1, source_target_pairs={{0,1},{1,2},{2,3},{3,4},{4,5},{5,6},{6,7},{7,0},{8,9},{9,10},{10,1... | collective-permute-start | bytes 786440 | tf_op jit(solution)/shard_map/ppermute | solution.py:53
  32.0 19.2 %collective-permute-start.13 = (bf16[512,256]{1,0:T(8,128)(2,1)S(1)}, bf16[512,256]{1,0:T(8,128)(2,1)}, u32[]{:S(2)}, u32[]{:S(2)}) collective-permute-start(bf16[512,256]{1,0:T(8,128)(2,1)S(1)} %collective-permute-done.refs_1_), channel_id=1, source_target_pairs={{0,8},{1,9},{2,10},{3,11},{4,12},{5,13},{6,14},{7,15},{8,0},{9,1},... | collective-permute-start | bytes 786440 | tf_op jit(solution)/shard_map/ppermute | solution.py:61
  32.3 18.8 %collective-permute-start.14 = (bf16[512,256]{1,0:T(8,128)(2,1)}, bf16[512,256]{1,0:T(8,128)(2,1)}, u32[]{:S(2)}, u32[]{:S(2)}) collective-permute-start(bf16[512,256]{1,0:T(8,128)(2,1)} %collective-permute-done.12.refs_5_), channel_id=1, source_target_pairs={{0,7},{1,0},{2,1},{3,2},{4,3},{5,4},{6,5},{7,6},{8,15},{9,8},{10,9... | collective-permute-start | bytes 786440 | tf_op jit(solution)/shard_map/ppermute | solution.py:57
  46.3 10.1 %collective-permute-start.3 = (bf16[512,256]{1,0:T(8,128)(2,1)}, bf16[512,256]{1,0:T(8,128)(2,1)S(1)}, u32[]{:S(2)}, u32[]{:S(2)}) collective-permute-start(bf16[512,256]{1,0:T(8,128)(2,1)} %collective-permute-done.2.refs_12_), channel_id=1, source_target_pairs={{0,1},{1,2},{2,3},{3,4},{4,5},{5,6},{6,7},{7,0},{8,9},{9,10},{10,1... | collective-permute-start | bytes 786440 | tf_op jit(solution)/shard_map/ppermute | solution.py:53
  46.4 10.0 %collective-permute-start.7 = (bf16[512,256]{1,0:T(8,128)(2,1)}, bf16[512,256]{1,0:T(8,128)(2,1)S(1)}, u32[]{:S(2)}, u32[]{:S(2)}) collective-permute-start(bf16[512,256]{1,0:T(8,128)(2,1)} %collective-permute-done.6.refs_11_), channel_id=1, source_target_pairs={{0,7},{1,0},{2,1},{3,2},{4,3},{5,4},{6,5},{7,6},{8,15},{9,8},{10,9... | collective-permute-start | bytes 786440 | tf_op jit(solution)/shard_map/ppermute | solution.py:57
  72.7 19.0 %collective-permute-start.32 = (bf16[64,512]{1,0:T(8,128)(2,1)S(1)}, bf16[64,512]{1,0:T(8,128)(2,1)S(1)}, u32[]{:S(2)}, u32[]{:S(2)}) collective-permute-start(bf16[64,512]{1,0:T(8,128)(2,1)S(1)} %add_convert_fusion.11), channel_id=1, source_target_pairs={{0,2},{1,3},{2,0},{3,1},{4,6},{5,7},{6,4},{7,5},{8,10},{9,11},{10,... | collective-permute-start | bytes 196616 | tf_op jit(solution)/shard_map/ppermute | solution.py:389
  86.9 10.4 %collective-permute-start.26 = (bf16[512,256]{1,0:T(8,128)(2,1)S(1)}, bf16[512,256]{1,0:T(8,128)(2,1)S(1)}, u32[]{:S(2)}, u32[]{:S(2)}) collective-permute-start(bf16[512,256]{1,0:T(8,128)(2,1)S(1)} %get-tuple-element.45), channel_id=1, source_target_pairs={{0,1},{1,2},{2,3},{3,4},{4,5},{5,6},{6,7},{7,0},{8,9},{9,10},{10,1... | collective-permute-start | bytes 786440 | tf_op jit(solution)/shard_map/ppermute | solution.py:53
  89.1 53.4 %collective-permute-start.29 = (bf16[512,256]{1,0:T(8,128)(2,1)S(1)}, bf16[512,256]{1,0:T(8,128)(2,1)S(1)}, u32[]{:S(2)}, u32[]{:S(2)}) collective-permute-start(bf16[512,256]{1,0:T(8,128)(2,1)S(1)} %get-tuple-element.46), channel_id=1, source_target_pairs={{0,8},{1,9},{2,10},{3,11},{4,12},{5,13},{6,14},{7,15},{8,0},{9,1},... | collective-permute-start | bytes 786440 | tf_op jit(solution)/shard_map/ppermute | solution.py:61
  90.7 11.8 %collective-permute-start.23 = (bf16[512,256]{1,0:T(8,128)(2,1)S(1)}, bf16[512,256]{1,0:T(8,128)(2,1)S(1)}, u32[]{:S(2)}, u32[]{:S(2)}) collective-permute-start(bf16[512,256]{1,0:T(8,128)(2,1)S(1)} %get-tuple-element.43), channel_id=1, source_target_pairs={{0,1},{1,2},{2,3},{3,4},{4,5},{5,6},{6,7},{7,0},{8,9},{9,10},{10,1... | collective-permute-start | bytes 786440 | tf_op jit(solution)/shard_map/ppermute | solution.py:53
  91.0 12.3 %collective-permute-start.17 = (bf16[512,256]{1,0:T(8,128)(2,1)S(1)}, bf16[512,256]{1,0:T(8,128)(2,1)S(1)}, u32[]{:S(2)}, u32[]{:S(2)}) collective-permute-start(bf16[512,256]{1,0:T(8,128)(2,1)S(1)} %get-tuple-element.38), channel_id=1, source_target_pairs={{0,8},{1,9},{2,10},{3,11},{4,12},{5,13},{6,14},{7,15},{8,0},{9,1},... | collective-permute-start | bytes 786440 | tf_op jit(solution)/shard_map/ppermute | solution.py:61
  91.7 18.3 %collective-permute-start.15 = (bf16[512,256]{1,0:T(8,128)(2,1)S(1)}, bf16[512,256]{1,0:T(8,128)(2,1)S(1)}, u32[]{:S(2)}, u32[]{:S(2)}) collective-permute-start(bf16[512,256]{1,0:T(8,128)(2,1)S(1)} %get-tuple-element.35), channel_id=1, source_target_pairs={{0,7},{1,0},{2,1},{3,2},{4,3},{5,4},{6,5},{7,6},{8,15},{9,8},{10,9... | collective-permute-start | bytes 786440 | tf_op jit(solution)/shard_map/ppermute | solution.py:57
  102.5 20.9 %collective-permute-start.27 = (bf16[512,256]{1,0:T(8,128)(2,1)S(1)}, bf16[512,256]{1,0:T(8,128)(2,1)}, u32[]{:S(2)}, u32[]{:S(2)}) collective-permute-start(bf16[512,256]{1,0:T(8,128)(2,1)S(1)} %add_convert_fusion.2), channel_id=1, source_target_pairs={{0,1},{1,2},{2,3},{3,4},{4,5},{5,6},{6,7},{7,0},{8,9},{9,10},{10,1... | collective-permute-start | bytes 786440 | tf_op jit(solution)/shard_map/ppermute | solution.py:53
  103.3 9.7 %collective-permute-start.24 = (bf16[512,256]{1,0:T(8,128)(2,1)}, bf16[512,256]{1,0:T(8,128)(2,1)}, u32[]{:S(2)}, u32[]{:S(2)}) collective-permute-start(bf16[512,256]{1,0:T(8,128)(2,1)} %add_convert_fusion.4), channel_id=1, source_target_pairs={{0,1},{1,2},{2,3},{3,4},{4,5},{5,6},{6,7},{7,0},{8,9},{9,10},{10,1... | collective-permute-start | bytes 786440 | tf_op jit(solution)/shard_map/ppermute | solution.py:53
  105.5 11.8 %collective-permute-start.18 = (bf16[512,256]{1,0:T(8,128)(2,1)}, bf16[512,256]{1,0:T(8,128)(2,1)}, u32[]{:S(2)}, u32[]{:S(2)}) collective-permute-start(bf16[512,256]{1,0:T(8,128)(2,1)} %add_convert_fusion.8), channel_id=1, source_target_pairs={{0,7},{1,0},{2,1},{3,2},{4,3},{5,4},{6,5},{7,6},{8,15},{9,8},{10,9... | collective-permute-start | bytes 786440 | tf_op jit(solution)/shard_map/ppermute | solution.py:57
  113.0 13.5 %collective-permute-start.16 = (bf16[512,256]{1,0:T(8,128)(2,1)S(1)}, bf16[512,256]{1,0:T(8,128)(2,1)S(1)}, u32[]{:S(2)}, u32[]{:S(2)}) collective-permute-start(bf16[512,256]{1,0:T(8,128)(2,1)S(1)} %add_convert_fusion.9), channel_id=1, source_target_pairs={{0,8},{1,9},{2,10},{3,11},{4,12},{5,13},{6,14},{7,15},{8,0},{9,1},... | collective-permute-start | bytes 786440 | tf_op jit(solution)/shard_map/ppermute | solution.py:61
  115.1 10.0 %collective-permute-start.25 = (bf16[512,256]{1,0:T(8,128)(2,1)S(1)}, bf16[512,256]{1,0:T(8,128)(2,1)S(1)}, u32[]{:S(2)}, u32[]{:S(2)}) collective-permute-start(bf16[512,256]{1,0:T(8,128)(2,1)S(1)} %add_convert_fusion.3), channel_id=1, source_target_pairs={{0,8},{1,9},{2,10},{3,11},{4,12},{5,13},{6,14},{7,15},{8,0},{9,1},... | collective-permute-start | bytes 786440 | tf_op jit(solution)/shard_map/ppermute | solution.py:61
  123.3 11.3 %collective-permute-start.21 = (bf16[512,256]{1,0:T(8,128)(2,1)S(1)}, bf16[512,256]{1,0:T(8,128)(2,1)S(1)}, u32[]{:S(2)}, u32[]{:S(2)}) collective-permute-start(bf16[512,256]{1,0:T(8,128)(2,1)S(1)} %get-tuple-element.39), channel_id=1, source_target_pairs={{0,8},{1,9},{2,10},{3,11},{4,12},{5,13},{6,14},{7,15},{8,0},{9,1},... | collective-permute-start | bytes 786440 | tf_op jit(solution)/shard_map/ppermute | solution.py:61
  126.5 16.0 %collective-permute-start.28 = (bf16[512,256]{1,0:T(8,128)(2,1)S(1)}, bf16[512,256]{1,0:T(8,128)(2,1)S(1)}, u32[]{:S(2)}, u32[]{:S(2)}) collective-permute-start(bf16[512,256]{1,0:T(8,128)(2,1)S(1)} %add_convert_fusion.1), channel_id=1, source_target_pairs={{0,1},{1,2},{2,3},{3,4},{4,5},{5,6},{6,7},{7,0},{8,9},{9,10},{10,1... | collective-permute-start | bytes 786440 | tf_op jit(solution)/shard_map/ppermute | solution.py:53
  (25 other events, 216.6 us)

commit v2 on v0

v2 whole, which is shorter than its diff:
```python
import functools
import math

import jax
import jax.numpy as jnp
from jax import lax
from jax.experimental import pallas as pl
from jax.experimental.pallas import tpu as pltpu
from jax.sharding import PartitionSpec as P

EPSILON = 1e-06
RING = 8
PAIR = 2
MERGE_ROWS = 512

EARLY = (
    (0, 0),
    (0, -1), (0, 1), (1, 0),
    (0, -2), (0, 2), (1, -1),
    (0, -3), (0, 3), (1, 1),
    (0, 4), (1, 2), (1, -2),
)
LATE = ((1, -3), (1, 3), (1, 4))
REST_OUT = (
    (0, 4), (1, 2), (1, -2), (0, -3), (0, 3), (1, 1), (0, -2), (0, 2), (1, -1),
    (0, -1), (0, 1), (1, 0), (0, 0),
)

VMEM = pl.BlockSpec(memory_space=pltpu.VMEM)
SMEM = pl.BlockSpec(memory_space=pltpu.SMEM)


def ring_perm(step):
    pairs = []
    for group in range(16):
        move = -step if group % 2 else step
        for pair in range(PAIR):
            for at in range(RING):
                source = (group * PAIR + pair) * RING + at
                pairs.append((source, source - at + (at + move) % RING))
    return pairs


def xor_perm(bits):
    return [(at, at ^ bits) for at in range(16)]


def up_ring(array):
    return lax.ppermute(array, ("dp", "tensor"), ring_perm(1))


def down_ring(array):
    return lax.ppermute(array, ("dp", "tensor"), ring_perm(-1))


def across(array):
    return lax.ppermute(array, "tensor", xor_perm(RING))


def dot(left, right, left_dim, right_dim):
    return lax.dot_general(
        left, right, (((left_dim,), (right_dim,)), ((), ())), preferred_element_type=jnp.float32
    )


def row_of(rank, offset, height, sign):
    pair, ring = offset
    ring = ring * sign
    own_pair, own_ring = rank // RING, rank % RING
    other = own_pair if pair == 0 else 1 - own_pair
    block = other * RING + (own_ring + ring + RING) % RING
    return pl.multiple_of(block * height, height)


def merge_rows(first, parts, weight_ref, down_ref, up_ref, merged_ref, square_ref):
    width = weight_ref.shape[1]

    @pl.loop(first, first + parts)
    def _(part):
        here = pl.ds(pl.multiple_of(part * MERGE_ROWS, MERGE_ROWS), MERGE_ROWS)
        down = down_ref[:, here]
        wide = weight_ref[here, :].astype(jnp.float32) + dot(down, up_ref[...], 0, 0)
        merged_ref[here, :width] = wide.astype(jnp.bfloat16)
        merged_ref[here, width:] = jnp.concatenate([down, jnp.zeros_like(down)], axis=0).T
        square_ref[...] += jnp.sum(wide * wide, axis=0, keepdims=True)


def merge_head_kernel(parts, weight_ref, down_ref, up_ref, merged_ref, square_ref):
    square_ref[...] = jnp.zeros_like(square_ref)
    merge_rows(0, parts, weight_ref, down_ref, up_ref, merged_ref, square_ref)


def merge_tail_kernel(
    first, parts, weight_ref, down_ref, up_ref, head_ref, head_square_ref, merged_ref, square_ref
):
    square_ref[...] = head_square_ref[...]
    merge_rows(first, parts, weight_ref, down_ref, up_ref, merged_ref, square_ref)


def merge(first, parts, operands, head):
    weight, down_t, _ = operands
    depth, width = weight.shape
    rank = down_t.shape[0]
    rows = parts * MERGE_ROWS
    if head:
        kernel, aliases = functools.partial(merge_tail_kernel, first, parts), {3: 0}
    else:
        kernel, aliases = functools.partial(merge_head_kernel, parts), {}
    return pl.pallas_call(
        kernel,
        in_specs=[VMEM] * (3 + len(head)),
        out_specs=[VMEM] * 2,
        out_shape=[
            jax.ShapeDtypeStruct((depth, width + 2 * rank), jnp.bfloat16),
            jax.ShapeDtypeStruct((1, width), jnp.float32),
        ],
        input_output_aliases=aliases,
        compiler_params=pltpu.CompilerParams(vmem_limit_bytes=6 * 2**20),
        cost_estimate=pl.CostEstimate(
            flops=2 * rows * width * rank, bytes_accessed=4 * rows * width, transcendentals=0
        ),
        name="merge_tail" if head else "merge_head",
    )(*operands, *head)


def split(array):
    high = array.astype(jnp.bfloat16)
    low = (array - high.astype(jnp.float32)).astype(jnp.bfloat16)
    return jnp.concatenate([high, low], axis=0)


def gradient_block(scaled_ref, rows, both_ref, block_ref, out_ref):
    tokens = scaled_ref.shape[0]
    low = both_ref.shape[0] // 2
    out_ref[:tokens, :] = dot(scaled_ref[...], rows, 1, 1).astype(jnp.bfloat16)
    down = dot(both_ref[...], block_ref[...], 1, 0)
    out_ref[tokens:, :] = (down[:low] + down[low:]).astype(jnp.bfloat16)


def gate_early_kernel(count, rank_ref, *refs):
    blocks, merged_ref, total_ref = refs[:count], refs[count], refs[count + 1]
    rank, sign = rank_ref[0], rank_ref[1]
    height = blocks[0].shape[1]
    for at, offset in enumerate(EARLY):
        rows = merged_ref[pl.ds(row_of(rank, offset, height, sign), height), :]
        part = dot(blocks[at][...], rows, 1, 0)
        if at == 0:
            total_ref[...] = part
        else:
            total_ref[...] += part


def gate_early(rank, blocks, merged):
    tokens, height = blocks[0].shape
    wide = merged.shape[1]
    count = len(blocks)
    return pl.pallas_call(
        functools.partial(gate_early_kernel, count),
        in_specs=[SMEM] + [VMEM] * (count + 1),
        out_specs=VMEM,
        out_shape=jax.ShapeDtypeStruct((tokens, wide), jnp.float32),
        compiler_params=pltpu.CompilerParams(vmem_limit_bytes=6 * 2**20),
        cost_estimate=pl.CostEstimate(
            flops=2 * tokens * height * wide * count,
            bytes_accessed=count * height * (wide + tokens) * 2 + tokens * wide * 4,
            transcendentals=0,
        ),
        name="gate_early",
    )(rank, *blocks, merged)


def gate_late_kernel(
    factor,
    rank_ref,
    late_a,
    late_b,
    late_c,
    merged_ref,
    total_ref,
    square_ref,
    magnitude_ref,
    hidden_ref,
    saved_ref,
    lowrank_up_ref,
    up_out_ref,
    scaled_ref,
    both_ref,
    latent_ref,
    magnitude_piece_ref,
    first_a,
    first_b,
    first_c,
):
    rank, sign = rank_ref[0], rank_ref[1]
    tokens, height = late_a.shape
    width = hidden_ref.shape[1]
    low = lowrank_up_ref.shape[0]
    norms = jnp.sqrt(square_ref[...] + EPSILON)
    scales = magnitude_ref[...] / norms
    tile = 128
    starts = [row_of(rank, offset, height, sign) for offset in LATE]
    magnitude_piece_ref[...] = jnp.zeros_like(magnitude_piece_ref)

    @pl.loop(0, tokens // tile)
    def _(step):
        here = pl.ds(pl.multiple_of(step * tile, tile), tile)
        total = total_ref[here, :]
        for block, start in zip((late_a, late_b, late_c), starts):
            total += dot(block[here, :], merged_ref[pl.ds(start, height), :], 1, 0)
        gate_pre = total[:, :width]
        latent = total[:, width : width + low]
        gate_out = gate_pre * scales
        gate_sig = 1.0 / (1.0 + jnp.exp(-gate_out))
        cotangent = hidden_ref[here, :].astype(jnp.float32)
        up_out_ref[here, :] = (cotangent * gate_out * gate_sig).astype(jnp.bfloat16)
        gate_grad = (
            cotangent
            * saved_ref[here, :].astype(jnp.float32)
            * gate_sig
            * (1.0 + gate_out * (1.0 - gate_sig))
        )
        magnitude_piece_ref[...] += jnp.sum(gate_grad * gate_pre, axis=0, keepdims=True)
        scaled_ref[here, :] = (gate_grad * scales).astype(jnp.bfloat16)
        latent_high = latent.astype(jnp.bfloat16)
        latent_rest = (latent - latent_high.astype(jnp.float32)).astype(jnp.bfloat16)
        latent_ref[here, :] = jnp.concatenate([latent_high, latent_rest], axis=1)

    magnitude_piece_ref[...] = magnitude_piece_ref[...] / norms * factor
    both_ref[...] = split(dot(lowrank_up_ref[...], scaled_ref[...], 1, 1))
    for offset, block, out in zip(LATE, (late_a, late_b, late_c), (first_a, first_b, first_c)):
        rows = merged_ref[pl.ds(row_of(rank, offset, height, sign), height), :width]
        gradient_block(scaled_ref, rows, both_ref, block, out)


def gate_late(factor, rank, late, merged, total, square, magnitude, hidden, saved, lowrank_up):
    tokens, height = late[0].shape
    wide = merged.shape[1]
    width = hidden.shape[1]
    low = lowrank_up.shape[0]
    block = jax.ShapeDtypeStruct((tokens + low, height), jnp.bfloat16)
    return pl.pallas_call(
        functools.partial(gate_late_kernel, factor),
        in_specs=[SMEM] + [VMEM] * 10,
        out_specs=[VMEM] * 8,
        out_shape=[
            jax.ShapeDtypeStruct((tokens, width), jnp.bfloat16),
            jax.ShapeDtypeStruct((tokens, width), jnp.bfloat16),
            jax.ShapeDtypeStruct((2 * low, tokens), jnp.bfloat16),
            jax.ShapeDtypeStruct((tokens, 2 * low), jnp.bfloat16),
            jax.ShapeDtypeStruct((1, width), jnp.float32),
            block,
            block,
            block,
        ],
        compiler_params=pltpu.CompilerParams(vmem_limit_bytes=6 * 2**20),
        cost_estimate=pl.CostEstimate(
            flops=2 * tokens * height * wide * 7,
            bytes_accessed=8 * 2**20,
            transcendentals=2 * tokens * width,
        ),
        name="gate_late",
    )(rank, *late, merged, total, square, magnitude, hidden, saved, lowrank_up)


def rest_kernel(factor, count, rank_ref, merged_ref, scaled_ref, latent_ref, both_ref, *refs):
    blocks, up_piece_ref, outs = refs[:count], refs[count], refs[count + 1 :]
    rank, sign = rank_ref[0], rank_ref[1]
    height = outs[0].shape[1]
    low, width = up_piece_ref.shape
    for offset, block, out in zip(REST_OUT, blocks, outs):
        rows = merged_ref[pl.ds(row_of(rank, offset, height, sign), height), :width]
        gradient_block(scaled_ref, rows, both_ref, block, out)
    both = dot(latent_ref[...], scaled_ref[...], 0, 0)
    up_piece_ref[...] = (both[:low] + both[low:]) * factor


def rest(factor, rank, merged, scaled, latent, both, blocks):
    tokens, width = scaled.shape
    height = blocks[0].shape[1]
    wide = merged.shape[1]
    count = len(REST_OUT)
    low = latent.shape[1] // 2
    return pl.pallas_call(
        functools.partial(rest_kernel, factor, count),
        in_specs=[SMEM] + [VMEM] * (4 + count),
        out_specs=[VMEM] * (count + 1),
        out_shape=[jax.ShapeDtypeStruct((low, width), jnp.float32)]
        + [jax.ShapeDtypeStruct((tokens + low, height), jnp.bfloat16)] * count,
        compiler_params=pltpu.CompilerParams(vmem_limit_bytes=6 * 2**20),
        cost_estimate=pl.CostEstimate(
            flops=2 * tokens * height * width * count,
            bytes_accessed=count * height * (wide + tokens) * 2,
            transcendentals=0,
        ),
        name="rest",
    )(rank, merged, scaled, latent, both, *blocks)


def payload_kernel(factor, tokens, rank_ref, up_ref, magnitude_ref, *refs):
    parts, (kept_ref, sent_ref) = refs[:4], refs[4:]
    low, width = up_ref.shape
    half = low // 2
    core = rank_ref[2]
    for out, upper in ((kept_ref, core), (sent_ref, 1 - core)):
        first = upper == 0
        here = pl.ds(pl.multiple_of(tokens + upper * half, half), half)
        down = sum(part[here, :].astype(jnp.float32) for part in parts) * factor
        out[...] = jnp.zeros_like(out)
        out[:half, :width] = jnp.where(first, up_ref[:half, :], up_ref[half:, :])
        out[:half, width:] = down
        out[half : half + 1, :width] = magnitude_ref[...]


def payload(factor, tokens, rank, up_piece, magnitude_piece, parts):
    low, width = up_piece.shape
    out = jax.ShapeDtypeStruct((low // 2 + 8, width + parts[0].shape[1]), jnp.float32)
    return pl.pallas_call(
        functools.partial(payload_kernel, factor, tokens),
        in_specs=[SMEM] + [VMEM] * 6,
        out_specs=[VMEM] * 2,
        out_shape=[out] * 2,
        compiler_params=pltpu.CompilerParams(vmem_limit_bytes=6 * 2**20),
        cost_estimate=pl.CostEstimate(flops=2**20, bytes_accessed=2**20, transcendentals=0),
        name="payload",
    )(rank, up_piece, magnitude_piece, *parts)


def f32(array):
    return array.astype(jnp.float32)


def narrow(*arrays):
    total = f32(arrays[0])
    for array in arrays[1:]:
        total = total + f32(array)
    return total.astype(jnp.bfloat16)


def sum_four(array, axis, bits):
    sent = lax.optimization_barrier(array.astype(jnp.bfloat16))
    one, two = bits
    near, far, both = (lax.ppermute(sent, axis, xor_perm(at)) for at in (one, two, one ^ two))
    return (f32(sent) + f32(near)) + (f32(far) + f32(both))


def pack(array, half):
    row = array[half : half + 1]
    high = lax.reduce_precision(row, 8, 7)
    pad = jnp.zeros((14, array.shape[1]), jnp.float32)
    return jnp.concatenate([array[:half], high, row - high, pad], axis=0)


def unpack(array, half):
    return jnp.concatenate(
        [array[:half], array[half : half + 1] + array[half + 1 : half + 2]], axis=0
    )


def together(*arrays):
    return lax.optimization_barrier(arrays)


def per_device(
    stored_layer_input,
    saved_up_output,
    hidden_gradient,
    frozen_gate_weight,
    lowrank_down,
    lowrank_up,
    magnitude,
):
    own = stored_layer_input
    tokens, height = own.shape
    width = frozen_gate_weight.shape[1]
    low = lowrank_up.shape[0]
    factor = 1.0 / math.sqrt(tokens * lax.axis_size("dp"))
    core = lax.axis_index("dp") % 2
    rank = jnp.stack([lax.axis_index("tensor"), 1 - 2 * core, core]).astype(jnp.int32)
    rank, magnitude_row, own = together(rank, magnitude.reshape(1, width), own)

    operands = (frozen_gate_weight, jnp.transpose(lowrank_down), lowrank_up)
    head = merge(0, 2, operands, ())

    got = {(0, 0): own}
    token = own[:16, :128]

    def arrive(move, source, target, *more):
        nonlocal token
        block = move(got[source])
        token, got[target], *more = together(token, block, *more)
        return more

    head = arrive(up_ring, (0, 0), (0, -1), *head)
    arrive(down_ring, (0, 0), (0, 1))
    arrive(across, (0, 0), (1, 0))
    merged, square = merge(2, 6, operands, head)
    merged, square = arrive(up_ring, (0, -1), (0, -2), merged, square)
    arrive(down_ring, (0, 1), (0, 2))
    arrive(across, (0, -1), (1, -1))
    arrive(up_ring, (0, -2), (0, -3))
    arrive(down_ring, (0, 2), (0, 3))
    arrive(across, (0, 1), (1, 1))
    arrive(up_ring, (0, -3), (0, 4))
    arrive(down_ring, (1, 1), (1, 2))
    arrive(across, (0, -2), (1, -2))
    total = gate_early(rank, [got[offset] for offset in EARLY], merged)
    (total,) = arrive(up_ring, (1, -2), (1, -3), total)
    arrive(down_ring, (1, 2), (1, 3))
    arrive(across, (0, 4), (1, 4))
    *late, total = together(*[got[offset] for offset in LATE], total)

    up_output_gradient, scaled, both, latent, magnitude_piece, *first = gate_late(
        factor,
        rank,
        late,
        merged,
        total,
        square,
        magnitude_row,
        hidden_gradient,
        saved_up_output,
        lowrank_up,
    )
    lower, upper, far = down_ring(first[0]), up_ring(first[1]), across(first[2])
    up_piece, *others = rest(
        factor, rank, merged, scaled, latent, both, [got[offset] for offset in REST_OUT]
    )
    far, lower, upper, up_piece, *others = together(far, lower, upper, up_piece, *others)
    part = dict(zip(REST_OUT, others))

    in_a = down_ring(narrow(part[0, 4], far))
    in_b = up_ring(narrow(part[1, 2], upper))
    in_c = across(narrow(part[1, -2], lower))
    in_a, in_b, in_c = together(in_a, in_b, in_c)

    in_d = down_ring(narrow(part[0, -3], in_a))
    in_e = up_ring(part[0, 3])
    in_f = across(narrow(part[1, 1], in_b))
    in_d, in_e, in_f = together(in_d, in_e, in_f)

    in_g = down_ring(narrow(part[0, -2], in_c, in_d))
    in_h = up_ring(narrow(part[0, 2], in_e))
    in_i = across(part[1, -1])
    in_g, in_h, in_i = together(in_g, in_h, in_i)

    in_j = down_ring(narrow(part[0, -1], in_g, in_i))
    in_k = up_ring(narrow(part[0, 1], in_f, in_h))
    in_l = across(part[1, 0])
    in_j, in_k, in_l = together(in_j, in_k, in_l)
    layer_input_gradient = narrow(*[one[:tokens] for one in (part[0, 0], in_j, in_k, in_l)])

    half = low // 2
    kept, sent = payload(
        factor, tokens, rank, up_piece, magnitude_piece, (part[0, 0], in_j, in_k, in_l)
    )
    pieces = kept + lax.ppermute(sent, "dp", xor_perm(1))
    pieces = unpack(sum_four(pack(pieces, half), "dp", (2, 4)), half)
    sent = lax.optimization_barrier(pack(pieces, half).astype(jnp.bfloat16))
    pieces = unpack(f32(sent) + f32(lax.ppermute(sent, "dp", xor_perm(8))), half)
    mine = pieces[:half]
    other = lax.ppermute(mine, "dp", xor_perm(1))
    summed = jnp.where(
        core == 0,
        jnp.concatenate([mine, other], axis=0),
        jnp.concatenate([other, mine], axis=0),
    )
    return (
        layer_input_gradient,
        up_output_gradient,
        jnp.transpose(summed[:, width:]),
        summed[:, :width],
        pieces[half, :width],
    )


def solution(mesh):
    return jax.shard_map(
        per_device,
        mesh=mesh,
        in_specs=(
            P("dp", "tensor"),
            P("dp", "tensor"),
            P("dp", "tensor"),
            P(None, "tensor"),
            P(),
            P(None, "tensor"),
            P("tensor"),
        ),
        out_specs=(
            P("dp", "tensor"),
            P("dp", "tensor"),
            P("tensor", None),
            P(None, "tensor"),
            P("tensor"),
        ),
        check_vma=False,
    )
```

time: 629 us -> 133 us (0.21)
  waiting for transfers between devices: 520 us -> 55.6 us
  starting transfers between devices: 0.16 us -> 46.7 us
  matrix products: 45.7 us -> 0 us
  blocking collectives: 43 us -> 0 us
  Pallas kernels: 0 us -> 19.3 us
  between operations: 13.8 us -> 0.91 us
    psum x2 -> x0, waiting for transfers between devices: 340 us -> none  [the longest x1 202 us: per_device(): down_summed = lax.psum(down_whole, ('dp', 'tensor'))]
    reduce_scatter x1 -> x0, waiting for transfers between devices: 103 us -> none  [per_device(): lax.psum_scatter(contract(merged, scaled_gradient, 1, 1), 'tensor', scatt...]
    all_gather x1 -> x0, waiting for transfers between devices: 76.5 us -> none  [per_device(): lax.all_gather(stored_layer_input, 'tensor', axis=1, tiled=True)]
    ppermute x0 -> x36, waiting for transfers between devices: none -> 55.6 us  [the longest x10 27.8 us: across(): return lax.ppermute(array, 'tensor', xor_perm(RING))]
    ppermute x0 -> x36, starting transfers between devices: none -> 46.7 us  [the longest x10 19.5 us: up_ring(): return lax.ppermute(array, ('dp', 'tensor'), ring_perm(1))]
    dot_general x9 -> x0, matrix products: 45.7 us -> none  [contract(): lax.dot_general(left, right, (((left_dim,), (right_dim,)), ((), ())), pre...]
    psum x1 -> x0, blocking collectives: 43 us -> none  [per_device(): lax.psum((up_piece, magnitude_piece), 'dp')]
    pallas_call x0 -> x6, Pallas kernels: none -> 19.3 us  [the longest x1 5.49 us: gate_late(): pl.pallas_call(functools.partial(gate_late_kernel, factor), in_specs=[SME...]
  transfers between devices with their start and end apart: 4 -> 36, of which waited for: 4 -> 21; matrix products, arithmetic and copies ran while one was open for 5% -> 2% of each run, Pallas kernels for 0% -> 10%
where the time goes in v2:
time: 133 us; the launch traced here: 132 us
  waiting for transfers between devices  55.6 us (42%)
  starting transfers between devices  46.7 us (35%)
  Pallas kernels  19.3 us (15%)
  local copies, waits for them, and re-layouts  7.19 us (5%)
  other arithmetic  2.63 us (2%)
    ppermute x10, waiting for transfers between devices, across(): return lax.ppermute(array, 'tensor', xor_perm(RING))  27.8 us
    ppermute x10, starting transfers between devices, up_ring(): return lax.ppermute(array, ('dp', 'tensor'), ring_perm(1))  19.5 us
    ppermute x10, waiting for transfers between devices, down_ring(): return lax.ppermute(array, ('dp', 'tensor'), ring_perm(-1))  11.3 us
    ppermute x10, starting transfers between devices, across(): return lax.ppermute(array, 'tensor', xor_perm(RING))  8.42 us
    ppermute x3, waiting for transfers between devices, sum_four(): lax.ppermute(sent, axis, xor_perm(at))  7.76 us
    ppermute x10, starting transfers between devices, down_ring(): return lax.ppermute(array, ('dp', 'tensor'), ring_perm(-1))  6.73 us
    pallas_call x1, Pallas kernels, gate_late(): pl.pallas_call(functools.partial(gate_late_kernel, factor), in_specs=[SME...  5.49 us
    ppermute x10, waiting for transfers between devices, up_ring(): return lax.ppermute(array, ('dp', 'tensor'), ring_perm(1))  5.48 us
  transfers between devices with their start and end apart: 36, of which 21 were waited for; matrix products, arithmetic and copies ran while one was open for 2% of the time, Pallas kernels for 10%

profile of v2, /device:TPU:1, one launch (start us, length us, event | category | flops | bytes accessed | tf_op | source)
XLA Modules:
  0.0 132.3 jit_solution(8457056326058362354)
XLA Ops:
  1.4 6.4 %collective-permute-start = (bf16[512,256]{1,0:T(8,128)(2,1)}, bf16[512,256]{1,0:T(8,128)(2,1)S(1)}, u32[]{:S(2)}, u32[]{:S(2)}) collective-permute-start(bf16[512,256]{1,0:T(8,128)(2,1)} %refs_12_), channel_id=1, source_target_pairs={{0,1},{1,2},{2,3},{3,4},{4,5},{5,6},{6,7},{7,0},{8,9},{9,10},{10,1... | collective-permute-start | bytes 786440 | tf_op jit(solution)/shard_map/ppermute | solution.py:49
  7.8 3.1 %copy-done = bf16[4096,896]{1,0:T(8,128)(2,1)S(1)} copy-done((bf16[4096,896]{1,0:T(8,128)(2,1)S(1)}, bf16[4096,896]{1,0:T(8,128)(2,1)}, u32[]{:S(2)}) %copy-start) | copy-done | bytes 7340056
  13.9 2.8 %collective-permute-start.1 = (bf16[512,256]{1,0:T(8,128)(2,1)S(1)}, bf16[512,256]{1,0:T(8,128)(2,1)S(1)}, u32[]{:S(2)}, u32[]{:S(2)}) collective-permute-start(bf16[512,256]{1,0:T(8,128)(2,1)S(1)} %collective-permute-done.refs_1_.refs_9_), channel_id=1, source_target_pairs={{0,1},{1,2},{2,3},{3,4},{4,5},{5,6},{6,7},{7,0},{8,9},{9,10},{10,1... | collective-permute-start | bytes 786440 | tf_op jit(solution)/shard_map/ppermute | solution.py:49
  17.8 3.0 %merge_tail.1 = (bf16[4096,1024]{1,0:T(8,128)(2,1)S(1)}, f32[1,896]{1,0:T(1,128)S(1)}) custom-call(bf16[4096,896]{1,0:T(8,128)(2,1)S(1)} %copy-done, bf16[64,4096]{1,0:T(8,128)(2,1)S(1)} %bitcast.7, bf16[64,896]{1,0:T(8,128)(2,1)S(1)} %copy-done.3, bf16[4096,1024]{1,0:T(8,128)(2,1)S(1)} %get-tuple-element.82.head_ref, ...), custom_call_target="tpu_custom_call", output_to_operand_aliasing={{0}: (3, {})} | custom-call | flops 352321536 | bytes 11010048 | tf_op jit(solution)/shard_map/merge_tail/pallas_call | solution.py:109
  20.9 2.7 %collective-permute-start.8 = (bf16[512,256]{1,0:T(8,128)(2,1)S(1)}, bf16[512,256]{1,0:T(8,128)(2,1)S(1)}, u32[]{:S(2)}, u32[]{:S(2)}) collective-permute-start(bf16[512,256]{1,0:T(8,128)(2,1)S(1)} %collective-permute-done.1.refs_4_.refs_6_), channel_id=1, source_target_pairs={{0,1},{1,2},{2,3},{3,4},{4,5},{5,6},{6,7},{7,0},{8,9},{9,10},{10,1... | collective-permute-start | bytes 786440 | tf_op jit(solution)/shard_map/ppermute | solution.py:49
  27.0 4.8 %collective-permute-done.5.refs_3_.refs_11_ = bf16[512,256]{1,0:T(8,128)(2,1)S(1)} collective-permute-done((bf16[512,256]{1,0:T(8,128)(2,1)S(1)}, bf16[512,256]{1,0:T(8,128)(2,1)S(1)}, u32[]{:S(2)}, u32[]{:S(2)}) %collective-permute-start.5) | collective-permute-done | bytes 262176 | tf_op jit(solution)/shard_map/ppermute | solution.py:57
  31.8 5.6 %collective-permute-done.7.refs_6_.refs_8_ = bf16[512,256]{1,0:T(8,128)(2,1)S(1)} collective-permute-done((bf16[512,256]{1,0:T(8,128)(2,1)S(1)}, bf16[512,256]{1,0:T(8,128)(2,1)S(1)}, u32[]{:S(2)}, u32[]{:S(2)}) %collective-permute-start.7) | collective-permute-done | bytes 262176 | tf_op jit(solution)/shard_map/ppermute | solution.py:57
  37.4 5.6 %collective-permute-done.2.refs_12_.refs_2_ = bf16[512,256]{1,0:T(8,128)(2,1)S(1)} collective-permute-done((bf16[512,256]{1,0:T(8,128)(2,1)S(1)}, bf16[512,256]{1,0:T(8,128)(2,1)S(1)}, u32[]{:S(2)}, u32[]{:S(2)}) %collective-permute-start.2) | collective-permute-done | bytes 262176 | tf_op jit(solution)/shard_map/ppermute | solution.py:57
  45.4 4.2 %gate_early.1.total_ref = f32[512,1024]{1,0:T(8,128)S(1)} custom-call(s32[3]{0:T(128)S(1)} %pad_add_fusion.rank_ref, bf16[512,256]{1,0:T(8,128)(2,1)S(1)} %copy-done.2, bf16[512,256]{1,0:T(8,128)(2,1)S(1)} %collective-permute-done.refs_1_.refs_9_, bf16[512,256]{1,0:T(8,128)(2,1)S(1)} %collective-permute-done.4.refs_2_.refs_10_, ...), custom_call_target="tpu_custom_call" | custom-call | flops 3489660928 | bytes 12320768 | tf_op jit(solution)/shard_map/gate_early/pallas_call | solution.py:157
  51.5 5.5 %gate_late.1 = (bf16[512,896]{1,0:T(8,128)(2,1)}, bf16[512,896]{1,0:T(8,128)(2,1)S(1)}, bf16[128,512]{1,0:T(8,128)(2,1)S(1)}, bf16[512,128]{1,0:T(8,128)(2,1)S(1...) custom-call(s32[3]{0:T(128)S(1)} %pad_add_fusion.rank_ref, ...), custom_call_target="tpu_custom_call" | custom-call | flops 1879048192 | bytes 8388608 | tf_op jit(solution)/shard_map/gate_late/pallas_call | solution.py:241
  60.2 5.0 %rest.1 = (f32[64,896]{1,0:T(8,128)S(1)}, bf16[576,256]{1,0:T(8,128)(2,1)S(1)}, bf16[576,256]{1,0:T(8,128)(2,1)S(1)}, bf16[576,256]{1,0:T(8,128)(2,1)S(1)}, bf16...) custom-call(s32[3]{0:T(128)S(1)} %pad_add_fusion.rank_ref, ...), custom_call_target="tpu_custom_call" | custom-call | flops 3053453312 | bytes 10223616 | tf_op jit(solution)/shard_map/rest/pallas_call | solution.py:283
  67.2 3.5 %collective-permute-start.19 = (bf16[576,256]{1,0:T(8,128)(2,1)S(1)}, bf16[576,256]{1,0:T(8,128)(2,1)S(1)}, u32[]{:S(2)}, u32[]{:S(2)}) collective-permute-start(bf16[576,256]{1,0:T(8,128)(2,1)S(1)} %add_convert_fusion.7), channel_id=1, source_target_pairs={{0,1},{1,2},{2,3},{3,4},{4,5},{5,6},{6,7},{7,0},{8,9},{9,10},{10,1... | collective-permute-start | bytes 884744 | tf_op jit(solution)/shard_map/ppermute | solution.py:49
  70.9 2.7 %collective-permute-start.22 = (bf16[576,256]{1,0:T(8,128)(2,1)S(1)}, bf16[576,256]{1,0:T(8,128)(2,1)S(1)}, u32[]{:S(2)}, u32[]{:S(2)}) collective-permute-start(bf16[576,256]{1,0:T(8,128)(2,1)S(1)} %get-tuple-element.128), channel_id=1, source_target_pairs={{0,1},{1,2},{2,3},{3,4},{4,5},{5,6},{6,7},{7,0},{8,9},{9,10},{10,1... | collective-permute-start | bytes 884744 | tf_op jit(solution)/shard_map/ppermute | solution.py:49
  74.4 6.7 %collective-permute-done.18 = bf16[576,256]{1,0:T(8,128)(2,1)S(1)} collective-permute-done((bf16[576,256]{1,0:T(8,128)(2,1)S(1)}, bf16[576,256]{1,0:T(8,128)(2,1)S(1)}, u32[]{:S(2)}, u32[]{:S(2)}) %collective-permute-start.18) | collective-permute-done | bytes 294944 | tf_op jit(solution)/shard_map/ppermute | solution.py:53
  83.0 6.4 %collective-permute-done.23 = bf16[576,256]{1,0:T(8,128)(2,1)S(1)} collective-permute-done((bf16[576,256]{1,0:T(8,128)(2,1)S(1)}, bf16[576,256]{1,0:T(8,128)(2,1)S(1)}, u32[]{:S(2)}, u32[]{:S(2)}) %collective-permute-start.23) | collective-permute-done | bytes 294944 | tf_op jit(solution)/shard_map/ppermute | solution.py:57
  91.5 4.2 %collective-permute-done.26 = bf16[576,256]{1,0:T(8,128)(2,1)S(1)} collective-permute-done((bf16[576,256]{1,0:T(8,128)(2,1)S(1)}, bf16[576,256]{1,0:T(8,128)(2,1)S(1)}, u32[]{:S(2)}, u32[]{:S(2)}) %collective-permute-start.26) | collective-permute-done | bytes 294944 | tf_op jit(solution)/shard_map/ppermute | solution.py:57
  97.8 2.1 %collective-permute-start.27 = (bf16[576,256]{1,0:T(8,128)(2,1)S(1)}, bf16[576,256]{1,0:T(8,128)(2,1)S(1)}, u32[]{:S(2)}, u32[]{:S(2)}) collective-permute-start(bf16[576,256]{1,0:T(8,128)(2,1)S(1)} %add_convert_fusion.1), channel_id=1, source_target_pairs={{0,7},{1,0},{2,1},{3,2},{4,3},{5,4},{6,5},{7,6},{8,15},{9,8},{10,9... | collective-permute-start | bytes 884744 | tf_op jit(solution)/shard_map/ppermute | solution.py:53
  101.1 2.8 %collective-permute-done.28.refs_2_ = bf16[576,256]{1,0:T(8,128)(2,1)S(1)} collective-permute-done((bf16[576,256]{1,0:T(8,128)(2,1)S(1)}, bf16[576,256]{1,0:T(8,128)(2,1)S(1)}, u32[]{:S(2)}, u32[]{:S(2)}) %collective-permute-start.28) | collective-permute-done | bytes 294944 | tf_op jit(solution)/shard_map/ppermute | solution.py:49
  106.1 3.3 %collective-permute-start.30 = (f32[40,1152]{1,0:T(8,128)S(1)}, f32[40,1152]{1,0:T(8,128)S(1)}, u32[]{:S(2)}, u32[]{:S(2)}) collective-permute-start(f32[40,1152]{1,0:T(8,128)S(1)} %get-tuple-element.148), channel_id=1, source_target_pairs={{0,16},{16,0},{32,48},{48,32},{64,80},{80,64},{96,112},{112,96},{1... | collective-permute-start | bytes 552968 | tf_op jit(solution)/shard_map/ppermute | solution.py:456
  111.9 2.6 %collective-permute-start.32 = (bf16[48,1152]{1,0:T(8,128)(2,1)S(1)}, bf16[48,1152]{1,0:T(8,128)(2,1)S(1)}, u32[]{:S(2)}, u32[]{:S(2)}) collective-permute-start(bf16[48,1152]{1,0:T(8,128)(2,1)S(1)} %maximum_maximum_fusion), channel_id=1, source_target_pairs={{0,64},{16,80},{32,96},{48,112},{64,0},{80,16},{96,32},{112,48},{1... | collective-permute-start | bytes 331784 | tf_op jit(solution)/shard_map/ppermute | solution.py:342
  114.9 4.8 %collective-permute-done.32 = bf16[48,1152]{1,0:T(8,128)(2,1)S(1)} collective-permute-done((bf16[48,1152]{1,0:T(8,128)(2,1)S(1)}, bf16[48,1152]{1,0:T(8,128)(2,1)S(1)}, u32[]{:S(2)}, u32[]{:S(2)}) %collective-permute-start.32) | collective-permute-done | bytes 110624 | tf_op jit(solution)/shard_map/ppermute | solution.py:342
  119.7 2.6 %collective-permute-done.33 = bf16[48,1152]{1,0:T(8,128)(2,1)S(1)} collective-permute-done((bf16[48,1152]{1,0:T(8,128)(2,1)S(1)}, bf16[48,1152]{1,0:T(8,128)(2,1)S(1)}, u32[]{:S(2)}, u32[]{:S(2)}) %collective-permute-start.33) | collective-permute-done | bytes 110624 | tf_op jit(solution)/shard_map/ppermute | solution.py:342
  122.5 3.3 %collective-permute-start.34 = (bf16[48,1152]{1,0:T(8,128)(2,1)S(1)}, bf16[48,1152]{1,0:T(8,128)(2,1)S(1)}, u32[]{:S(2)}, u32[]{:S(2)}) collective-permute-start(bf16[48,1152]{1,0:T(8,128)(2,1)S(1)} %maximum_maximum_fusion.1), channel_id=1, source_target_pairs={{0,128},{16,144},{32,160},{48,176},{64,192},{80,208},{96,224},{112... | collective-permute-start | bytes 331784 | tf_op jit(solution)/shard_map/ppermute | solution.py:459
  126.6 1.8 %collective-permute-done.34 = bf16[48,1152]{1,0:T(8,128)(2,1)S(1)} collective-permute-done((bf16[48,1152]{1,0:T(8,128)(2,1)S(1)}, bf16[48,1152]{1,0:T(8,128)(2,1)S(1)}, u32[]{:S(2)}, u32[]{:S(2)}) %collective-permute-start.34) | collective-permute-done | bytes 110624 | tf_op jit(solution)/shard_map/ppermute | solution.py:459
  (96 shorter events, 35.8 us)
Async XLA Ops:
  1.4 12.5 %collective-permute-start = (bf16[512,256]{1,0:T(8,128)(2,1)}, bf16[512,256]{1,0:T(8,128)(2,1)S(1)}, u32[]{:S(2)}, u32[]{:S(2)}) collective-permute-start(bf16[512,256]{1,0:T(8,128)(2,1)} %refs_12_), channel_id=1, source_target_pairs={{0,1},{1,2},{2,3},{3,4},{4,5},{5,6},{6,7},{7,0},{8,9},{9,10},{10,1... | collective-permute-start | bytes 786440 | tf_op jit(solution)/shard_map/ppermute | solution.py:49
  7.8 8.8 %collective-permute-start.4 = (bf16[512,256]{1,0:T(8,128)(2,1)}, bf16[512,256]{1,0:T(8,128)(2,1)S(1)}, u32[]{:S(2)}, u32[]{:S(2)}) collective-permute-start(bf16[512,256]{1,0:T(8,128)(2,1)} %refs_12_), channel_id=1, source_target_pairs={{0,7},{1,0},{2,1},{3,2},{4,3},{5,4},{6,5},{7,6},{8,15},{9,8},{10,9... | collective-permute-start | bytes 786440 | tf_op jit(solution)/shard_map/ppermute | solution.py:53
  16.6 8.5 %collective-permute-start.10 = (bf16[512,256]{1,0:T(8,128)(2,1)S(1)}, bf16[512,256]{1,0:T(8,128)(2,1)S(1)}, u32[]{:S(2)}, u32[]{:S(2)}) collective-permute-start(bf16[512,256]{1,0:T(8,128)(2,1)S(1)} %collective-permute-done.4.refs_2_.refs_10_), channel_id=1, source_target_pairs={{0,8},{1,9},{2,10},{3,11},{4,12},{5,13},{6,14},{7,15},{8,0},{9,1},... | collective-permute-start | bytes 786440 | tf_op jit(solution)/shard_map/ppermute | solution.py:57
  17.8 8.6 %collective-permute-start.6 = (bf16[512,256]{1,0:T(8,128)(2,1)S(1)}, bf16[512,256]{1,0:T(8,128)(2,1)S(1)}, u32[]{:S(2)}, u32[]{:S(2)}) collective-permute-start(bf16[512,256]{1,0:T(8,128)(2,1)S(1)} %collective-permute-done.4.refs_2_.refs_10_), channel_id=1, source_target_pairs={{0,7},{1,0},{2,1},{3,2},{4,3},{5,4},{6,5},{7,6},{8,15},{9,8},{10,9... | collective-permute-start | bytes 786440 | tf_op jit(solution)/shard_map/ppermute | solution.py:53
  23.6 8.1 %collective-permute-start.5 = (bf16[512,256]{1,0:T(8,128)(2,1)S(1)}, bf16[512,256]{1,0:T(8,128)(2,1)S(1)}, u32[]{:S(2)}, u32[]{:S(2)}) collective-permute-start(bf16[512,256]{1,0:T(8,128)(2,1)S(1)} %copy-done.2), channel_id=1, source_target_pairs={{0,8},{1,9},{2,10},{3,11},{4,12},{5,13},{6,14},{7,15},{8,0},{9,1},... | collective-permute-start | bytes 786440 | tf_op jit(solution)/shard_map/ppermute | solution.py:57
  25.0 12.4 %collective-permute-start.7 = (bf16[512,256]{1,0:T(8,128)(2,1)S(1)}, bf16[512,256]{1,0:T(8,128)(2,1)S(1)}, u32[]{:S(2)}, u32[]{:S(2)}) collective-permute-start(bf16[512,256]{1,0:T(8,128)(2,1)S(1)} %collective-permute-done.refs_1_.refs_9_), channel_id=1, source_target_pairs={{0,8},{1,9},{2,10},{3,11},{4,12},{5,13},{6,14},{7,15},{8,0},{9,1},... | collective-permute-start | bytes 786440 | tf_op jit(solution)/shard_map/ppermute | solution.py:57
  25.1 17.9 %collective-permute-start.2 = (bf16[512,256]{1,0:T(8,128)(2,1)S(1)}, bf16[512,256]{1,0:T(8,128)(2,1)S(1)}, u32[]{:S(2)}, u32[]{:S(2)}) collective-permute-start(bf16[512,256]{1,0:T(8,128)(2,1)S(1)} %collective-permute-done.1.refs_4_.refs_6_), channel_id=1, source_target_pairs={{0,8},{1,9},{2,10},{3,11},{4,12},{5,13},{6,14},{7,15},{8,0},{9,1},... | collective-permute-start | bytes 786440 | tf_op jit(solution)/shard_map/ppermute | solution.py:57
  26.4 16.6 %collective-permute-start.12 = (bf16[512,256]{1,0:T(8,128)(2,1)S(1)}, bf16[512,256]{1,0:T(8,128)(2,1)S(1)}, u32[]{:S(2)}, u32[]{:S(2)}) collective-permute-start(bf16[512,256]{1,0:T(8,128)(2,1)S(1)} %collective-permute-done.10.refs_9_.refs_5_), channel_id=1, source_target_pairs={{0,7},{1,0},{2,1},{3,2},{4,3},{5,4},{6,5},{7,6},{8,15},{9,8},{10,9... | collective-permute-start | bytes 786440 | tf_op jit(solution)/shard_map/ppermute | solution.py:53
  27.0 17.5 %collective-permute-start.9 = (bf16[512,256]{1,0:T(8,128)(2,1)S(1)}, bf16[512,256]{1,0:T(8,128)(2,1)S(1)}, u32[]{:S(2)}, u32[]{:S(2)}) collective-permute-start(bf16[512,256]{1,0:T(8,128)(2,1)S(1)} %collective-permute-done.6.refs_5_.refs_7_), channel_id=1, source_target_pairs={{0,7},{1,0},{2,1},{3,2},{4,3},{5,4},{6,5},{7,6},{8,15},{9,8},{10,9... | collective-permute-start | bytes 786440 | tf_op jit(solution)/shard_map/ppermute | solution.py:53
  31.8 12.7 %collective-permute-start.11 = (bf16[512,256]{1,0:T(8,128)(2,1)S(1)}, bf16[512,256]{1,0:T(8,128)(2,1)S(1)}, u32[]{:S(2)}, u32[]{:S(2)}) collective-permute-start(bf16[512,256]{1,0:T(8,128)(2,1)S(1)} %collective-permute-done.8.refs_7_.refs_3_), channel_id=1, source_target_pairs={{0,1},{1,2},{2,3},{3,4},{4,5},{5,6},{6,7},{7,0},{8,9},{9,10},{10,1... | collective-permute-start | bytes 786440 | tf_op jit(solution)/shard_map/ppermute | solution.py:49
  43.0 8.5 %collective-permute-start.13 = (bf16[512,256]{1,0:T(8,128)(2,1)S(1)}, bf16[512,256]{1,0:T(8,128)(2,1)S(1)}, u32[]{:S(2)}, u32[]{:S(2)}) collective-permute-start(bf16[512,256]{1,0:T(8,128)(2,1)S(1)} %collective-permute-done.12.refs_11_.refs_1_), channel_id=1, source_target_pairs={{0,7},{1,0},{2,1},{3,2},{4,3},{5,4},{6,5},{7,6},{8,15},{9,8},{10,9... | collective-permute-start | bytes 786440 | tf_op jit(solution)/shard_map/ppermute | solution.py:53
  57.0 8.2 %collective-permute-start.15 = (bf16[576,256]{1,0:T(8,128)(2,1)S(1)}, bf16[576,256]{1,0:T(8,128)(2,1)S(1)}, u32[]{:S(2)}, u32[]{:S(2)}) collective-permute-start(bf16[576,256]{1,0:T(8,128)(2,1)S(1)} %get-tuple-element.96), channel_id=1, source_target_pairs={{0,8},{1,9},{2,10},{3,11},{4,12},{5,13},{6,14},{7,15},{8,0},{9,1},... | collective-permute-start | bytes 884744 | tf_op jit(solution)/shard_map/ppermute | solution.py:57
  57.5 7.7 %collective-permute-start.16 = (bf16[576,256]{1,0:T(8,128)(2,1)S(1)}, bf16[576,256]{1,0:T(8,128)(2,1)S(1)}, u32[]{:S(2)}, u32[]{:S(2)}) collective-permute-start(bf16[576,256]{1,0:T(8,128)(2,1)S(1)} %get-tuple-element.97), channel_id=1, source_target_pairs={{0,7},{1,0},{2,1},{3,2},{4,3},{5,4},{6,5},{7,6},{8,15},{9,8},{10,9... | collective-permute-start | bytes 884744 | tf_op jit(solution)/shard_map/ppermute | solution.py:53
  66.1 7.4 %collective-permute-start.20 = (bf16[576,256]{1,0:T(8,128)(2,1)S(1)}, bf16[576,256]{1,0:T(8,128)(2,1)S(1)}, u32[]{:S(2)}, u32[]{:S(2)}) collective-permute-start(bf16[576,256]{1,0:T(8,128)(2,1)S(1)} %add_convert_fusion.6), channel_id=1, source_target_pairs={{0,8},{1,9},{2,10},{3,11},{4,12},{5,13},{6,14},{7,15},{8,0},{9,1},... | collective-permute-start | bytes 884744 | tf_op jit(solution)/shard_map/ppermute | solution.py:57
  70.8 10.3 %collective-permute-start.18 = (bf16[576,256]{1,0:T(8,128)(2,1)S(1)}, bf16[576,256]{1,0:T(8,128)(2,1)S(1)}, u32[]{:S(2)}, u32[]{:S(2)}) collective-permute-start(bf16[576,256]{1,0:T(8,128)(2,1)S(1)} %add_convert_fusion.8), channel_id=1, source_target_pairs={{0,7},{1,0},{2,1},{3,2},{4,3},{5,4},{6,5},{7,6},{8,15},{9,8},{10,9... | collective-permute-start | bytes 884744 | tf_op jit(solution)/shard_map/ppermute | solution.py:53
  70.9 12.1 %collective-permute-start.22 = (bf16[576,256]{1,0:T(8,128)(2,1)S(1)}, bf16[576,256]{1,0:T(8,128)(2,1)S(1)}, u32[]{:S(2)}, u32[]{:S(2)}) collective-permute-start(bf16[576,256]{1,0:T(8,128)(2,1)S(1)} %get-tuple-element.128), channel_id=1, source_target_pairs={{0,1},{1,2},{2,3},{3,4},{4,5},{5,6},{6,7},{7,0},{8,9},{9,10},{10,1... | collective-permute-start | bytes 884744 | tf_op jit(solution)/shard_map/ppermute | solution.py:49
  81.2 8.2 %collective-permute-start.23 = (bf16[576,256]{1,0:T(8,128)(2,1)S(1)}, bf16[576,256]{1,0:T(8,128)(2,1)S(1)}, u32[]{:S(2)}, u32[]{:S(2)}) collective-permute-start(bf16[576,256]{1,0:T(8,128)(2,1)S(1)} %add_convert_fusion.4), channel_id=1, source_target_pairs={{0,8},{1,9},{2,10},{3,11},{4,12},{5,13},{6,14},{7,15},{8,0},{9,1},... | collective-permute-start | bytes 884744 | tf_op jit(solution)/shard_map/ppermute | solution.py:57
  81.3 8.0 %collective-permute-start.21 = (bf16[576,256]{1,0:T(8,128)(2,1)S(1)}, bf16[576,256]{1,0:T(8,128)(2,1)S(1)}, u32[]{:S(2)}, u32[]{:S(2)}) collective-permute-start(bf16[576,256]{1,0:T(8,128)(2,1)S(1)} %add_convert_fusion.5), channel_id=1, source_target_pairs={{0,7},{1,0},{2,1},{3,2},{4,3},{5,4},{6,5},{7,6},{8,15},{9,8},{10,9... | collective-permute-start | bytes 884744 | tf_op jit(solution)/shard_map/ppermute | solution.py:53
  81.4 14.3 %collective-permute-start.26 = (bf16[576,256]{1,0:T(8,128)(2,1)S(1)}, bf16[576,256]{1,0:T(8,128)(2,1)S(1)}, u32[]{:S(2)}, u32[]{:S(2)}) collective-permute-start(bf16[576,256]{1,0:T(8,128)(2,1)S(1)} %get-tuple-element.134), channel_id=1, source_target_pairs={{0,8},{1,9},{2,10},{3,11},{4,12},{5,13},{6,14},{7,15},{8,0},{9,1},... | collective-permute-start | bytes 884744 | tf_op jit(solution)/shard_map/ppermute | solution.py:57
  89.7 7.8 %collective-permute-start.24 = (bf16[576,256]{1,0:T(8,128)(2,1)S(1)}, bf16[576,256]{1,0:T(8,128)(2,1)S(1)}, u32[]{:S(2)}, u32[]{:S(2)}) collective-permute-start(bf16[576,256]{1,0:T(8,128)(2,1)S(1)} %add_convert_fusion.3), channel_id=1, source_target_pairs={{0,7},{1,0},{2,1},{3,2},{4,3},{5,4},{6,5},{7,6},{8,15},{9,8},{10,9... | collective-permute-start | bytes 884744 | tf_op jit(solution)/shard_map/ppermute | solution.py:53
  91.2 9.9 %collective-permute-start.29 = (bf16[576,256]{1,0:T(8,128)(2,1)S(1)}, bf16[576,256]{1,0:T(8,128)(2,1)S(1)}, u32[]{:S(2)}, u32[]{:S(2)}) collective-permute-start(bf16[576,256]{1,0:T(8,128)(2,1)S(1)} %get-tuple-element.140), channel_id=1, source_target_pairs={{0,8},{1,9},{2,10},{3,11},{4,12},{5,13},{6,14},{7,15},{8,0},{9,1},... | collective-permute-start | bytes 884744 | tf_op jit(solution)/shard_map/ppermute | solution.py:57
  97.8 7.6 %collective-permute-start.27 = (bf16[576,256]{1,0:T(8,128)(2,1)S(1)}, bf16[576,256]{1,0:T(8,128)(2,1)S(1)}, u32[]{:S(2)}, u32[]{:S(2)}) collective-permute-start(bf16[576,256]{1,0:T(8,128)(2,1)S(1)} %add_convert_fusion.1), channel_id=1, source_target_pairs={{0,7},{1,0},{2,1},{3,2},{4,3},{5,4},{6,5},{7,6},{8,15},{9,8},{10,9... | collective-permute-start | bytes 884744 | tf_op jit(solution)/shard_map/ppermute | solution.py:53
  111.9 7.8 %collective-permute-start.32 = (bf16[48,1152]{1,0:T(8,128)(2,1)S(1)}, bf16[48,1152]{1,0:T(8,128)(2,1)S(1)}, u32[]{:S(2)}, u32[]{:S(2)}) collective-permute-start(bf16[48,1152]{1,0:T(8,128)(2,1)S(1)} %maximum_maximum_fusion), channel_id=1, source_target_pairs={{0,64},{16,80},{32,96},{48,112},{64,0},{80,16},{96,32},{112,48},{1... | collective-permute-start | bytes 331784 | tf_op jit(solution)/shard_map/ppermute | solution.py:342
  114.6 7.8 %collective-permute-start.33 = (bf16[48,1152]{1,0:T(8,128)(2,1)S(1)}, bf16[48,1152]{1,0:T(8,128)(2,1)S(1)}, u32[]{:S(2)}, u32[]{:S(2)}) collective-permute-start(bf16[48,1152]{1,0:T(8,128)(2,1)S(1)} %maximum_maximum_fusion), channel_id=1, source_target_pairs={{0,96},{16,112},{32,64},{48,80},{64,32},{80,48},{96,0},{112,16},{1... | collective-permute-start | bytes 331784 | tf_op jit(solution)/shard_map/ppermute | solution.py:342
  (18 other events, 147.3 us)

commit v3 on v2

--- a/solution.py
+++ b/solution.py
@@ -12,6 +12,7 @@
 RING = 8
 PAIR = 2
 MERGE_ROWS = 512
+LANES = 128
 
 EARLY = (
     (0, 0),
@@ -305,15 +306,18 @@
         first = upper == 0
         here = pl.ds(pl.multiple_of(tokens + upper * half, half), half)
         down = sum(part[here, :].astype(jnp.float32) for part in parts) * factor
-        out[...] = jnp.zeros_like(out)
-        out[:half, :width] = jnp.where(first, up_ref[:half, :], up_ref[half:, :])
-        out[:half, width:] = down
-        out[half : half + 1, :width] = magnitude_ref[...]
+        out[:, :width] = jnp.where(first, up_ref[:half, :], up_ref[half:, :])
+        out[:, width : width + down.shape[1]] = down
+        out[:, width + down.shape[1] :] = jnp.zeros((half, LANES), jnp.float32)
+        for row in range(width // LANES):
+            out[row : row + 1, width + down.shape[1] :] = magnitude_ref[
+                :, row * LANES : (row + 1) * LANES
+            ]
 
 
 def payload(factor, tokens, rank, up_piece, magnitude_piece, parts):
     low, width = up_piece.shape
-    out = jax.ShapeDtypeStruct((low // 2 + 8, width + parts[0].shape[1]), jnp.float32)
+    out = jax.ShapeDtypeStruct((low // 2, width + parts[0].shape[1] + LANES), jnp.float32)
     return pl.pallas_call(
         functools.partial(payload_kernel, factor, tokens),
         in_specs=[SMEM] + [VMEM] * 6,
@@ -343,17 +347,17 @@
     return (f32(sent) + f32(near)) + (f32(far) + f32(both))
 
 
-def pack(array, half):
-    row = array[half : half + 1]
+def pack(array):
+    main, row = array[:, :-LANES], array[:16, -LANES:]
     high = lax.reduce_precision(row, 8, 7)
-    pad = jnp.zeros((14, array.shape[1]), jnp.float32)
-    return jnp.concatenate([array[:half], high, row - high, pad], axis=0)
-
-
-def unpack(array, half):
-    return jnp.concatenate(
-        [array[:half], array[half : half + 1] + array[half + 1 : half + 2]], axis=0
-    )
+    return jnp.concatenate([main, jnp.concatenate([high, row - high], axis=0)], axis=1)
+
+
+def unpack(array):
+    main, row = array[:, :-LANES], array[:, -LANES:]
+    row = row[:16] + row[16:]
+    row = jnp.concatenate([row, jnp.zeros_like(row)], axis=0)
+    return jnp.concatenate([main, row], axis=1)
 
 
 def together(*arrays):
@@ -376,7 +380,7 @@
     factor = 1.0 / math.sqrt(tokens * lax.axis_size("dp"))
     core = lax.axis_index("dp") % 2
     rank = jnp.stack([lax.axis_index("tensor"), 1 - 2 * core, core]).astype(jnp.int32)
-    rank, magnitude_row, own = together(rank, magnitude.reshape(1, width), own)
+    rank, own = together(rank, own)
 
     operands = (frozen_gate_weight, jnp.transpose(lowrank_down), lowrank_up)
     head = merge(0, 2, operands, ())
@@ -416,7 +420,7 @@
         merged,
         total,
         square,
-        magnitude_row,
+        magnitude.reshape(1, width),
         hidden_gradient,
         saved_up_output,
         lowrank_up,
@@ -425,40 +429,44 @@
     up_piece, *others = rest(
         factor, rank, merged, scaled, latent, both, [got[offset] for offset in REST_OUT]
     )
-    far, lower, upper, up_piece, *others = together(far, lower, upper, up_piece, *others)
-    part = dict(zip(REST_OUT, others))
-
-    in_a = down_ring(narrow(part[0, 4], far))
-    in_b = up_ring(narrow(part[1, 2], upper))
-    in_c = across(narrow(part[1, -2], lower))
-    in_a, in_b, in_c = together(in_a, in_b, in_c)
-
-    in_d = down_ring(narrow(part[0, -3], in_a))
-    in_e = up_ring(part[0, 3])
-    in_f = across(narrow(part[1, 1], in_b))
-    in_d, in_e, in_f = together(in_d, in_e, in_f)
-
-    in_g = down_ring(narrow(part[0, -2], in_c, in_d))
-    in_h = up_ring(narrow(part[0, 2], in_e))
-    in_i = across(part[1, -1])
-    in_g, in_h, in_i = together(in_g, in_h, in_i)
-
-    in_j = down_ring(narrow(part[0, -1], in_g, in_i))
-    in_k = up_ring(narrow(part[0, 1], in_f, in_h))
-    in_l = across(part[1, 0])
-    in_j, in_k, in_l = together(in_j, in_k, in_l)
-    layer_input_gradient = narrow(*[one[:tokens] for one in (part[0, 0], in_j, in_k, in_l)])
-
-    half = low // 2
+    sums = {offset: [block] for offset, block in zip(REST_OUT, others)}
+
+    def land(target, block):
+        nonlocal up_piece
+        up_piece, block = together(up_piece, block)
+        sums[target].append(block)
+
+    def send(move, source, target):
+        land(target, move(narrow(*sums[source]) if len(sums[source]) > 1 else sums[source][0]))
+
+    land((0, 4), far)
+    land((1, 2), upper)
+    land((1, -2), lower)
+    send(down_ring, (0, 4), (0, -3))
+    send(up_ring, (1, 2), (1, 1))
+    send(across, (1, -2), (0, -2))
+    send(up_ring, (0, 3), (0, 2))
+    send(down_ring, (0, -3), (0, -2))
+    send(across, (1, 1), (0, 1))
+    send(across, (1, -1), (0, -1))
+    send(up_ring, (0, 2), (0, 1))
+    send(down_ring, (0, -2), (0, -1))
+    send(across, (1, 0), (0, 0))
+    send(up_ring, (0, 1), (0, 0))
+    send(down_ring, (0, -1), (0, 0))
+    last = together(*sums[0, 0])
+    layer_input_gradient = narrow(*[one[:tokens] for one in last])
+
     kept, sent = payload(
-        factor, tokens, rank, up_piece, magnitude_piece, (part[0, 0], in_j, in_k, in_l)
+        factor, tokens, rank, up_piece, magnitude_piece, last
     )
     pieces = kept + lax.ppermute(sent, "dp", xor_perm(1))
-    pieces = unpack(sum_four(pack(pieces, half), "dp", (2, 4)), half)
-    sent = lax.optimization_barrier(pack(pieces, half).astype(jnp.bfloat16))
-    pieces = unpack(f32(sent) + f32(lax.ppermute(sent, "dp", xor_perm(8))), half)
-    mine = pieces[:half]
+    pieces = unpack(sum_four(pack(pieces), "dp", (2, 4)))
+    sent = lax.optimization_barrier(pack(pieces).astype(jnp.bfloat16))
+    pieces = unpack(f32(sent) + f32(lax.ppermute(sent, "dp", xor_perm(8))))
+    mine = pieces[:, :-LANES]
     other = lax.ppermute(mine, "dp", xor_perm(1))
+    magnitude_gradient = pieces[: width // LANES, -LANES:].reshape(width)
     summed = jnp.where(
         core == 0,
         jnp.concatenate([mine, other], axis=0),
@@ -469,7 +477,7 @@
         up_output_gradient,
         jnp.transpose(summed[:, width:]),
         summed[:, :width],
-        pieces[half, :width],
+        magnitude_gradient,
     )
 
 

time: 133 us -> 126 us (0.947)
  starting transfers between devices: 46.7 us -> 43.1 us
  waiting for transfers between devices: 55.6 us -> 53.3 us
    ppermute x10, waiting for transfers between devices: 11.3 us -> 19.6 us  [down_ring(): return lax.ppermute(array, ('dp', 'tensor'), ring_perm(-1))]
    ppermute x10, waiting for transfers between devices: 27.8 us -> 19.9 us  [across(): return lax.ppermute(array, 'tensor', xor_perm(RING))]
    ppermute x10, starting transfers between devices: 6.73 us -> 2.39 us  [down_ring(): return lax.ppermute(array, ('dp', 'tensor'), ring_perm(-1))]
    ppermute x3, waiting for transfers between devices: 7.76 us -> 5.9 us  [sum_four(): lax.ppermute(sent, axis, xor_perm(at))]
    unnamed x12 -> x14, local copies, waits for them, and re-layouts: 5.04 us -> 5.05 us
  transfers between devices with their start and end apart: 36 -> 36, of which waited for: 21 -> 19; matrix products, arithmetic and copies ran while one was open for 2% -> 2% of each run, Pallas kernels for 10% -> 11%
where the time goes in v3:
time: 126 us; the launch traced here: 125 us
  waiting for transfers between devices  53.3 us (42%)
  starting transfers between devices  43.1 us (34%)
  Pallas kernels  19.3 us (15%)
  local copies, waits for them, and re-layouts  6.42 us (5%)
  other arithmetic  2.44 us (2%)
    ppermute x10, starting transfers between devices, up_ring(): return lax.ppermute(array, ('dp', 'tensor'), ring_perm(1))  20.3 us
    ppermute x10, waiting for transfers between devices, across(): return lax.ppermute(array, 'tensor', xor_perm(RING))  19.9 us
    ppermute x10, waiting for transfers between devices, down_ring(): return lax.ppermute(array, ('dp', 'tensor'), ring_perm(-1))  19.6 us
    ppermute x10, starting transfers between devices, across(): return lax.ppermute(array, 'tensor', xor_perm(RING))  9.18 us
    ppermute x3, waiting for transfers between devices, sum_four(): lax.ppermute(sent, axis, xor_perm(at))  5.9 us
    pallas_call x1, Pallas kernels, gate_late(): pl.pallas_call(functools.partial(gate_late_kernel, factor), in_specs=[SME...  5.46 us
    unnamed x14, local copies, waits for them, and re-layouts  5.05 us
    pallas_call x1, Pallas kernels, rest(): pl.pallas_call(functools.partial(rest_kernel, factor, count), in_specs=[S...  4.99 us
  transfers between devices with their start and end apart: 36, of which 19 were waited for; matrix products, arithmetic and copies ran while one was open for 2% of the time, Pallas kernels for 11%

profile of v3, /device:TPU:1, one launch (start us, length us, event | category | flops | bytes accessed | tf_op | source)
XLA Modules:
  0.0 125.4 jit_solution(10610984586134190328)
XLA Ops:
  0.7 6.4 %collective-permute-start = (bf16[512,256]{1,0:T(8,128)(2,1)}, bf16[512,256]{1,0:T(8,128)(2,1)S(1)}, u32[]{:S(2)}, u32[]{:S(2)}) collective-permute-start(bf16[512,256]{1,0:T(8,128)(2,1)} %refs_12_), channel_id=1, source_target_pairs={{0,1},{1,2},{2,3},{3,4},{4,5},{5,6},{6,7},{7,0},{8,9},{9,10},{10,1... | collective-permute-start | bytes 786440 | tf_op jit(solution)/shard_map/ppermute | solution.py:50
  7.1 3.1 %copy-done = bf16[4096,896]{1,0:T(8,128)(2,1)S(1)} copy-done((bf16[4096,896]{1,0:T(8,128)(2,1)S(1)}, bf16[4096,896]{1,0:T(8,128)(2,1)}, u32[]{:S(2)}) %copy-start) | copy-done | bytes 7340056
  13.2 2.7 %collective-permute-start.1 = (bf16[512,256]{1,0:T(8,128)(2,1)S(1)}, bf16[512,256]{1,0:T(8,128)(2,1)S(1)}, u32[]{:S(2)}, u32[]{:S(2)}) collective-permute-start(bf16[512,256]{1,0:T(8,128)(2,1)S(1)} %collective-permute-done.refs_1_.refs_9_), channel_id=1, source_target_pairs={{0,1},{1,2},{2,3},{3,4},{4,5},{5,6},{6,7},{7,0},{8,9},{9,10},{10,1... | collective-permute-start | bytes 786440 | tf_op jit(solution)/shard_map/ppermute | solution.py:50
  17.2 3.0 %merge_tail.1 = (bf16[4096,1024]{1,0:T(8,128)(2,1)S(1)}, f32[1,896]{1,0:T(1,128)S(1)}) custom-call(bf16[4096,896]{1,0:T(8,128)(2,1)S(1)} %copy-done, bf16[64,4096]{1,0:T(8,128)(2,1)S(1)} %bitcast.9, bf16[64,896]{1,0:T(8,128)(2,1)S(1)} %copy-done.3, bf16[4096,1024]{1,0:T(8,128)(2,1)S(1)} %get-tuple-element.86.head_ref, ...), custom_call_target="tpu_custom_call", output_to_operand_aliasing={{0}: (3, {})} | custom-call | flops 352321536 | bytes 11010048 | tf_op jit(solution)/shard_map/merge_tail/pallas_call | solution.py:110
  20.2 2.7 %collective-permute-start.8 = (bf16[512,256]{1,0:T(8,128)(2,1)S(1)}, bf16[512,256]{1,0:T(8,128)(2,1)S(1)}, u32[]{:S(2)}, u32[]{:S(2)}) collective-permute-start(bf16[512,256]{1,0:T(8,128)(2,1)S(1)} %collective-permute-done.1.refs_4_.refs_6_), channel_id=1, source_target_pairs={{0,1},{1,2},{2,3},{3,4},{4,5},{5,6},{6,7},{7,0},{8,9},{9,10},{10,1... | collective-permute-start | bytes 786440 | tf_op jit(solution)/shard_map/ppermute | solution.py:50
  26.3 4.8 %collective-permute-done.5.refs_3_.refs_11_ = bf16[512,256]{1,0:T(8,128)(2,1)S(1)} collective-permute-done((bf16[512,256]{1,0:T(8,128)(2,1)S(1)}, bf16[512,256]{1,0:T(8,128)(2,1)S(1)}, u32[]{:S(2)}, u32[]{:S(2)}) %collective-permute-start.5) | collective-permute-done | bytes 262176 | tf_op jit(solution)/shard_map/ppermute | solution.py:58
  31.1 5.6 %collective-permute-done.7.refs_6_.refs_8_ = bf16[512,256]{1,0:T(8,128)(2,1)S(1)} collective-permute-done((bf16[512,256]{1,0:T(8,128)(2,1)S(1)}, bf16[512,256]{1,0:T(8,128)(2,1)S(1)}, u32[]{:S(2)}, u32[]{:S(2)}) %collective-permute-start.7) | collective-permute-done | bytes 262176 | tf_op jit(solution)/shard_map/ppermute | solution.py:58
  36.7 5.6 %collective-permute-done.2.refs_12_.refs_2_ = bf16[512,256]{1,0:T(8,128)(2,1)S(1)} collective-permute-done((bf16[512,256]{1,0:T(8,128)(2,1)S(1)}, bf16[512,256]{1,0:T(8,128)(2,1)S(1)}, u32[]{:S(2)}, u32[]{:S(2)}) %collective-permute-start.2) | collective-permute-done | bytes 262176 | tf_op jit(solution)/shard_map/ppermute | solution.py:58
  44.8 4.2 %gate_early.1.total_ref = f32[512,1024]{1,0:T(8,128)S(1)} custom-call(s32[3]{0:T(128)S(1)} %pad_add_fusion.rank_ref, bf16[512,256]{1,0:T(8,128)(2,1)S(1)} %copy-done.2, bf16[512,256]{1,0:T(8,128)(2,1)S(1)} %collective-permute-done.refs_1_.refs_9_, bf16[512,256]{1,0:T(8,128)(2,1)S(1)} %collective-permute-done.4.refs_2_.refs_10_, ...), custom_call_target="tpu_custom_call" | custom-call | flops 3489660928 | bytes 12320768 | tf_op jit(solution)/shard_map/gate_early/pallas_call | solution.py:158
  50.8 5.5 %gate_late.1 = (bf16[512,896]{1,0:T(8,128)(2,1)}, bf16[512,896]{1,0:T(8,128)(2,1)S(1)}, bf16[128,512]{1,0:T(8,128)(2,1)S(1)}, bf16[512,128]{1,0:T(8,128)(2,1)S(1...) custom-call(s32[3]{0:T(128)S(1)} %pad_add_fusion.rank_ref, ...), custom_call_target="tpu_custom_call" | custom-call | flops 1879048192 | bytes 8388608 | tf_op jit(solution)/shard_map/gate_late/pallas_call | solution.py:242
  58.3 5.0 %rest.1 = (f32[64,896]{1,0:T(8,128)S(1)}, bf16[576,256]{1,0:T(8,128)(2,1)S(1)}, bf16[576,256]{1,0:T(8,128)(2,1)S(1)}, bf16[576,256]{1,0:T(8,128)(2,1)S(1)}, bf16...) custom-call(s32[3]{0:T(128)S(1)} %pad_add_fusion.rank_ref, ...), custom_call_target="tpu_custom_call" | custom-call | flops 3053453312 | bytes 10223616 | tf_op jit(solution)/shard_map/rest/pallas_call | solution.py:284
  63.3 2.2 %collective-permute-start.21 = (bf16[576,256]{1,0:T(8,128)(2,1)S(1)}, bf16[576,256]{1,0:T(8,128)(2,1)S(1)}, u32[]{:S(2)}, u32[]{:S(2)}) collective-permute-start(bf16[576,256]{1,0:T(8,128)(2,1)S(1)} %get-tuple-element.119), channel_id=1, source_target_pairs={{0,1},{1,2},{2,3},{3,4},{4,5},{5,6},{6,7},{7,0},{8,9},{9,10},{10,1... | collective-permute-start | bytes 884744 | tf_op jit(solution)/shard_map/ppermute | solution.py:50
  66.6 3.0 %collective-permute-start.19 = (bf16[576,256]{1,0:T(8,128)(2,1)S(1)}, bf16[576,256]{1,0:T(8,128)(2,1)S(1)}, u32[]{:S(2)}, u32[]{:S(2)}) collective-permute-start(bf16[576,256]{1,0:T(8,128)(2,1)S(1)} %add_convert_fusion.7), channel_id=1, source_target_pairs={{0,1},{1,2},{2,3},{3,4},{4,5},{5,6},{6,7},{7,0},{8,9},{9,10},{10,1... | collective-permute-start | bytes 884744 | tf_op jit(solution)/shard_map/ppermute | solution.py:50
  70.3 4.3 %collective-permute-done.18 = bf16[576,256]{1,0:T(8,128)(2,1)S(1)} collective-permute-done((bf16[576,256]{1,0:T(8,128)(2,1)S(1)}, bf16[576,256]{1,0:T(8,128)(2,1)S(1)}, u32[]{:S(2)}, u32[]{:S(2)}) %collective-permute-start.18) | collective-permute-done | bytes 294944 | tf_op jit(solution)/shard_map/ppermute | solution.py:54
  74.9 3.8 %collective-permute-done.20 = bf16[576,256]{1,0:T(8,128)(2,1)S(1)} collective-permute-done((bf16[576,256]{1,0:T(8,128)(2,1)S(1)}, bf16[576,256]{1,0:T(8,128)(2,1)S(1)}, u32[]{:S(2)}, u32[]{:S(2)}) %collective-permute-start.20) | collective-permute-done | bytes 294944 | tf_op jit(solution)/shard_map/ppermute | solution.py:58
  79.6 3.1 %collective-permute-done.22 = bf16[576,256]{1,0:T(8,128)(2,1)S(1)} collective-permute-done((bf16[576,256]{1,0:T(8,128)(2,1)S(1)}, bf16[576,256]{1,0:T(8,128)(2,1)S(1)}, u32[]{:S(2)}, u32[]{:S(2)}) %collective-permute-start.22) | collective-permute-done | bytes 294944 | tf_op jit(solution)/shard_map/ppermute | solution.py:54
  86.5 2.3 %collective-permute-start.28 = (bf16[576,256]{1,0:T(8,128)(2,1)S(1)}, bf16[576,256]{1,0:T(8,128)(2,1)S(1)}, u32[]{:S(2)}, u32[]{:S(2)}) collective-permute-start(bf16[576,256]{1,0:T(8,128)(2,1)S(1)} %add_convert_fusion.1), channel_id=1, source_target_pairs={{0,1},{1,2},{2,3},{3,4},{4,5},{5,6},{6,7},{7,0},{8,9},{9,10},{10,1... | collective-permute-start | bytes 884744 | tf_op jit(solution)/shard_map/ppermute | solution.py:50
  88.8 3.9 %collective-permute-done.26 = bf16[576,256]{1,0:T(8,128)(2,1)S(1)} collective-permute-done((bf16[576,256]{1,0:T(8,128)(2,1)S(1)}, bf16[576,256]{1,0:T(8,128)(2,1)S(1)}, u32[]{:S(2)}, u32[]{:S(2)}) %collective-permute-start.26) | collective-permute-done | bytes 294944 | tf_op jit(solution)/shard_map/ppermute | solution.py:54
  94.7 7.1 %collective-permute-done.29.refs_3_ = bf16[576,256]{1,0:T(8,128)(2,1)S(1)} collective-permute-done((bf16[576,256]{1,0:T(8,128)(2,1)S(1)}, bf16[576,256]{1,0:T(8,128)(2,1)S(1)}, u32[]{:S(2)}, u32[]{:S(2)}) %collective-permute-start.29) | collective-permute-done | bytes 294944 | tf_op jit(solution)/shard_map/ppermute | solution.py:54
  102.4 2.5 %collective-permute-start.30 = (f32[32,1280]{1,0:T(8,128)S(1)}, f32[32,1280]{1,0:T(8,128)S(1)}, u32[]{:S(2)}, u32[]{:S(2)}) collective-permute-start(f32[32,1280]{1,0:T(8,128)S(1)} %get-tuple-element.156), channel_id=1, source_target_pairs={{0,16},{16,0},{32,48},{48,32},{64,80},{80,64},{96,112},{112,96},{1... | collective-permute-start | bytes 491528 | tf_op jit(solution)/shard_map/ppermute | solution.py:463
  107.3 2.6 %collective-permute-start.32 = (bf16[32,1280]{1,0:T(8,128)(2,1)S(1)}, bf16[32,1280]{1,0:T(8,128)(2,1)S(1)}, u32[]{:S(2)}, u32[]{:S(2)}) collective-permute-start(bf16[32,1280]{1,0:T(8,128)(2,1)S(1)} %maximum_maximum_fusion), channel_id=1, source_target_pairs={{0,64},{16,80},{32,96},{48,112},{64,0},{80,16},{96,32},{112,48},{1... | collective-permute-start | bytes 245768 | tf_op jit(solution)/shard_map/ppermute | solution.py:346
  109.9 3.9 %collective-permute-done.32 = bf16[32,1280]{1,0:T(8,128)(2,1)S(1)} collective-permute-done((bf16[32,1280]{1,0:T(8,128)(2,1)S(1)}, bf16[32,1280]{1,0:T(8,128)(2,1)S(1)}, u32[]{:S(2)}, u32[]{:S(2)}) %collective-permute-start.32) | collective-permute-done | bytes 81952 | tf_op jit(solution)/shard_map/ppermute | solution.py:346
  115.9 2.5 %collective-permute-start.34 = (bf16[32,1280]{1,0:T(8,128)(2,1)S(1)}, bf16[32,1280]{1,0:T(8,128)(2,1)S(1)}, u32[]{:S(2)}, u32[]{:S(2)}) collective-permute-start(bf16[32,1280]{1,0:T(8,128)(2,1)S(1)} %maximum_maximum_fusion.1), channel_id=1, source_target_pairs={{0,128},{16,144},{32,160},{48,176},{64,192},{80,208},{96,224},{112... | collective-permute-start | bytes 245768 | tf_op jit(solution)/shard_map/ppermute | solution.py:466
  120.8 2.2 %collective-permute-start.35 = (f32[32,1152]{1,0:T(8,128)S(1)}, f32[32,1152]{1,0:T(8,128)S(1)}, u32[]{:S(2)}, u32[]{:S(2)}) collective-permute-start(f32[32,1152]{1,0:T(8,128)S(1)} %slice.77), channel_id=1, source_target_pairs={{0,16},{16,0},{32,48},{48,32},{64,80},{80,64},{96,112},{112,96},{1... | collective-permute-start | bytes 442376 | tf_op jit(solution)/shard_map/ppermute | solution.py:468
  (95 shorter events, 32.5 us)
Async XLA Ops:
  0.7 12.5 %collective-permute-start = (bf16[512,256]{1,0:T(8,128)(2,1)}, bf16[512,256]{1,0:T(8,128)(2,1)S(1)}, u32[]{:S(2)}, u32[]{:S(2)}) collective-permute-start(bf16[512,256]{1,0:T(8,128)(2,1)} %refs_12_), channel_id=1, source_target_pairs={{0,1},{1,2},{2,3},{3,4},{4,5},{5,6},{6,7},{7,0},{8,9},{9,10},{10,1... | collective-permute-start | bytes 786440 | tf_op jit(solution)/shard_map/ppermute | solution.py:50
  7.1 8.8 %collective-permute-start.4 = (bf16[512,256]{1,0:T(8,128)(2,1)}, bf16[512,256]{1,0:T(8,128)(2,1)S(1)}, u32[]{:S(2)}, u32[]{:S(2)}) collective-permute-start(bf16[512,256]{1,0:T(8,128)(2,1)} %refs_12_), channel_id=1, source_target_pairs={{0,7},{1,0},{2,1},{3,2},{4,3},{5,4},{6,5},{7,6},{8,15},{9,8},{10,9... | collective-permute-start | bytes 786440 | tf_op jit(solution)/shard_map/ppermute | solution.py:54
  16.0 8.5 %collective-permute-start.10 = (bf16[512,256]{1,0:T(8,128)(2,1)S(1)}, bf16[512,256]{1,0:T(8,128)(2,1)S(1)}, u32[]{:S(2)}, u32[]{:S(2)}) collective-permute-start(bf16[512,256]{1,0:T(8,128)(2,1)S(1)} %collective-permute-done.4.refs_2_.refs_10_), channel_id=1, source_target_pairs={{0,8},{1,9},{2,10},{3,11},{4,12},{5,13},{6,14},{7,15},{8,0},{9,1},... | collective-permute-start | bytes 786440 | tf_op jit(solution)/shard_map/ppermute | solution.py:58
  17.2 8.6 %collective-permute-start.6 = (bf16[512,256]{1,0:T(8,128)(2,1)S(1)}, bf16[512,256]{1,0:T(8,128)(2,1)S(1)}, u32[]{:S(2)}, u32[]{:S(2)}) collective-permute-start(bf16[512,256]{1,0:T(8,128)(2,1)S(1)} %collective-permute-done.4.refs_2_.refs_10_), channel_id=1, source_target_pairs={{0,7},{1,0},{2,1},{3,2},{4,3},{5,4},{6,5},{7,6},{8,15},{9,8},{10,9... | collective-permute-start | bytes 786440 | tf_op jit(solution)/shard_map/ppermute | solution.py:54
  23.0 8.1 %collective-permute-start.5 = (bf16[512,256]{1,0:T(8,128)(2,1)S(1)}, bf16[512,256]{1,0:T(8,128)(2,1)S(1)}, u32[]{:S(2)}, u32[]{:S(2)}) collective-permute-start(bf16[512,256]{1,0:T(8,128)(2,1)S(1)} %copy-done.2), channel_id=1, source_target_pairs={{0,8},{1,9},{2,10},{3,11},{4,12},{5,13},{6,14},{7,15},{8,0},{9,1},... | collective-permute-start | bytes 786440 | tf_op jit(solution)/shard_map/ppermute | solution.py:58
  24.3 12.4 %collective-permute-start.7 = (bf16[512,256]{1,0:T(8,128)(2,1)S(1)}, bf16[512,256]{1,0:T(8,128)(2,1)S(1)}, u32[]{:S(2)}, u32[]{:S(2)}) collective-permute-start(bf16[512,256]{1,0:T(8,128)(2,1)S(1)} %collective-permute-done.refs_1_.refs_9_), channel_id=1, source_target_pairs={{0,8},{1,9},{2,10},{3,11},{4,12},{5,13},{6,14},{7,15},{8,0},{9,1},... | collective-permute-start | bytes 786440 | tf_op jit(solution)/shard_map/ppermute | solution.py:58
  24.4 17.9 %collective-permute-start.2 = (bf16[512,256]{1,0:T(8,128)(2,1)S(1)}, bf16[512,256]{1,0:T(8,128)(2,1)S(1)}, u32[]{:S(2)}, u32[]{:S(2)}) collective-permute-start(bf16[512,256]{1,0:T(8,128)(2,1)S(1)} %collective-permute-done.1.refs_4_.refs_6_), channel_id=1, source_target_pairs={{0,8},{1,9},{2,10},{3,11},{4,12},{5,13},{6,14},{7,15},{8,0},{9,1},... | collective-permute-start | bytes 786440 | tf_op jit(solution)/shard_map/ppermute | solution.py:58
  25.8 16.5 %collective-permute-start.12 = (bf16[512,256]{1,0:T(8,128)(2,1)S(1)}, bf16[512,256]{1,0:T(8,128)(2,1)S(1)}, u32[]{:S(2)}, u32[]{:S(2)}) collective-permute-start(bf16[512,256]{1,0:T(8,128)(2,1)S(1)} %collective-permute-done.10.refs_9_.refs_5_), channel_id=1, source_target_pairs={{0,7},{1,0},{2,1},{3,2},{4,3},{5,4},{6,5},{7,6},{8,15},{9,8},{10,9... | collective-permute-start | bytes 786440 | tf_op jit(solution)/shard_map/ppermute | solution.py:54
  26.3 17.5 %collective-permute-start.9 = (bf16[512,256]{1,0:T(8,128)(2,1)S(1)}, bf16[512,256]{1,0:T(8,128)(2,1)S(1)}, u32[]{:S(2)}, u32[]{:S(2)}) collective-permute-start(bf16[512,256]{1,0:T(8,128)(2,1)S(1)} %collective-permute-done.6.refs_5_.refs_7_), channel_id=1, source_target_pairs={{0,7},{1,0},{2,1},{3,2},{4,3},{5,4},{6,5},{7,6},{8,15},{9,8},{10,9... | collective-permute-start | bytes 786440 | tf_op jit(solution)/shard_map/ppermute | solution.py:54
  31.1 12.7 %collective-permute-start.11 = (bf16[512,256]{1,0:T(8,128)(2,1)S(1)}, bf16[512,256]{1,0:T(8,128)(2,1)S(1)}, u32[]{:S(2)}, u32[]{:S(2)}) collective-permute-start(bf16[512,256]{1,0:T(8,128)(2,1)S(1)} %collective-permute-done.8.refs_7_.refs_3_), channel_id=1, source_target_pairs={{0,1},{1,2},{2,3},{3,4},{4,5},{5,6},{6,7},{7,0},{8,9},{9,10},{10,1... | collective-permute-start | bytes 786440 | tf_op jit(solution)/shard_map/ppermute | solution.py:50
  42.3 8.4 %collective-permute-start.13 = (bf16[512,256]{1,0:T(8,128)(2,1)S(1)}, bf16[512,256]{1,0:T(8,128)(2,1)S(1)}, u32[]{:S(2)}, u32[]{:S(2)}) collective-permute-start(bf16[512,256]{1,0:T(8,128)(2,1)S(1)} %collective-permute-done.12.refs_11_.refs_1_), channel_id=1, source_target_pairs={{0,7},{1,0},{2,1},{3,2},{4,3},{5,4},{6,5},{7,6},{8,15},{9,8},{10,9... | collective-permute-start | bytes 786440 | tf_op jit(solution)/shard_map/ppermute | solution.py:54
  56.2 10.1 %collective-permute-start.15 = (bf16[576,256]{1,0:T(8,128)(2,1)S(1)}, bf16[576,256]{1,0:T(8,128)(2,1)S(1)}, u32[]{:S(2)}, u32[]{:S(2)}) collective-permute-start(bf16[576,256]{1,0:T(8,128)(2,1)S(1)} %get-tuple-element.104), channel_id=1, source_target_pairs={{0,8},{1,9},{2,10},{3,11},{4,12},{5,13},{6,14},{7,15},{8,0},{9,1},... | collective-permute-start | bytes 884744 | tf_op jit(solution)/shard_map/ppermute | solution.py:58
  56.8 9.6 %collective-permute-start.16 = (bf16[576,256]{1,0:T(8,128)(2,1)S(1)}, bf16[576,256]{1,0:T(8,128)(2,1)S(1)}, u32[]{:S(2)}, u32[]{:S(2)}) collective-permute-start(bf16[576,256]{1,0:T(8,128)(2,1)S(1)} %get-tuple-element.106), channel_id=1, source_target_pairs={{0,1},{1,2},{2,3},{3,4},{4,5},{5,6},{6,7},{7,0},{8,9},{9,10},{10,1... | collective-permute-start | bytes 884744 | tf_op jit(solution)/shard_map/ppermute | solution.py:50
  57.7 8.8 %collective-permute-start.17 = (bf16[576,256]{1,0:T(8,128)(2,1)S(1)}, bf16[576,256]{1,0:T(8,128)(2,1)S(1)}, u32[]{:S(2)}, u32[]{:S(2)}) collective-permute-start(bf16[576,256]{1,0:T(8,128)(2,1)S(1)} %get-tuple-element.108), channel_id=1, source_target_pairs={{0,7},{1,0},{2,1},{3,2},{4,3},{5,4},{6,5},{7,6},{8,15},{9,8},{10,9... | collective-permute-start | bytes 884744 | tf_op jit(solution)/shard_map/ppermute | solution.py:54
  63.3 15.4 %collective-permute-start.21 = (bf16[576,256]{1,0:T(8,128)(2,1)S(1)}, bf16[576,256]{1,0:T(8,128)(2,1)S(1)}, u32[]{:S(2)}, u32[]{:S(2)}) collective-permute-start(bf16[576,256]{1,0:T(8,128)(2,1)S(1)} %get-tuple-element.119), channel_id=1, source_target_pairs={{0,1},{1,2},{2,3},{3,4},{4,5},{5,6},{6,7},{7,0},{8,9},{9,10},{10,1... | collective-permute-start | bytes 884744 | tf_op jit(solution)/shard_map/ppermute | solution.py:50
  65.5 18.8 %collective-permute-start.24 = (bf16[576,256]{1,0:T(8,128)(2,1)S(1)}, bf16[576,256]{1,0:T(8,128)(2,1)S(1)}, u32[]{:S(2)}, u32[]{:S(2)}) collective-permute-start(bf16[576,256]{1,0:T(8,128)(2,1)S(1)} %get-tuple-element.127), channel_id=1, source_target_pairs={{0,8},{1,9},{2,10},{3,11},{4,12},{5,13},{6,14},{7,15},{8,0},{9,1},... | collective-permute-start | bytes 884744 | tf_op jit(solution)/shard_map/ppermute | solution.py:58
  66.4 8.3 %collective-permute-start.18 = (bf16[576,256]{1,0:T(8,128)(2,1)S(1)}, bf16[576,256]{1,0:T(8,128)(2,1)S(1)}, u32[]{:S(2)}, u32[]{:S(2)}) collective-permute-start(bf16[576,256]{1,0:T(8,128)(2,1)S(1)} %add_convert_fusion.8), channel_id=1, source_target_pairs={{0,7},{1,0},{2,1},{3,2},{4,3},{5,4},{6,5},{7,6},{8,15},{9,8},{10,9... | collective-permute-start | bytes 884744 | tf_op jit(solution)/shard_map/ppermute | solution.py:54
  66.6 8.3 %collective-permute-start.19 = (bf16[576,256]{1,0:T(8,128)(2,1)S(1)}, bf16[576,256]{1,0:T(8,128)(2,1)S(1)}, u32[]{:S(2)}, u32[]{:S(2)}) collective-permute-start(bf16[576,256]{1,0:T(8,128)(2,1)S(1)} %add_convert_fusion.7), channel_id=1, source_target_pairs={{0,1},{1,2},{2,3},{3,4},{4,5},{5,6},{6,7},{7,0},{8,9},{9,10},{10,1... | collective-permute-start | bytes 884744 | tf_op jit(solution)/shard_map/ppermute | solution.py:50
  69.6 9.1 %collective-permute-start.20 = (bf16[576,256]{1,0:T(8,128)(2,1)S(1)}, bf16[576,256]{1,0:T(8,128)(2,1)S(1)}, u32[]{:S(2)}, u32[]{:S(2)}) collective-permute-start(bf16[576,256]{1,0:T(8,128)(2,1)S(1)} %add_convert_fusion.6), channel_id=1, source_target_pairs={{0,8},{1,9},{2,10},{3,11},{4,12},{5,13},{6,14},{7,15},{8,0},{9,1},... | collective-permute-start | bytes 884744 | tf_op jit(solution)/shard_map/ppermute | solution.py:58
  74.7 8.0 %collective-permute-start.22 = (bf16[576,256]{1,0:T(8,128)(2,1)S(1)}, bf16[576,256]{1,0:T(8,128)(2,1)S(1)}, u32[]{:S(2)}, u32[]{:S(2)}) collective-permute-start(bf16[576,256]{1,0:T(8,128)(2,1)S(1)} %add_convert_fusion.5), channel_id=1, source_target_pairs={{0,7},{1,0},{2,1},{3,2},{4,3},{5,4},{6,5},{7,6},{8,15},{9,8},{10,9... | collective-permute-start | bytes 884744 | tf_op jit(solution)/shard_map/ppermute | solution.py:54
  82.8 9.9 %collective-permute-start.26 = (bf16[576,256]{1,0:T(8,128)(2,1)S(1)}, bf16[576,256]{1,0:T(8,128)(2,1)S(1)}, u32[]{:S(2)}, u32[]{:S(2)}) collective-permute-start(bf16[576,256]{1,0:T(8,128)(2,1)S(1)} %add_convert_fusion.2), channel_id=1, source_target_pairs={{0,7},{1,0},{2,1},{3,2},{4,3},{5,4},{6,5},{7,6},{8,15},{9,8},{10,9... | collective-permute-start | bytes 884744 | tf_op jit(solution)/shard_map/ppermute | solution.py:54
  82.9 10.0 %collective-permute-start.27 = (bf16[576,256]{1,0:T(8,128)(2,1)S(1)}, bf16[576,256]{1,0:T(8,128)(2,1)S(1)}, u32[]{:S(2)}, u32[]{:S(2)}) collective-permute-start(bf16[576,256]{1,0:T(8,128)(2,1)S(1)} %get-tuple-element.136), channel_id=1, source_target_pairs={{0,8},{1,9},{2,10},{3,11},{4,12},{5,13},{6,14},{7,15},{8,0},{9,1},... | collective-permute-start | bytes 884744 | tf_op jit(solution)/shard_map/ppermute | solution.py:58
  86.5 8.2 %collective-permute-start.28 = (bf16[576,256]{1,0:T(8,128)(2,1)S(1)}, bf16[576,256]{1,0:T(8,128)(2,1)S(1)}, u32[]{:S(2)}, u32[]{:S(2)}) collective-permute-start(bf16[576,256]{1,0:T(8,128)(2,1)S(1)} %add_convert_fusion.1), channel_id=1, source_target_pairs={{0,1},{1,2},{2,3},{3,4},{4,5},{5,6},{6,7},{7,0},{8,9},{9,10},{10,1... | collective-permute-start | bytes 884744 | tf_op jit(solution)/shard_map/ppermute | solution.py:50
  92.8 8.9 %collective-permute-start.29 = (bf16[576,256]{1,0:T(8,128)(2,1)S(1)}, bf16[576,256]{1,0:T(8,128)(2,1)S(1)}, u32[]{:S(2)}, u32[]{:S(2)}) collective-permute-start(bf16[576,256]{1,0:T(8,128)(2,1)S(1)} %add_convert_fusion), channel_id=1, source_target_pairs={{0,7},{1,0},{2,1},{3,2},{4,3},{5,4},{6,5},{7,6},{8,15},{9,8},{10,9... | collective-permute-start | bytes 884744 | tf_op jit(solution)/shard_map/ppermute | solution.py:54
  (19 other events, 161.6 us)

commit v4 on v3

--- a/solution.py
+++ b/solution.py
@@ -198,7 +198,7 @@
     low = lowrank_up_ref.shape[0]
     norms = jnp.sqrt(square_ref[...] + EPSILON)
     scales = magnitude_ref[...] / norms
-    tile = 128
+    tile = tokens
     starts = [row_of(rank, offset, height, sign) for offset in LATE]
     magnitude_piece_ref[...] = jnp.zeros_like(magnitude_piece_ref)
 
@@ -329,6 +329,32 @@
     )(rank, up_piece, magnitude_piece, *parts)
 
 
+def finish_kernel(rank_ref, mine_ref, other_ref, up_ref, down_ref):
+    half, width = mine_ref.shape[0], up_ref.shape[1]
+    first = rank_ref[2] == 0
+    for at in range(2):
+        here = slice(at * half, (at + 1) * half)
+        rows = jnp.where(first == (at == 0), mine_ref[...], other_ref[...])
+        up_ref[here, :] = rows[:, :width]
+        down_ref[here, :] = rows[:, width:]
+
+
+def finish(rank, mine, other, width):
+    half, wide = mine.shape
+    return pl.pallas_call(
+        finish_kernel,
+        in_specs=[SMEM] + [VMEM] * 2,
+        out_specs=[VMEM] * 2,
+        out_shape=[
+            jax.ShapeDtypeStruct((2 * half, width), jnp.float32),
+            jax.ShapeDtypeStruct((2 * half, wide - width), jnp.float32),
+        ],
+        compiler_params=pltpu.CompilerParams(vmem_limit_bytes=6 * 2**20),
+        cost_estimate=pl.CostEstimate(flops=2**16, bytes_accessed=2**20, transcendentals=0),
+        name="finish",
+    )(rank, mine, other)
+
+
 def f32(array):
     return array.astype(jnp.float32)
 
@@ -383,33 +409,35 @@
     rank, own = together(rank, own)
 
     operands = (frozen_gate_weight, jnp.transpose(lowrank_down), lowrank_up)
-    head = merge(0, 2, operands, ())
+    head = merge(0, 1, operands, ())
 
     got = {(0, 0): own}
     token = own[:16, :128]
 
-    def arrive(move, source, target, *more):
+    def arrive(move, source, target, *more, after=None):
         nonlocal token
-        block = move(got[source])
-        token, got[target], *more = together(token, block, *more)
+        block = got[source]
+        if after is not None:
+            block, _ = together(block, got[after])
+        token, got[target], *more = together(token, move(block), *more)
         return more
 
-    head = arrive(up_ring, (0, 0), (0, -1), *head)
-    arrive(down_ring, (0, 0), (0, 1))
-    arrive(across, (0, 0), (1, 0))
-    merged, square = merge(2, 6, operands, head)
+    got[0, -1], got[0, 1], got[1, 0], *head = together(
+        up_ring(own), down_ring(own), across(own), *head
+    )
+    merged, square = merge(1, 7, operands, head)
     merged, square = arrive(up_ring, (0, -1), (0, -2), merged, square)
+    arrive(across, (0, 1), (1, 1))
     arrive(down_ring, (0, 1), (0, 2))
-    arrive(across, (0, -1), (1, -1))
     arrive(up_ring, (0, -2), (0, -3))
-    arrive(down_ring, (0, 2), (0, 3))
-    arrive(across, (0, 1), (1, 1))
+    arrive(across, (0, -2), (1, -2))
+    arrive(down_ring, (1, 1), (1, 2), after=(0, -2))
     arrive(up_ring, (0, -3), (0, 4))
-    arrive(down_ring, (1, 1), (1, 2))
-    arrive(across, (0, -2), (1, -2))
+    arrive(across, (0, -1), (1, -1), after=(0, -3))
+    arrive(down_ring, (0, 2), (0, 3), after=(0, -3))
     total = gate_early(rank, [got[offset] for offset in EARLY], merged)
-    (total,) = arrive(up_ring, (1, -2), (1, -3), total)
-    arrive(down_ring, (1, 2), (1, 3))
+    (total,) = arrive(up_ring, (1, -2), (1, -3), total, after=(0, -3))
+    arrive(down_ring, (1, 2), (1, 3), after=(0, -3))
     arrive(across, (0, 4), (1, 4))
     *late, total = together(*[got[offset] for offset in LATE], total)
 
@@ -429,7 +457,10 @@
     up_piece, *others = rest(
         factor, rank, merged, scaled, latent, both, [got[offset] for offset in REST_OUT]
     )
+    far, lower, up_piece, *others = together(far, lower, up_piece, *others)
     sums = {offset: [block] for offset, block in zip(REST_OUT, others)}
+    sums[0, 4].append(far)
+    sums[1, -2].append(lower)
 
     def land(target, block):
         nonlocal up_piece
@@ -439,9 +470,7 @@
     def send(move, source, target):
         land(target, move(narrow(*sums[source]) if len(sums[source]) > 1 else sums[source][0]))
 
-    land((0, 4), far)
     land((1, 2), upper)
-    land((1, -2), lower)
     send(down_ring, (0, 4), (0, -3))
     send(up_ring, (1, 2), (1, 1))
     send(across, (1, -2), (0, -2))
@@ -466,17 +495,13 @@
     pieces = unpack(f32(sent) + f32(lax.ppermute(sent, "dp", xor_perm(8))))
     mine = pieces[:, :-LANES]
     other = lax.ppermute(mine, "dp", xor_perm(1))
+    lowrank_up_gradient, down_gradient = finish(rank, mine, other, width)
     magnitude_gradient = pieces[: width // LANES, -LANES:].reshape(width)
-    summed = jnp.where(
-        core == 0,
-        jnp.concatenate([mine, other], axis=0),
-        jnp.concatenate([other, mine], axis=0),
-    )
     return (
         layer_input_gradient,
         up_output_gradient,
-        jnp.transpose(summed[:, width:]),
-        summed[:, :width],
+        jnp.transpose(down_gradient),
+        lowrank_up_gradient,
         magnitude_gradient,
     )
 

time: 126 us -> 122 us (0.968)
  waiting for transfers between devices: 53.3 us -> 33.1 us
  starting transfers between devices: 43.1 us -> 58.7 us
    ppermute x10, waiting for transfers between devices: 19.9 us -> 2.07 us  [across(): return lax.ppermute(array, 'tensor', xor_perm(RING))]
    ppermute x10, starting transfers between devices: 20.3 us -> 27.4 us  [up_ring(): return lax.ppermute(array, ('dp', 'tensor'), ring_perm(1))]
    ppermute x1, starting transfers between devices: 2.52 us -> 7.73 us  [per_device(): pieces = kept + lax.ppermute(sent, 'dp', xor_perm(1))]
    ppermute x10, starting transfers between devices: 9.18 us -> 11.3 us  [across(): return lax.ppermute(array, 'tensor', xor_perm(RING))]
    ppermute x10, waiting for transfers between devices: 4.86 us -> 6.65 us  [up_ring(): return lax.ppermute(array, ('dp', 'tensor'), ring_perm(1))]
    ppermute x10, waiting for transfers between devices: 19.6 us -> 17.8 us  [down_ring(): return lax.ppermute(array, ('dp', 'tensor'), ring_perm(-1))]
    ppermute x3, waiting for transfers between devices: 5.9 us -> 4.12 us  [sum_four(): lax.ppermute(sent, axis, xor_perm(at))]
    pallas_call x0 -> x1, Pallas kernels: none -> 1.27 us  [finish(): pl.pallas_call(finish_kernel, in_specs=[SMEM] + [VMEM] * 2, out_specs=[VM...]
where the time goes in v4:
time: 122 us; the launch traced here: 120 us
  starting transfers between devices  58.7 us (48%)
  waiting for transfers between devices  33.1 us (27%)
  Pallas kernels  19.3 us (16%)
  local copies, waits for them, and re-layouts  5.98 us (5%)
  other arithmetic  2.4 us (2%)
    ppermute x10, starting transfers between devices, up_ring(): return lax.ppermute(array, ('dp', 'tensor'), ring_perm(1))  27.4 us
    ppermute x10, waiting for transfers between devices, down_ring(): return lax.ppermute(array, ('dp', 'tensor'), ring_perm(-1))  17.8 us
    ppermute x10, starting transfers between devices, across(): return lax.ppermute(array, 'tensor', xor_perm(RING))  11.3 us
    ppermute x1, starting transfers between devices, per_device(): pieces = kept + lax.ppermute(sent, 'dp', xor_perm(1))  7.73 us
    ppermute x10, waiting for transfers between devices, up_ring(): return lax.ppermute(array, ('dp', 'tensor'), ring_perm(1))  6.65 us
    unnamed x16, local copies, waits for them, and re-layouts  5.94 us
    pallas_call x1, Pallas kernels, rest(): pl.pallas_call(functools.partial(rest_kernel, factor, count), in_specs=[S...  4.99 us
    pallas_call x1, Pallas kernels, gate_early(): pl.pallas_call(functools.partial(gate_early_kernel, count), in_specs=[SME...  4.23 us
  transfers between devices with their start and end apart: 36, of which 19 were waited for; matrix products, arithmetic and copies ran while one was open for 2% of the time, Pallas kernels for 11%

profile of v4, /device:TPU:1, one launch (start us, length us, event | category | flops | bytes accessed | tf_op | source)
XLA Modules:
  0.0 120.4 jit_solution(17784150110230347516)
XLA Ops:
  0.7 2.1 %collective-permute-start.2 = (bf16[512,256]{1,0:T(8,128)(2,1)}, bf16[512,256]{1,0:T(8,128)(2,1)S(1)}, u32[]{:S(2)}, u32[]{:S(2)}) collective-permute-start(bf16[512,256]{1,0:T(8,128)(2,1)} %refs_12_), channel_id=1, source_target_pairs={{0,8},{1,9},{2,10},{3,11},{4,12},{5,13},{6,14},{7,15},{8,0},{9,1},... | collective-permute-start | bytes 786440 | tf_op jit(solution)/shard_map/ppermute | solution.py:58
  4.4 3.9 %collective-permute-start = (bf16[512,256]{1,0:T(8,128)(2,1)}, bf16[512,256]{1,0:T(8,128)(2,1)S(1)}, u32[]{:S(2)}, u32[]{:S(2)}) collective-permute-start(bf16[512,256]{1,0:T(8,128)(2,1)} %refs_12_), channel_id=1, source_target_pairs={{0,1},{1,2},{2,3},{3,4},{4,5},{5,6},{6,7},{7,0},{8,9},{9,10},{10,1... | collective-permute-start | bytes 786440 | tf_op jit(solution)/shard_map/ppermute | solution.py:50
  8.4 3.1 %copy-done = bf16[4096,896]{1,0:T(8,128)(2,1)S(1)} copy-done((bf16[4096,896]{1,0:T(8,128)(2,1)S(1)}, bf16[4096,896]{1,0:T(8,128)(2,1)}, u32[]{:S(2)}) %copy-start) | copy-done | bytes 7340056
  13.9 2.7 %collective-permute-start.3 = (bf16[512,256]{1,0:T(8,128)(2,1)S(1)}, bf16[512,256]{1,0:T(8,128)(2,1)S(1)}, u32[]{:S(2)}, u32[]{:S(2)}) collective-permute-start(bf16[512,256]{1,0:T(8,128)(2,1)S(1)} %collective-permute-done.refs_1_.refs_9_), channel_id=1, source_target_pairs={{0,1},{1,2},{2,3},{3,4},{4,5},{5,6},{6,7},{7,0},{8,9},{9,10},{10,1... | collective-permute-start | bytes 786440 | tf_op jit(solution)/shard_map/ppermute | solution.py:50
  17.8 3.5 %merge_tail.1 = (bf16[4096,1024]{1,0:T(8,128)(2,1)S(1)}, f32[1,896]{1,0:T(1,128)S(1)}) custom-call(bf16[4096,896]{1,0:T(8,128)(2,1)S(1)} %copy-done, bf16[64,4096]{1,0:T(8,128)(2,1)S(1)} %bitcast.8, bf16[64,896]{1,0:T(8,128)(2,1)S(1)} %copy-done.4, bf16[4096,1024]{1,0:T(8,128)(2,1)S(1)} %get-tuple-element.107.head_ref, ...), custom_call_target="tpu_custom_call", output_to_operand_aliasing={{0}: (3, {})} | custom-call | flops 411041792 | bytes 12845056 | tf_op jit(solution)/shard_map/merge_tail/pallas_call | solution.py:110
  21.3 2.8 %collective-permute-start.5 = (bf16[512,256]{1,0:T(8,128)(2,1)S(1)}, bf16[512,256]{1,0:T(8,128)(2,1)S(1)}, u32[]{:S(2)}, u32[]{:S(2)}) collective-permute-start(bf16[512,256]{1,0:T(8,128)(2,1)S(1)} %collective-permute-done.3.refs_4_.refs_6_), channel_id=1, source_target_pairs={{0,1},{1,2},{2,3},{3,4},{4,5},{5,6},{6,7},{7,0},{8,9},{9,10},{10,1... | collective-permute-start | bytes 786440 | tf_op jit(solution)/shard_map/ppermute | solution.py:50
  27.5 3.1 %collective-permute-start.11 = (bf16[512,256]{1,0:T(8,128)(2,1)S(1)}, bf16[512,256]{1,0:T(8,128)(2,1)S(1)}, u32[]{:S(2)}, u32[]{:S(2)}) collective-permute-start(bf16[512,256]{1,0:T(8,128)(2,1)S(1)} %collective-permute-done.5.refs_7_.refs_3_), channel_id=1, source_target_pairs={{0,1},{1,2},{2,3},{3,4},{4,5},{5,6},{6,7},{7,0},{8,9},{9,10},{10,1... | collective-permute-start | bytes 786440 | tf_op jit(solution)/shard_map/ppermute | solution.py:50
  31.8 2.7 %collective-permute-start.6 = (bf16[512,256]{1,0:T(8,128)(2,1)S(1)}, bf16[512,256]{1,0:T(8,128)(2,1)S(1)}, u32[]{:S(2)}, u32[]{:S(2)}) collective-permute-start(bf16[512,256]{1,0:T(8,128)(2,1)S(1)} %collective-permute-done.4.refs_12_.refs_2_), channel_id=1, source_target_pairs={{0,1},{1,2},{2,3},{3,4},{4,5},{5,6},{6,7},{7,0},{8,9},{9,10},{10,1... | collective-permute-start | bytes 786440 | tf_op jit(solution)/shard_map/ppermute | solution.py:50
  35.5 2.2 %collective-permute-start.14 = (bf16[512,256]{1,0:T(8,128)(2,1)S(1)}, bf16[512,256]{1,0:T(8,128)(2,1)S(1)}, u32[]{:S(2)}, u32[]{:S(2)}) collective-permute-start(bf16[512,256]{1,0:T(8,128)(2,1)S(1)} %collective-permute-done.11.refs_10_.refs_0_), channel_id=1, source_target_pairs={{0,8},{1,9},{2,10},{3,11},{4,12},{5,13},{6,14},{7,15},{8,0},{9,1},... | collective-permute-start | bytes 786440 | tf_op jit(solution)/shard_map/ppermute | solution.py:58
  38.2 4.2 %gate_early.1.total_ref = f32[512,1024]{1,0:T(8,128)S(1)} custom-call(s32[3]{0:T(128)S(1)} %pad_add_fusion.rank_ref, bf16[512,256]{1,0:T(8,128)(2,1)S(1)} %copy-done.2, bf16[512,256]{1,0:T(8,128)(2,1)S(1)} %collective-permute-done.refs_1_.refs_9_, bf16[512,256]{1,0:T(8,128)(2,1)S(1)} %collective-permute-done.1.refs_2_.refs_10_, ...), custom_call_target="tpu_custom_call" | custom-call | flops 3489660928 | bytes 12320768 | tf_op jit(solution)/shard_map/gate_early/pallas_call | solution.py:158
  44.0 4.2 %gate_late.1 = (bf16[512,896]{1,0:T(8,128)(2,1)}, bf16[512,896]{1,0:T(8,128)(2,1)S(1)}, bf16[128,512]{1,0:T(8,128)(2,1)S(1)}, bf16[512,128]{1,0:T(8,128)(2,1)S(1...) custom-call(s32[3]{0:T(128)S(1)} %pad_add_fusion.rank_ref, ...), custom_call_target="tpu_custom_call" | custom-call | flops 1879048192 | bytes 8388608 | tf_op jit(solution)/shard_map/gate_late/pallas_call | solution.py:242
  48.7 3.0 %collective-permute-start.17 = (bf16[576,256]{1,0:T(8,128)(2,1)S(1)}, bf16[576,256]{1,0:T(8,128)(2,1)S(1)}, u32[]{:S(2)}, u32[]{:S(2)}) collective-permute-start(bf16[576,256]{1,0:T(8,128)(2,1)S(1)} %get-tuple-element.148), channel_id=1, source_target_pairs={{0,1},{1,2},{2,3},{3,4},{4,5},{5,6},{6,7},{7,0},{8,9},{9,10},{10,1... | collective-permute-start | bytes 884744 | tf_op jit(solution)/shard_map/ppermute | solution.py:50
  51.7 5.0 %rest.1 = (f32[64,896]{1,0:T(8,128)S(1)}, bf16[576,256]{1,0:T(8,128)(2,1)S(1)}, bf16[576,256]{1,0:T(8,128)(2,1)S(1)}, bf16[576,256]{1,0:T(8,128)(2,1)S(1)}, bf16...) custom-call(s32[3]{0:T(128)S(1)} %pad_add_fusion.rank_ref, ...), custom_call_target="tpu_custom_call" | custom-call | flops 3053453312 | bytes 10223616 | tf_op jit(solution)/shard_map/rest/pallas_call | solution.py:284
  57.0 3.0 %collective-permute-start.19 = (bf16[576,256]{1,0:T(8,128)(2,1)S(1)}, bf16[576,256]{1,0:T(8,128)(2,1)S(1)}, u32[]{:S(2)}, u32[]{:S(2)}) collective-permute-start(bf16[576,256]{1,0:T(8,128)(2,1)S(1)} %add_convert_fusion.7), channel_id=1, source_target_pairs={{0,1},{1,2},{2,3},{3,4},{4,5},{5,6},{6,7},{7,0},{8,9},{9,10},{10,1... | collective-permute-start | bytes 884744 | tf_op jit(solution)/shard_map/ppermute | solution.py:50
  61.8 5.0 %collective-permute-done.18 = bf16[576,256]{1,0:T(8,128)(2,1)S(1)} collective-permute-done((bf16[576,256]{1,0:T(8,128)(2,1)S(1)}, bf16[576,256]{1,0:T(8,128)(2,1)S(1)}, u32[]{:S(2)}, u32[]{:S(2)}) %collective-permute-start.18) | collective-permute-done | bytes 294944 | tf_op jit(solution)/shard_map/ppermute | solution.py:54
  70.5 2.4 %collective-permute-start.25 = (bf16[576,256]{1,0:T(8,128)(2,1)S(1)}, bf16[576,256]{1,0:T(8,128)(2,1)S(1)}, u32[]{:S(2)}, u32[]{:S(2)}) collective-permute-start(bf16[576,256]{1,0:T(8,128)(2,1)S(1)} %add_convert_fusion.3), channel_id=1, source_target_pairs={{0,1},{1,2},{2,3},{3,4},{4,5},{5,6},{6,7},{7,0},{8,9},{9,10},{10,1... | collective-permute-start | bytes 884744 | tf_op jit(solution)/shard_map/ppermute | solution.py:50
  72.9 3.0 %collective-permute-done.22 = bf16[576,256]{1,0:T(8,128)(2,1)S(1)} collective-permute-done((bf16[576,256]{1,0:T(8,128)(2,1)S(1)}, bf16[576,256]{1,0:T(8,128)(2,1)S(1)}, u32[]{:S(2)}, u32[]{:S(2)}) %collective-permute-start.22) | collective-permute-done | bytes 294944 | tf_op jit(solution)/shard_map/ppermute | solution.py:54
  78.2 3.5 %collective-permute-start.28 = (bf16[576,256]{1,0:T(8,128)(2,1)S(1)}, bf16[576,256]{1,0:T(8,128)(2,1)S(1)}, u32[]{:S(2)}, u32[]{:S(2)}) collective-permute-start(bf16[576,256]{1,0:T(8,128)(2,1)S(1)} %add_convert_fusion.1), channel_id=1, source_target_pairs={{0,1},{1,2},{2,3},{3,4},{4,5},{5,6},{6,7},{7,0},{8,9},{9,10},{10,1... | collective-permute-start | bytes 884744 | tf_op jit(solution)/shard_map/ppermute | solution.py:50
  85.3 6.9 %collective-permute-done.29.refs_3_ = bf16[576,256]{1,0:T(8,128)(2,1)S(1)} collective-permute-done((bf16[576,256]{1,0:T(8,128)(2,1)S(1)}, bf16[576,256]{1,0:T(8,128)(2,1)S(1)}, u32[]{:S(2)}, u32[]{:S(2)}) %collective-permute-start.29) | collective-permute-done | bytes 294944 | tf_op jit(solution)/shard_map/ppermute | solution.py:54
  92.9 7.7 %collective-permute-start.30 = (f32[32,1280]{1,0:T(8,128)S(1)}, f32[32,1280]{1,0:T(8,128)S(1)}, u32[]{:S(2)}, u32[]{:S(2)}) collective-permute-start(f32[32,1280]{1,0:T(8,128)S(1)} %get-tuple-element.196), channel_id=1, source_target_pairs={{0,16},{16,0},{32,48},{48,32},{64,80},{80,64},{96,112},{112,96},{1... | collective-permute-start | bytes 491528 | tf_op jit(solution)/shard_map/ppermute | solution.py:492
  101.7 2.9 %collective-permute-start.33 = (bf16[32,1280]{1,0:T(8,128)(2,1)S(1)}, bf16[32,1280]{1,0:T(8,128)(2,1)S(1)}, u32[]{:S(2)}, u32[]{:S(2)}) collective-permute-start(bf16[32,1280]{1,0:T(8,128)(2,1)S(1)} %maximum_maximum_fusion), channel_id=1, source_target_pairs={{0,96},{16,112},{32,64},{48,80},{64,32},{80,48},{96,0},{112,16},{1... | collective-permute-start | bytes 245768 | tf_op jit(solution)/shard_map/ppermute | solution.py:372
  105.2 2.6 %collective-permute-done.33 = bf16[32,1280]{1,0:T(8,128)(2,1)S(1)} collective-permute-done((bf16[32,1280]{1,0:T(8,128)(2,1)S(1)}, bf16[32,1280]{1,0:T(8,128)(2,1)S(1)}, u32[]{:S(2)}, u32[]{:S(2)}) %collective-permute-start.33) | collective-permute-done | bytes 81952 | tf_op jit(solution)/shard_map/ppermute | solution.py:372
  109.4 3.4 %collective-permute-start.34 = (bf16[32,1280]{1,0:T(8,128)(2,1)S(1)}, bf16[32,1280]{1,0:T(8,128)(2,1)S(1)}, u32[]{:S(2)}, u32[]{:S(2)}) collective-permute-start(bf16[32,1280]{1,0:T(8,128)(2,1)S(1)} %maximum_maximum_fusion.1), channel_id=1, source_target_pairs={{0,128},{16,144},{32,160},{48,176},{64,192},{80,208},{96,224},{112... | collective-permute-start | bytes 245768 | tf_op jit(solution)/shard_map/ppermute | solution.py:495
  114.8 3.4 %collective-permute-start.35 = (f32[32,1152]{1,0:T(8,128)S(1)}, f32[32,1152]{1,0:T(8,128)S(1)}, u32[]{:S(2)}, u32[]{:S(2)}) collective-permute-start(f32[32,1152]{1,0:T(8,128)S(1)} %slice.66.mine_ref), channel_id=1, source_target_pairs={{0,16},{16,0},{32,48},{48,32},{64,80},{80,64},{96,112},{112,96},{1... | collective-permute-start | bytes 442376 | tf_op jit(solution)/shard_map/ppermute | solution.py:497
  (95 shorter events, 33.1 us)
Async XLA Ops:
  0.7 13.2 %collective-permute-start.2 = (bf16[512,256]{1,0:T(8,128)(2,1)}, bf16[512,256]{1,0:T(8,128)(2,1)S(1)}, u32[]{:S(2)}, u32[]{:S(2)}) collective-permute-start(bf16[512,256]{1,0:T(8,128)(2,1)} %refs_12_), channel_id=1, source_target_pairs={{0,8},{1,9},{2,10},{3,11},{4,12},{5,13},{6,14},{7,15},{8,0},{9,1},... | collective-permute-start | bytes 786440 | tf_op jit(solution)/shard_map/ppermute | solution.py:58
  2.8 11.1 %collective-permute-start.1 = (bf16[512,256]{1,0:T(8,128)(2,1)}, bf16[512,256]{1,0:T(8,128)(2,1)S(1)}, u32[]{:S(2)}, u32[]{:S(2)}) collective-permute-start(bf16[512,256]{1,0:T(8,128)(2,1)} %refs_12_), channel_id=1, source_target_pairs={{0,7},{1,0},{2,1},{3,2},{4,3},{5,4},{6,5},{7,6},{8,15},{9,8},{10,9... | collective-permute-start | bytes 786440 | tf_op jit(solution)/shard_map/ppermute | solution.py:54
  4.4 9.5 %collective-permute-start = (bf16[512,256]{1,0:T(8,128)(2,1)}, bf16[512,256]{1,0:T(8,128)(2,1)S(1)}, u32[]{:S(2)}, u32[]{:S(2)}) collective-permute-start(bf16[512,256]{1,0:T(8,128)(2,1)} %refs_12_), channel_id=1, source_target_pairs={{0,1},{1,2},{2,3},{3,4},{4,5},{5,6},{6,7},{7,0},{8,9},{9,10},{10,1... | collective-permute-start | bytes 786440 | tf_op jit(solution)/shard_map/ppermute | solution.py:50
  16.6 8.7 %collective-permute-start.10 = (bf16[512,256]{1,0:T(8,128)(2,1)S(1)}, bf16[512,256]{1,0:T(8,128)(2,1)S(1)}, u32[]{:S(2)}, u32[]{:S(2)}) collective-permute-start(bf16[512,256]{1,0:T(8,128)(2,1)S(1)} %collective-permute-done.1.refs_2_.refs_10_), channel_id=1, source_target_pairs={{0,8},{1,9},{2,10},{3,11},{4,12},{5,13},{6,14},{7,15},{8,0},{9,1},... | collective-permute-start | bytes 786440 | tf_op jit(solution)/shard_map/ppermute | solution.py:58
  16.9 8.6 %collective-permute-start.7 = (bf16[512,256]{1,0:T(8,128)(2,1)S(1)}, bf16[512,256]{1,0:T(8,128)(2,1)S(1)}, u32[]{:S(2)}, u32[]{:S(2)}) collective-permute-start(bf16[512,256]{1,0:T(8,128)(2,1)S(1)} %collective-permute-done.1.refs_2_.refs_10_), channel_id=1, source_target_pairs={{0,7},{1,0},{2,1},{3,2},{4,3},{5,4},{6,5},{7,6},{8,15},{9,8},{10,9... | collective-permute-start | bytes 786440 | tf_op jit(solution)/shard_map/ppermute | solution.py:54
  24.1 7.7 %collective-permute-start.4 = (bf16[512,256]{1,0:T(8,128)(2,1)S(1)}, bf16[512,256]{1,0:T(8,128)(2,1)S(1)}, u32[]{:S(2)}, u32[]{:S(2)}) collective-permute-start(bf16[512,256]{1,0:T(8,128)(2,1)S(1)} %collective-permute-done.3.refs_4_.refs_6_), channel_id=1, source_target_pairs={{0,8},{1,9},{2,10},{3,11},{4,12},{5,13},{6,14},{7,15},{8,0},{9,1},... | collective-permute-start | bytes 786440 | tf_op jit(solution)/shard_map/ppermute | solution.py:58
  25.3 9.3 %collective-permute-start.12 = (bf16[512,256]{1,0:T(8,128)(2,1)S(1)}, bf16[512,256]{1,0:T(8,128)(2,1)S(1)}, u32[]{:S(2)}, u32[]{:S(2)}) collective-permute-start(bf16[512,256]{1,0:T(8,128)(2,1)S(1)} %collective-permute-done.10.refs_9_.refs_5_), channel_id=1, source_target_pairs={{0,7},{1,0},{2,1},{3,2},{4,3},{5,4},{6,5},{7,6},{8,15},{9,8},{10,9... | collective-permute-start | bytes 786440 | tf_op jit(solution)/shard_map/ppermute | solution.py:54
  27.5 8.1 %collective-permute-start.11 = (bf16[512,256]{1,0:T(8,128)(2,1)S(1)}, bf16[512,256]{1,0:T(8,128)(2,1)S(1)}, u32[]{:S(2)}, u32[]{:S(2)}) collective-permute-start(bf16[512,256]{1,0:T(8,128)(2,1)S(1)} %collective-permute-done.5.refs_7_.refs_3_), channel_id=1, source_target_pairs={{0,1},{1,2},{2,3},{3,4},{4,5},{5,6},{6,7},{7,0},{8,9},{9,10},{10,1... | collective-permute-start | bytes 786440 | tf_op jit(solution)/shard_map/ppermute | solution.py:50
  31.8 10.7 %collective-permute-start.6 = (bf16[512,256]{1,0:T(8,128)(2,1)S(1)}, bf16[512,256]{1,0:T(8,128)(2,1)S(1)}, u32[]{:S(2)}, u32[]{:S(2)}) collective-permute-start(bf16[512,256]{1,0:T(8,128)(2,1)S(1)} %collective-permute-done.4.refs_12_.refs_2_), channel_id=1, source_target_pairs={{0,1},{1,2},{2,3},{3,4},{4,5},{5,6},{6,7},{7,0},{8,9},{9,10},{10,1... | collective-permute-start | bytes 786440 | tf_op jit(solution)/shard_map/ppermute | solution.py:50
  34.6 8.4 %collective-permute-start.13 = (bf16[512,256]{1,0:T(8,128)(2,1)S(1)}, bf16[512,256]{1,0:T(8,128)(2,1)S(1)}, u32[]{:S(2)}, u32[]{:S(2)}) collective-permute-start(bf16[512,256]{1,0:T(8,128)(2,1)S(1)} %collective-permute-done.12.refs_11_.refs_1_), channel_id=1, source_target_pairs={{0,7},{1,0},{2,1},{3,2},{4,3},{5,4},{6,5},{7,6},{8,15},{9,8},{10,9... | collective-permute-start | bytes 786440 | tf_op jit(solution)/shard_map/ppermute | solution.py:54
  35.5 8.5 %collective-permute-start.14 = (bf16[512,256]{1,0:T(8,128)(2,1)S(1)}, bf16[512,256]{1,0:T(8,128)(2,1)S(1)}, u32[]{:S(2)}, u32[]{:S(2)}) collective-permute-start(bf16[512,256]{1,0:T(8,128)(2,1)S(1)} %collective-permute-done.11.refs_10_.refs_0_), channel_id=1, source_target_pairs={{0,8},{1,9},{2,10},{3,11},{4,12},{5,13},{6,14},{7,15},{8,0},{9,1},... | collective-permute-start | bytes 786440 | tf_op jit(solution)/shard_map/ppermute | solution.py:58
  48.3 8.5 %collective-permute-start.15 = (bf16[576,256]{1,0:T(8,128)(2,1)S(1)}, bf16[576,256]{1,0:T(8,128)(2,1)S(1)}, u32[]{:S(2)}, u32[]{:S(2)}) collective-permute-start(bf16[576,256]{1,0:T(8,128)(2,1)S(1)} %get-tuple-element.127), channel_id=1, source_target_pairs={{0,8},{1,9},{2,10},{3,11},{4,12},{5,13},{6,14},{7,15},{8,0},{9,1},... | collective-permute-start | bytes 884744 | tf_op jit(solution)/shard_map/ppermute | solution.py:58
  48.7 8.0 %collective-permute-start.16 = (bf16[576,256]{1,0:T(8,128)(2,1)S(1)}, bf16[576,256]{1,0:T(8,128)(2,1)S(1)}, u32[]{:S(2)}, u32[]{:S(2)}) collective-permute-start(bf16[576,256]{1,0:T(8,128)(2,1)S(1)} %get-tuple-element.128), channel_id=1, source_target_pairs={{0,7},{1,0},{2,1},{3,2},{4,3},{5,4},{6,5},{7,6},{8,15},{9,8},{10,9... | collective-permute-start | bytes 884744 | tf_op jit(solution)/shard_map/ppermute | solution.py:54
  48.7 8.2 %collective-permute-start.17 = (bf16[576,256]{1,0:T(8,128)(2,1)S(1)}, bf16[576,256]{1,0:T(8,128)(2,1)S(1)}, u32[]{:S(2)}, u32[]{:S(2)}) collective-permute-start(bf16[576,256]{1,0:T(8,128)(2,1)S(1)} %get-tuple-element.148), channel_id=1, source_target_pairs={{0,1},{1,2},{2,3},{3,4},{4,5},{5,6},{6,7},{7,0},{8,9},{9,10},{10,1... | collective-permute-start | bytes 884744 | tf_op jit(solution)/shard_map/ppermute | solution.py:50
  56.8 10.1 %collective-permute-start.18 = (bf16[576,256]{1,0:T(8,128)(2,1)S(1)}, bf16[576,256]{1,0:T(8,128)(2,1)S(1)}, u32[]{:S(2)}, u32[]{:S(2)}) collective-permute-start(bf16[576,256]{1,0:T(8,128)(2,1)S(1)} %add_convert_fusion.8), channel_id=1, source_target_pairs={{0,7},{1,0},{2,1},{3,2},{4,3},{5,4},{6,5},{7,6},{8,15},{9,8},{10,9... | collective-permute-start | bytes 884744 | tf_op jit(solution)/shard_map/ppermute | solution.py:54
  57.0 10.0 %collective-permute-start.19 = (bf16[576,256]{1,0:T(8,128)(2,1)S(1)}, bf16[576,256]{1,0:T(8,128)(2,1)S(1)}, u32[]{:S(2)}, u32[]{:S(2)}) collective-permute-start(bf16[576,256]{1,0:T(8,128)(2,1)S(1)} %add_convert_fusion.7), channel_id=1, source_target_pairs={{0,1},{1,2},{2,3},{3,4},{4,5},{5,6},{6,7},{7,0},{8,9},{9,10},{10,1... | collective-permute-start | bytes 884744 | tf_op jit(solution)/shard_map/ppermute | solution.py:50
  61.2 7.9 %collective-permute-start.21 = (bf16[576,256]{1,0:T(8,128)(2,1)S(1)}, bf16[576,256]{1,0:T(8,128)(2,1)S(1)}, u32[]{:S(2)}, u32[]{:S(2)}) collective-permute-start(bf16[576,256]{1,0:T(8,128)(2,1)S(1)} %get-tuple-element.159), channel_id=1, source_target_pairs={{0,1},{1,2},{2,3},{3,4},{4,5},{5,6},{6,7},{7,0},{8,9},{9,10},{10,1... | collective-permute-start | bytes 884744 | tf_op jit(solution)/shard_map/ppermute | solution.py:50
  61.4 16.6 %collective-permute-start.24 = (bf16[576,256]{1,0:T(8,128)(2,1)S(1)}, bf16[576,256]{1,0:T(8,128)(2,1)S(1)}, u32[]{:S(2)}, u32[]{:S(2)}) collective-permute-start(bf16[576,256]{1,0:T(8,128)(2,1)S(1)} %get-tuple-element.167), channel_id=1, source_target_pairs={{0,8},{1,9},{2,10},{3,11},{4,12},{5,13},{6,14},{7,15},{8,0},{9,1},... | collective-permute-start | bytes 884744 | tf_op jit(solution)/shard_map/ppermute | solution.py:58
  67.0 8.9 %collective-permute-start.22 = (bf16[576,256]{1,0:T(8,128)(2,1)S(1)}, bf16[576,256]{1,0:T(8,128)(2,1)S(1)}, u32[]{:S(2)}, u32[]{:S(2)}) collective-permute-start(bf16[576,256]{1,0:T(8,128)(2,1)S(1)} %add_convert_fusion.5), channel_id=1, source_target_pairs={{0,7},{1,0},{2,1},{3,2},{4,3},{5,4},{6,5},{7,6},{8,15},{9,8},{10,9... | collective-permute-start | bytes 884744 | tf_op jit(solution)/shard_map/ppermute | solution.py:54
  69.1 9.0 %collective-permute-start.23 = (bf16[576,256]{1,0:T(8,128)(2,1)S(1)}, bf16[576,256]{1,0:T(8,128)(2,1)S(1)}, u32[]{:S(2)}, u32[]{:S(2)}) collective-permute-start(bf16[576,256]{1,0:T(8,128)(2,1)S(1)} %add_convert_fusion.4), channel_id=1, source_target_pairs={{0,8},{1,9},{2,10},{3,11},{4,12},{5,13},{6,14},{7,15},{8,0},{9,1},... | collective-permute-start | bytes 884744 | tf_op jit(solution)/shard_map/ppermute | solution.py:58
  70.5 7.6 %collective-permute-start.25 = (bf16[576,256]{1,0:T(8,128)(2,1)S(1)}, bf16[576,256]{1,0:T(8,128)(2,1)S(1)}, u32[]{:S(2)}, u32[]{:S(2)}) collective-permute-start(bf16[576,256]{1,0:T(8,128)(2,1)S(1)} %add_convert_fusion.3), channel_id=1, source_target_pairs={{0,1},{1,2},{2,3},{3,4},{4,5},{5,6},{6,7},{7,0},{8,9},{9,10},{10,1... | collective-permute-start | bytes 884744 | tf_op jit(solution)/shard_map/ppermute | solution.py:50
  76.1 7.5 %collective-permute-start.27 = (bf16[576,256]{1,0:T(8,128)(2,1)S(1)}, bf16[576,256]{1,0:T(8,128)(2,1)S(1)}, u32[]{:S(2)}, u32[]{:S(2)}) collective-permute-start(bf16[576,256]{1,0:T(8,128)(2,1)S(1)} %get-tuple-element.176), channel_id=1, source_target_pairs={{0,8},{1,9},{2,10},{3,11},{4,12},{5,13},{6,14},{7,15},{8,0},{9,1},... | collective-permute-start | bytes 884744 | tf_op jit(solution)/shard_map/ppermute | solution.py:58
  83.4 8.9 %collective-permute-start.29 = (bf16[576,256]{1,0:T(8,128)(2,1)S(1)}, bf16[576,256]{1,0:T(8,128)(2,1)S(1)}, u32[]{:S(2)}, u32[]{:S(2)}) collective-permute-start(bf16[576,256]{1,0:T(8,128)(2,1)S(1)} %add_convert_fusion), channel_id=1, source_target_pairs={{0,7},{1,0},{2,1},{3,2},{4,3},{5,4},{6,5},{7,6},{8,15},{9,8},{10,9... | collective-permute-start | bytes 884744 | tf_op jit(solution)/shard_map/ppermute | solution.py:54
  92.9 8.8 %collective-permute-start.30 = (f32[32,1280]{1,0:T(8,128)S(1)}, f32[32,1280]{1,0:T(8,128)S(1)}, u32[]{:S(2)}, u32[]{:S(2)}) collective-permute-start(f32[32,1280]{1,0:T(8,128)S(1)} %get-tuple-element.196), channel_id=1, source_target_pairs={{0,16},{16,0},{32,48},{48,32},{64,80},{80,64},{96,112},{112,96},{1... | collective-permute-start | bytes 491528 | tf_op jit(solution)/shard_map/ppermute | solution.py:492
  (20 other events, 167.8 us)

commit v5 on v4

--- a/solution.py
+++ b/solution.py
@@ -14,13 +14,9 @@
 MERGE_ROWS = 512
 LANES = 128
 
-EARLY = (
-    (0, 0),
-    (0, -1), (0, 1), (1, 0),
-    (0, -2), (0, 2), (1, -1),
-    (0, -3), (0, 3), (1, 1),
-    (0, 4), (1, 2), (1, -2),
-)
+GATE_FIRST = ((0, 0), (0, -1), (0, 1), (1, 0), (0, -2), (1, 1), (0, 2))
+GATE_SECOND = ((0, -3), (1, -2), (1, 2), (0, 4), (1, -1), (0, 3))
+GATE_THIRD = ((1, -3), (1, 3))
 LATE = ((1, -3), (1, 3), (1, 4))
 REST_OUT = (
     (0, 4), (1, 2), (1, -2), (0, -3), (0, 3), (1, 1), (0, -2), (0, 2), (1, -1),
@@ -138,36 +134,40 @@
     out_ref[tokens:, :] = (down[:low] + down[low:]).astype(jnp.bfloat16)
 
 
-def gate_early_kernel(count, rank_ref, *refs):
-    blocks, merged_ref, total_ref = refs[:count], refs[count], refs[count + 1]
+def gate_part_kernel(offsets, rank_ref, *refs):
+    count = len(offsets)
+    blocks, merged_ref, before, total_ref = refs[:count], refs[count], refs[count + 1 : -1], refs[-1]
     rank, sign = rank_ref[0], rank_ref[1]
     height = blocks[0].shape[1]
-    for at, offset in enumerate(EARLY):
+    for at, offset in enumerate(offsets):
         rows = merged_ref[pl.ds(row_of(rank, offset, height, sign), height), :]
         part = dot(blocks[at][...], rows, 1, 0)
-        if at == 0:
+        if at:
+            total_ref[...] += part
+        elif before:
+            total_ref[...] = before[0][...] + part
+        else:
             total_ref[...] = part
-        else:
-            total_ref[...] += part
-
-
-def gate_early(rank, blocks, merged):
+
+
+def gate_part(offsets, rank, blocks, merged, before=()):
     tokens, height = blocks[0].shape
     wide = merged.shape[1]
     count = len(blocks)
     return pl.pallas_call(
-        functools.partial(gate_early_kernel, count),
-        in_specs=[SMEM] + [VMEM] * (count + 1),
+        functools.partial(gate_part_kernel, offsets),
+        in_specs=[SMEM] + [VMEM] * (count + 1 + len(before)),
         out_specs=VMEM,
         out_shape=jax.ShapeDtypeStruct((tokens, wide), jnp.float32),
+        input_output_aliases={count + 2: 0} if before else {},
         compiler_params=pltpu.CompilerParams(vmem_limit_bytes=6 * 2**20),
         cost_estimate=pl.CostEstimate(
             flops=2 * tokens * height * wide * count,
             bytes_accessed=count * height * (wide + tokens) * 2 + tokens * wide * 4,
             transcendentals=0,
         ),
-        name="gate_early",
-    )(rank, *blocks, merged)
+        name="gate_part",
+    )(rank, *blocks, merged, *before)
 
 
 def gate_late_kernel(
@@ -199,15 +199,14 @@
     norms = jnp.sqrt(square_ref[...] + EPSILON)
     scales = magnitude_ref[...] / norms
     tile = tokens
-    starts = [row_of(rank, offset, height, sign) for offset in LATE]
+    start = row_of(rank, LATE[-1], height, sign)
     magnitude_piece_ref[...] = jnp.zeros_like(magnitude_piece_ref)
 
     @pl.loop(0, tokens // tile)
     def _(step):
         here = pl.ds(pl.multiple_of(step * tile, tile), tile)
         total = total_ref[here, :]
-        for block, start in zip((late_a, late_b, late_c), starts):
-            total += dot(block[here, :], merged_ref[pl.ds(start, height), :], 1, 0)
+        total += dot(late_c[here, :], merged_ref[pl.ds(start, height), :], 1, 0)
         gate_pre = total[:, :width]
         latent = total[:, width : width + low]
         gate_out = gate_pre * scales
@@ -329,25 +328,27 @@
     )(rank, up_piece, magnitude_piece, *parts)
 
 
-def finish_kernel(rank_ref, mine_ref, other_ref, up_ref, down_ref):
+def finish_kernel(rank_ref, mine_ref, other_ref, up_ref, down_ref, magnitude_ref):
     half, width = mine_ref.shape[0], up_ref.shape[1]
-    first = rank_ref[2] == 0
-    for at in range(2):
-        here = slice(at * half, (at + 1) * half)
-        rows = jnp.where(first == (at == 0), mine_ref[...], other_ref[...])
-        up_ref[here, :] = rows[:, :width]
-        down_ref[here, :] = rows[:, width:]
+    core = rank_ref[2]
+    for ref, upper in ((mine_ref, core), (other_ref, 1 - core)):
+        here = pl.ds(pl.multiple_of(upper * half, half), half)
+        up_ref[here, :] = ref[:, :width]
+        down_ref[here, :] = ref[:, width : width + down_ref.shape[1]]
+    for row in range(width // LANES):
+        magnitude_ref[pl.ds(row * LANES, LANES)] = mine_ref[row, -LANES:]
 
 
 def finish(rank, mine, other, width):
-    half, wide = mine.shape
+    half, wide = other.shape
     return pl.pallas_call(
         finish_kernel,
         in_specs=[SMEM] + [VMEM] * 2,
-        out_specs=[VMEM] * 2,
+        out_specs=[VMEM] * 3,
         out_shape=[
             jax.ShapeDtypeStruct((2 * half, width), jnp.float32),
             jax.ShapeDtypeStruct((2 * half, wide - width), jnp.float32),
+            jax.ShapeDtypeStruct((width,), jnp.float32),
         ],
         compiler_params=pltpu.CompilerParams(vmem_limit_bytes=6 * 2**20),
         cost_estimate=pl.CostEstimate(flops=2**16, bytes_accessed=2**20, transcendentals=0),
@@ -429,15 +430,19 @@
     merged, square = arrive(up_ring, (0, -1), (0, -2), merged, square)
     arrive(across, (0, 1), (1, 1))
     arrive(down_ring, (0, 1), (0, 2))
-    arrive(up_ring, (0, -2), (0, -3))
+    total = gate_part(GATE_FIRST, rank, [got[offset] for offset in GATE_FIRST], merged)
+    (total,) = arrive(up_ring, (0, -2), (0, -3), total)
     arrive(across, (0, -2), (1, -2))
     arrive(down_ring, (1, 1), (1, 2), after=(0, -2))
     arrive(up_ring, (0, -3), (0, 4))
     arrive(across, (0, -1), (1, -1), after=(0, -3))
     arrive(down_ring, (0, 2), (0, 3), after=(0, -3))
-    total = gate_early(rank, [got[offset] for offset in EARLY], merged)
+    total = gate_part(
+        GATE_SECOND, rank, [got[offset] for offset in GATE_SECOND], merged, (total,)
+    )
     (total,) = arrive(up_ring, (1, -2), (1, -3), total, after=(0, -3))
     arrive(down_ring, (1, 2), (1, 3), after=(0, -3))
+    total = gate_part(GATE_THIRD, rank, [got[offset] for offset in GATE_THIRD], merged, (total,))
     arrive(across, (0, 4), (1, 4))
     *late, total = together(*[got[offset] for offset in LATE], total)
 
@@ -493,10 +498,8 @@
     pieces = unpack(sum_four(pack(pieces), "dp", (2, 4)))
     sent = lax.optimization_barrier(pack(pieces).astype(jnp.bfloat16))
     pieces = unpack(f32(sent) + f32(lax.ppermute(sent, "dp", xor_perm(8))))
-    mine = pieces[:, :-LANES]
-    other = lax.ppermute(mine, "dp", xor_perm(1))
-    lowrank_up_gradient, down_gradient = finish(rank, mine, other, width)
-    magnitude_gradient = pieces[: width // LANES, -LANES:].reshape(width)
+    other = lax.ppermute(pieces[:, :-LANES], "dp", xor_perm(1))
+    lowrank_up_gradient, down_gradient, magnitude_gradient = finish(rank, pieces, other, width)
     return (
         layer_input_gradient,
         up_output_gradient,

time: 122 us -> 120 us (0.984); the launches traced: 120 us -> 120 us
  Pallas kernels: 19.3 us -> 21.1 us
    ppermute x10, waiting for transfers between devices: 6.65 us -> 10 us  [up_ring(): return lax.ppermute(array, ('dp', 'tensor'), ring_perm(1))]
    pallas_call x1 -> x3, Pallas kernels: 4.23 us -> 6.3 us  [gate_part(): pl.pallas_call(functools.partial(gate_part_kernel, offsets), in_specs=[SM...]
    ppermute x10, waiting for transfers between devices: 2.07 us -> 0.03 us  [across(): return lax.ppermute(array, 'tensor', xor_perm(RING))]
    ppermute x10, waiting for transfers between devices: 17.8 us -> 15.9 us  [down_ring(): return lax.ppermute(array, ('dp', 'tensor'), ring_perm(-1))]
  transfers between devices with their start and end apart: 36 -> 36, of which waited for: 19 -> 15; matrix products, arithmetic and copies ran while one was open for 2% -> 1% of each run, Pallas kernels for 11% -> 13%
where the time goes in v5:
time: 120 us
  starting transfers between devices  57.8 us (48%)
  waiting for transfers between devices  33.1 us (28%)
  Pallas kernels  21.1 us (18%)
  local copies, waits for them, and re-layouts  5.09 us (4%)
  other arithmetic  1.83 us (2%)
    ppermute x10, starting transfers between devices, up_ring(): return lax.ppermute(array, ('dp', 'tensor'), ring_perm(1))  26.7 us
    ppermute x10, waiting for transfers between devices, down_ring(): return lax.ppermute(array, ('dp', 'tensor'), ring_perm(-1))  15.9 us
    ppermute x10, starting transfers between devices, across(): return lax.ppermute(array, 'tensor', xor_perm(RING))  11.5 us
    ppermute x10, waiting for transfers between devices, up_ring(): return lax.ppermute(array, ('dp', 'tensor'), ring_perm(1))  10 us
    ppermute x1, starting transfers between devices, per_device(): pieces = kept + lax.ppermute(sent, 'dp', xor_perm(1))  7.48 us
    pallas_call x3, Pallas kernels, gate_part(): pl.pallas_call(functools.partial(gate_part_kernel, offsets), in_specs=[SM...  6.3 us
    unnamed x16, local copies, waits for them, and re-layouts  5.05 us
    pallas_call x1, Pallas kernels, rest(): pl.pallas_call(functools.partial(rest_kernel, factor, count), in_specs=[S...  5.01 us
  transfers between devices with their start and end apart: 36, of which 15 were waited for; matrix products, arithmetic and copies ran while one was open for 1% of the time, Pallas kernels for 13%

profile of v5, /device:TPU:1, one launch (start us, length us, event | category | flops | bytes accessed | tf_op | source)
XLA Modules:
  0.0 119.9 jit_solution(16193823815275840141)
XLA Ops:
  4.4 3.9 %collective-permute-start = (bf16[512,256]{1,0:T(8,128)(2,1)}, bf16[512,256]{1,0:T(8,128)(2,1)S(1)}, u32[]{:S(2)}, u32[]{:S(2)}) collective-permute-start(bf16[512,256]{1,0:T(8,128)(2,1)} %refs_12_), channel_id=1, source_target_pairs={{0,1},{1,2},{2,3},{3,4},{4,5},{5,6},{6,7},{7,0},{8,9},{9,10},{10,1... | collective-permute-start | bytes 786440 | tf_op jit(solution)/shard_map/ppermute | solution.py:46
  8.4 3.1 %copy-done = bf16[4096,896]{1,0:T(8,128)(2,1)S(1)} copy-done((bf16[4096,896]{1,0:T(8,128)(2,1)S(1)}, bf16[4096,896]{1,0:T(8,128)(2,1)}, u32[]{:S(2)}) %copy-start) | copy-done | bytes 7340056
  13.9 2.7 %collective-permute-start.3 = (bf16[512,256]{1,0:T(8,128)(2,1)S(1)}, bf16[512,256]{1,0:T(8,128)(2,1)S(1)}, u32[]{:S(2)}, u32[]{:S(2)}) collective-permute-start(bf16[512,256]{1,0:T(8,128)(2,1)S(1)} %collective-permute-done.refs_1_.refs_9_), channel_id=1, source_target_pairs={{0,1},{1,2},{2,3},{3,4},{4,5},{5,6},{6,7},{7,0},{8,9},{9,10},{10,1... | collective-permute-start | bytes 786440 | tf_op jit(solution)/shard_map/ppermute | solution.py:46
  16.9 3.5 %merge_tail.1 = (bf16[4096,1024]{1,0:T(8,128)(2,1)S(1)}, f32[1,896]{1,0:T(1,128)S(1)}) custom-call(bf16[4096,896]{1,0:T(8,128)(2,1)S(1)} %copy-done, bf16[64,4096]{1,0:T(8,128)(2,1)S(1)} %bitcast.6, bf16[64,896]{1,0:T(8,128)(2,1)S(1)} %copy-done.4, bf16[4096,1024]{1,0:T(8,128)(2,1)S(1)} %get-tuple-element.110.head_ref, ...), custom_call_target="tpu_custom_call", output_to_operand_aliasing={{0}: (3, {})} | custom-call | flops 411041792 | bytes 12845056 | tf_op jit(solution)/shard_map/merge_tail/pallas_call | solution.py:106
  20.4 2.8 %collective-permute-start.5 = (bf16[512,256]{1,0:T(8,128)(2,1)S(1)}, bf16[512,256]{1,0:T(8,128)(2,1)S(1)}, u32[]{:S(2)}, u32[]{:S(2)}) collective-permute-start(bf16[512,256]{1,0:T(8,128)(2,1)S(1)} %collective-permute-done.3.refs_4_.refs_6_), channel_id=1, source_target_pairs={{0,1},{1,2},{2,3},{3,4},{4,5},{5,6},{6,7},{7,0},{8,9},{9,10},{10,1... | collective-permute-start | bytes 786440 | tf_op jit(solution)/shard_map/ppermute | solution.py:46
  25.5 2.6 %gate_part.3.refs_7_ = f32[512,1024]{1,0:T(8,128)S(1)} custom-call(s32[3]{0:T(128)S(1)} %pad_add_fusion.rank_ref, bf16[512,256]{1,0:T(8,128)(2,1)S(1)} %copy-done.2, bf16[512,256]{1,0:T(8,128)(2,1)S(1)} %collective-permute-done.refs_1_.refs_9_, bf16[512,256]{1,0:T(8,128)(2,1)S(1)} %collective-permute-done.1.refs_2_.refs_10_, ...), custom_call_target="tpu_custom_call" | custom-call | flops 1879048192 | bytes 7602176 | tf_op jit(solution)/shard_map/gate_part/pallas_call | solution.py:157
  28.1 2.5 %collective-permute-start.10 = (bf16[512,256]{1,0:T(8,128)(2,1)S(1)}, bf16[512,256]{1,0:T(8,128)(2,1)S(1)}, u32[]{:S(2)}, u32[]{:S(2)}) collective-permute-start(bf16[512,256]{1,0:T(8,128)(2,1)S(1)} %collective-permute-done.5.refs_0_.refs_3_), channel_id=1, source_target_pairs={{0,1},{1,2},{2,3},{3,4},{4,5},{5,6},{6,7},{7,0},{8,9},{9,10},{10,1... | collective-permute-start | bytes 786440 | tf_op jit(solution)/shard_map/ppermute | solution.py:46
  31.8 2.7 %collective-permute-start.8 = (bf16[512,256]{1,0:T(8,128)(2,1)S(1)}, bf16[512,256]{1,0:T(8,128)(2,1)S(1)}, u32[]{:S(2)}, u32[]{:S(2)}) collective-permute-start(bf16[512,256]{1,0:T(8,128)(2,1)S(1)} %collective-permute-done.4.refs_1_.refs_2_), channel_id=1, source_target_pairs={{0,1},{1,2},{2,3},{3,4},{4,5},{5,6},{6,7},{7,0},{8,9},{9,10},{10,1... | collective-permute-start | bytes 786440 | tf_op jit(solution)/shard_map/ppermute | solution.py:46
  40.7 3.2 %collective-permute-done.13.refs_1_.late_b = bf16[512,256]{1,0:T(8,128)(2,1)S(1)} collective-permute-done((bf16[512,256]{1,0:T(8,128)(2,1)S(1)}, bf16[512,256]{1,0:T(8,128)(2,1)S(1)}, u32[]{:S(2)}, u32[]{:S(2)}) %collective-permute-start.13) | collective-permute-done | bytes 262176 | tf_op jit(solution)/shard_map/ppermute | solution.py:50
  45.2 3.9 %gate_late.1 = (bf16[512,896]{1,0:T(8,128)(2,1)}, bf16[512,896]{1,0:T(8,128)(2,1)S(1)}, bf16[128,512]{1,0:T(8,128)(2,1)S(1)}, bf16[512,128]{1,0:T(8,128)(2,1)S(1...) custom-call(s32[3]{0:T(128)S(1)} %pad_add_fusion.rank_ref, ...), custom_call_target="tpu_custom_call" | custom-call | flops 1879048192 | bytes 8388608 | tf_op jit(solution)/shard_map/gate_late/pallas_call | solution.py:241
  49.1 2.7 %collective-permute-start.17 = (bf16[576,256]{1,0:T(8,128)(2,1)S(1)}, bf16[576,256]{1,0:T(8,128)(2,1)S(1)}, u32[]{:S(2)}, u32[]{:S(2)}) collective-permute-start(bf16[576,256]{1,0:T(8,128)(2,1)S(1)} %get-tuple-element.153), channel_id=1, source_target_pairs={{0,1},{1,2},{2,3},{3,4},{4,5},{5,6},{6,7},{7,0},{8,9},{9,10},{10,1... | collective-permute-start | bytes 884744 | tf_op jit(solution)/shard_map/ppermute | solution.py:46
  51.7 5.0 %rest.1 = (f32[64,896]{1,0:T(8,128)S(1)}, bf16[576,256]{1,0:T(8,128)(2,1)S(1)}, bf16[576,256]{1,0:T(8,128)(2,1)S(1)}, bf16[576,256]{1,0:T(8,128)(2,1)S(1)}, bf16...) custom-call(s32[3]{0:T(128)S(1)} %pad_add_fusion.rank_ref, ...), custom_call_target="tpu_custom_call" | custom-call | flops 3053453312 | bytes 10223616 | tf_op jit(solution)/shard_map/rest/pallas_call | solution.py:283
  57.0 2.7 %collective-permute-start.19 = (bf16[576,256]{1,0:T(8,128)(2,1)S(1)}, bf16[576,256]{1,0:T(8,128)(2,1)S(1)}, u32[]{:S(2)}, u32[]{:S(2)}) collective-permute-start(bf16[576,256]{1,0:T(8,128)(2,1)S(1)} %add_convert_fusion.7), channel_id=1, source_target_pairs={{0,1},{1,2},{2,3},{3,4},{4,5},{5,6},{6,7},{7,0},{8,9},{9,10},{10,1... | collective-permute-start | bytes 884744 | tf_op jit(solution)/shard_map/ppermute | solution.py:46
  61.8 4.6 %collective-permute-done.18 = bf16[576,256]{1,0:T(8,128)(2,1)S(1)} collective-permute-done((bf16[576,256]{1,0:T(8,128)(2,1)S(1)}, bf16[576,256]{1,0:T(8,128)(2,1)S(1)}, u32[]{:S(2)}, u32[]{:S(2)}) %collective-permute-start.18) | collective-permute-done | bytes 294944 | tf_op jit(solution)/shard_map/ppermute | solution.py:50
  70.3 3.3 %collective-permute-start.25 = (bf16[576,256]{1,0:T(8,128)(2,1)S(1)}, bf16[576,256]{1,0:T(8,128)(2,1)S(1)}, u32[]{:S(2)}, u32[]{:S(2)}) collective-permute-start(bf16[576,256]{1,0:T(8,128)(2,1)S(1)} %add_convert_fusion.3), channel_id=1, source_target_pairs={{0,1},{1,2},{2,3},{3,4},{4,5},{5,6},{6,7},{7,0},{8,9},{9,10},{10,1... | collective-permute-start | bytes 884744 | tf_op jit(solution)/shard_map/ppermute | solution.py:46
  73.5 2.6 %collective-permute-done.22 = bf16[576,256]{1,0:T(8,128)(2,1)S(1)} collective-permute-done((bf16[576,256]{1,0:T(8,128)(2,1)S(1)}, bf16[576,256]{1,0:T(8,128)(2,1)S(1)}, u32[]{:S(2)}, u32[]{:S(2)}) %collective-permute-start.22) | collective-permute-done | bytes 294944 | tf_op jit(solution)/shard_map/ppermute | solution.py:50
  79.9 3.5 %collective-permute-start.28 = (bf16[576,256]{1,0:T(8,128)(2,1)S(1)}, bf16[576,256]{1,0:T(8,128)(2,1)S(1)}, u32[]{:S(2)}, u32[]{:S(2)}) collective-permute-start(bf16[576,256]{1,0:T(8,128)(2,1)S(1)} %add_convert_fusion.1), channel_id=1, source_target_pairs={{0,1},{1,2},{2,3},{3,4},{4,5},{5,6},{6,7},{7,0},{8,9},{9,10},{10,1... | collective-permute-start | bytes 884744 | tf_op jit(solution)/shard_map/ppermute | solution.py:46
  83.6 4.6 %collective-permute-done.28.refs_2_ = bf16[576,256]{1,0:T(8,128)(2,1)S(1)} collective-permute-done((bf16[576,256]{1,0:T(8,128)(2,1)S(1)}, bf16[576,256]{1,0:T(8,128)(2,1)S(1)}, u32[]{:S(2)}, u32[]{:S(2)}) %collective-permute-start.28) | collective-permute-done | bytes 294944 | tf_op jit(solution)/shard_map/ppermute | solution.py:46
  88.2 4.0 %collective-permute-done.29.refs_3_ = bf16[576,256]{1,0:T(8,128)(2,1)S(1)} collective-permute-done((bf16[576,256]{1,0:T(8,128)(2,1)S(1)}, bf16[576,256]{1,0:T(8,128)(2,1)S(1)}, u32[]{:S(2)}, u32[]{:S(2)}) %collective-permute-start.29) | collective-permute-done | bytes 294944 | tf_op jit(solution)/shard_map/ppermute | solution.py:50
  92.7 7.5 %collective-permute-start.30 = (f32[32,1280]{1,0:T(8,128)S(1)}, f32[32,1280]{1,0:T(8,128)S(1)}, u32[]{:S(2)}, u32[]{:S(2)}) collective-permute-start(f32[32,1280]{1,0:T(8,128)S(1)} %get-tuple-element.201), channel_id=1, source_target_pairs={{0,16},{16,0},{32,48},{48,32},{64,80},{80,64},{96,112},{112,96},{1... | collective-permute-start | bytes 491528 | tf_op jit(solution)/shard_map/ppermute | solution.py:497
  101.3 2.8 %collective-permute-start.33 = (bf16[32,1280]{1,0:T(8,128)(2,1)S(1)}, bf16[32,1280]{1,0:T(8,128)(2,1)S(1)}, u32[]{:S(2)}, u32[]{:S(2)}) collective-permute-start(bf16[32,1280]{1,0:T(8,128)(2,1)S(1)} %maximum_maximum_fusion), channel_id=1, source_target_pairs={{0,96},{16,112},{32,64},{48,80},{64,32},{80,48},{96,0},{112,16},{1... | collective-permute-start | bytes 245768 | tf_op jit(solution)/shard_map/ppermute | solution.py:373
  104.8 2.5 %collective-permute-done.33 = bf16[32,1280]{1,0:T(8,128)(2,1)S(1)} collective-permute-done((bf16[32,1280]{1,0:T(8,128)(2,1)S(1)}, bf16[32,1280]{1,0:T(8,128)(2,1)S(1)}, u32[]{:S(2)}, u32[]{:S(2)}) %collective-permute-start.33) | collective-permute-done | bytes 81952 | tf_op jit(solution)/shard_map/ppermute | solution.py:373
  109.0 3.0 %collective-permute-start.34 = (bf16[32,1280]{1,0:T(8,128)(2,1)S(1)}, bf16[32,1280]{1,0:T(8,128)(2,1)S(1)}, u32[]{:S(2)}, u32[]{:S(2)}) collective-permute-start(bf16[32,1280]{1,0:T(8,128)(2,1)S(1)} %maximum_maximum_fusion.1), channel_id=1, source_target_pairs={{0,128},{16,144},{32,160},{48,176},{64,192},{80,208},{96,224},{112... | collective-permute-start | bytes 245768 | tf_op jit(solution)/shard_map/ppermute | solution.py:500
  114.0 3.7 %collective-permute-start.35 = (f32[32,1152]{1,0:T(8,128)S(1)}, f32[32,1152]{1,0:T(8,128)S(1)}, u32[]{:S(2)}, u32[]{:S(2)}) collective-permute-start(f32[32,1152]{1,0:T(8,128)S(1)} %slice.62), channel_id=1, source_target_pairs={{0,16},{16,0},{32,48},{48,32},{64,80},{80,64},{96,112},{112,96},{1... | collective-permute-start | bytes 442376 | tf_op jit(solution)/shard_map/ppermute | solution.py:501
  (97 shorter events, 35.9 us)
Async XLA Ops:
  0.7 13.2 %collective-permute-start.2 = (bf16[512,256]{1,0:T(8,128)(2,1)}, bf16[512,256]{1,0:T(8,128)(2,1)S(1)}, u32[]{:S(2)}, u32[]{:S(2)}) collective-permute-start(bf16[512,256]{1,0:T(8,128)(2,1)} %refs_12_), channel_id=1, source_target_pairs={{0,8},{1,9},{2,10},{3,11},{4,12},{5,13},{6,14},{7,15},{8,0},{9,1},... | collective-permute-start | bytes 786440 | tf_op jit(solution)/shard_map/ppermute | solution.py:54
  2.8 11.1 %collective-permute-start.1 = (bf16[512,256]{1,0:T(8,128)(2,1)}, bf16[512,256]{1,0:T(8,128)(2,1)S(1)}, u32[]{:S(2)}, u32[]{:S(2)}) collective-permute-start(bf16[512,256]{1,0:T(8,128)(2,1)} %refs_12_), channel_id=1, source_target_pairs={{0,7},{1,0},{2,1},{3,2},{4,3},{5,4},{6,5},{7,6},{8,15},{9,8},{10,9... | collective-permute-start | bytes 786440 | tf_op jit(solution)/shard_map/ppermute | solution.py:50
  4.4 9.5 %collective-permute-start = (bf16[512,256]{1,0:T(8,128)(2,1)}, bf16[512,256]{1,0:T(8,128)(2,1)S(1)}, u32[]{:S(2)}, u32[]{:S(2)}) collective-permute-start(bf16[512,256]{1,0:T(8,128)(2,1)} %refs_12_), channel_id=1, source_target_pairs={{0,1},{1,2},{2,3},{3,4},{4,5},{5,6},{6,7},{7,0},{8,9},{9,10},{10,1... | collective-permute-start | bytes 786440 | tf_op jit(solution)/shard_map/ppermute | solution.py:46
  16.6 7.8 %collective-permute-start.6 = (bf16[512,256]{1,0:T(8,128)(2,1)S(1)}, bf16[512,256]{1,0:T(8,128)(2,1)S(1)}, u32[]{:S(2)}, u32[]{:S(2)}) collective-permute-start(bf16[512,256]{1,0:T(8,128)(2,1)S(1)} %collective-permute-done.1.refs_2_.refs_10_), channel_id=1, source_target_pairs={{0,8},{1,9},{2,10},{3,11},{4,12},{5,13},{6,14},{7,15},{8,0},{9,1},... | collective-permute-start | bytes 786440 | tf_op jit(solution)/shard_map/ppermute | solution.py:54
  16.9 8.6 %collective-permute-start.7 = (bf16[512,256]{1,0:T(8,128)(2,1)S(1)}, bf16[512,256]{1,0:T(8,128)(2,1)S(1)}, u32[]{:S(2)}, u32[]{:S(2)}) collective-permute-start(bf16[512,256]{1,0:T(8,128)(2,1)S(1)} %collective-permute-done.1.refs_2_.refs_10_), channel_id=1, source_target_pairs={{0,7},{1,0},{2,1},{3,2},{4,3},{5,4},{6,5},{7,6},{8,15},{9,8},{10,9... | collective-permute-start | bytes 786440 | tf_op jit(solution)/shard_map/ppermute | solution.py:50
  20.4 7.7 %collective-permute-start.5 = (bf16[512,256]{1,0:T(8,128)(2,1)S(1)}, bf16[512,256]{1,0:T(8,128)(2,1)S(1)}, u32[]{:S(2)}, u32[]{:S(2)}) collective-permute-start(bf16[512,256]{1,0:T(8,128)(2,1)S(1)} %collective-permute-done.3.refs_4_.refs_6_), channel_id=1, source_target_pairs={{0,1},{1,2},{2,3},{3,4},{4,5},{5,6},{6,7},{7,0},{8,9},{9,10},{10,1... | collective-permute-start | bytes 786440 | tf_op jit(solution)/shard_map/ppermute | solution.py:46
  23.2 8.6 %collective-permute-start.4 = (bf16[512,256]{1,0:T(8,128)(2,1)S(1)}, bf16[512,256]{1,0:T(8,128)(2,1)S(1)}, u32[]{:S(2)}, u32[]{:S(2)}) collective-permute-start(bf16[512,256]{1,0:T(8,128)(2,1)S(1)} %collective-permute-done.3.refs_4_.refs_6_), channel_id=1, source_target_pairs={{0,8},{1,9},{2,10},{3,11},{4,12},{5,13},{6,14},{7,15},{8,0},{9,1},... | collective-permute-start | bytes 786440 | tf_op jit(solution)/shard_map/ppermute | solution.py:54
  24.4 7.4 %collective-permute-start.9 = (bf16[512,256]{1,0:T(8,128)(2,1)S(1)}, bf16[512,256]{1,0:T(8,128)(2,1)S(1)}, u32[]{:S(2)}, u32[]{:S(2)}) collective-permute-start(bf16[512,256]{1,0:T(8,128)(2,1)S(1)} %collective-permute-done.6.refs_5_), channel_id=1, source_target_pairs={{0,7},{1,0},{2,1},{3,2},{4,3},{5,4},{6,5},{7,6},{8,15},{9,8},{10,9... | collective-permute-start | bytes 786440 | tf_op jit(solution)/shard_map/ppermute | solution.py:50
  28.1 7.8 %collective-permute-start.10 = (bf16[512,256]{1,0:T(8,128)(2,1)S(1)}, bf16[512,256]{1,0:T(8,128)(2,1)S(1)}, u32[]{:S(2)}, u32[]{:S(2)}) collective-permute-start(bf16[512,256]{1,0:T(8,128)(2,1)S(1)} %collective-permute-done.5.refs_0_.refs_3_), channel_id=1, source_target_pairs={{0,1},{1,2},{2,3},{3,4},{4,5},{5,6},{6,7},{7,0},{8,9},{9,10},{10,1... | collective-permute-start | bytes 786440 | tf_op jit(solution)/shard_map/ppermute | solution.py:46
  31.8 8.8 %collective-permute-start.8 = (bf16[512,256]{1,0:T(8,128)(2,1)S(1)}, bf16[512,256]{1,0:T(8,128)(2,1)S(1)}, u32[]{:S(2)}, u32[]{:S(2)}) collective-permute-start(bf16[512,256]{1,0:T(8,128)(2,1)S(1)} %collective-permute-done.4.refs_1_.refs_2_), channel_id=1, source_target_pairs={{0,1},{1,2},{2,3},{3,4},{4,5},{5,6},{6,7},{7,0},{8,9},{9,10},{10,1... | collective-permute-start | bytes 786440 | tf_op jit(solution)/shard_map/ppermute | solution.py:46
  34.5 9.3 %collective-permute-start.13 = (bf16[512,256]{1,0:T(8,128)(2,1)S(1)}, bf16[512,256]{1,0:T(8,128)(2,1)S(1)}, u32[]{:S(2)}, u32[]{:S(2)}) collective-permute-start(bf16[512,256]{1,0:T(8,128)(2,1)S(1)} %collective-permute-done.9.refs_2_.refs_1_), channel_id=1, source_target_pairs={{0,7},{1,0},{2,1},{3,2},{4,3},{5,4},{6,5},{7,6},{8,15},{9,8},{10,9... | collective-permute-start | bytes 786440 | tf_op jit(solution)/shard_map/ppermute | solution.py:50
  36.0 9.2 %collective-permute-start.14 = (bf16[512,256]{1,0:T(8,128)(2,1)S(1)}, bf16[512,256]{1,0:T(8,128)(2,1)S(1)}, u32[]{:S(2)}, u32[]{:S(2)}) collective-permute-start(bf16[512,256]{1,0:T(8,128)(2,1)S(1)} %collective-permute-done.10.refs_3_.refs_0_), channel_id=1, source_target_pairs={{0,8},{1,9},{2,10},{3,11},{4,12},{5,13},{6,14},{7,15},{8,0},{9,1},... | collective-permute-start | bytes 786440 | tf_op jit(solution)/shard_map/ppermute | solution.py:54
  49.1 7.7 %collective-permute-start.15 = (bf16[576,256]{1,0:T(8,128)(2,1)S(1)}, bf16[576,256]{1,0:T(8,128)(2,1)S(1)}, u32[]{:S(2)}, u32[]{:S(2)}) collective-permute-start(bf16[576,256]{1,0:T(8,128)(2,1)S(1)} %get-tuple-element.132), channel_id=1, source_target_pairs={{0,8},{1,9},{2,10},{3,11},{4,12},{5,13},{6,14},{7,15},{8,0},{9,1},... | collective-permute-start | bytes 884744 | tf_op jit(solution)/shard_map/ppermute | solution.py:54
  49.1 7.7 %collective-permute-start.16 = (bf16[576,256]{1,0:T(8,128)(2,1)S(1)}, bf16[576,256]{1,0:T(8,128)(2,1)S(1)}, u32[]{:S(2)}, u32[]{:S(2)}) collective-permute-start(bf16[576,256]{1,0:T(8,128)(2,1)S(1)} %get-tuple-element.133), channel_id=1, source_target_pairs={{0,7},{1,0},{2,1},{3,2},{4,3},{5,4},{6,5},{7,6},{8,15},{9,8},{10,9... | collective-permute-start | bytes 884744 | tf_op jit(solution)/shard_map/ppermute | solution.py:50
  49.1 7.9 %collective-permute-start.17 = (bf16[576,256]{1,0:T(8,128)(2,1)S(1)}, bf16[576,256]{1,0:T(8,128)(2,1)S(1)}, u32[]{:S(2)}, u32[]{:S(2)}) collective-permute-start(bf16[576,256]{1,0:T(8,128)(2,1)S(1)} %get-tuple-element.153), channel_id=1, source_target_pairs={{0,1},{1,2},{2,3},{3,4},{4,5},{5,6},{6,7},{7,0},{8,9},{9,10},{10,1... | collective-permute-start | bytes 884744 | tf_op jit(solution)/shard_map/ppermute | solution.py:46
  56.9 9.5 %collective-permute-start.18 = (bf16[576,256]{1,0:T(8,128)(2,1)S(1)}, bf16[576,256]{1,0:T(8,128)(2,1)S(1)}, u32[]{:S(2)}, u32[]{:S(2)}) collective-permute-start(bf16[576,256]{1,0:T(8,128)(2,1)S(1)} %add_convert_fusion.8), channel_id=1, source_target_pairs={{0,7},{1,0},{2,1},{3,2},{4,3},{5,4},{6,5},{7,6},{8,15},{9,8},{10,9... | collective-permute-start | bytes 884744 | tf_op jit(solution)/shard_map/ppermute | solution.py:50
  57.0 9.5 %collective-permute-start.19 = (bf16[576,256]{1,0:T(8,128)(2,1)S(1)}, bf16[576,256]{1,0:T(8,128)(2,1)S(1)}, u32[]{:S(2)}, u32[]{:S(2)}) collective-permute-start(bf16[576,256]{1,0:T(8,128)(2,1)S(1)} %add_convert_fusion.7), channel_id=1, source_target_pairs={{0,1},{1,2},{2,3},{3,4},{4,5},{5,6},{6,7},{7,0},{8,9},{9,10},{10,1... | collective-permute-start | bytes 884744 | tf_op jit(solution)/shard_map/ppermute | solution.py:46
  61.6 16.2 %collective-permute-start.24 = (bf16[576,256]{1,0:T(8,128)(2,1)S(1)}, bf16[576,256]{1,0:T(8,128)(2,1)S(1)}, u32[]{:S(2)}, u32[]{:S(2)}) collective-permute-start(bf16[576,256]{1,0:T(8,128)(2,1)S(1)} %get-tuple-element.172), channel_id=1, source_target_pairs={{0,8},{1,9},{2,10},{3,11},{4,12},{5,13},{6,14},{7,15},{8,0},{9,1},... | collective-permute-start | bytes 884744 | tf_op jit(solution)/shard_map/ppermute | solution.py:54
  66.4 9.7 %collective-permute-start.22 = (bf16[576,256]{1,0:T(8,128)(2,1)S(1)}, bf16[576,256]{1,0:T(8,128)(2,1)S(1)}, u32[]{:S(2)}, u32[]{:S(2)}) collective-permute-start(bf16[576,256]{1,0:T(8,128)(2,1)S(1)} %add_convert_fusion.5), channel_id=1, source_target_pairs={{0,7},{1,0},{2,1},{3,2},{4,3},{5,4},{6,5},{7,6},{8,15},{9,8},{10,9... | collective-permute-start | bytes 884744 | tf_op jit(solution)/shard_map/ppermute | solution.py:50
  68.7 9.2 %collective-permute-start.23 = (bf16[576,256]{1,0:T(8,128)(2,1)S(1)}, bf16[576,256]{1,0:T(8,128)(2,1)S(1)}, u32[]{:S(2)}, u32[]{:S(2)}) collective-permute-start(bf16[576,256]{1,0:T(8,128)(2,1)S(1)} %add_convert_fusion.4), channel_id=1, source_target_pairs={{0,8},{1,9},{2,10},{3,11},{4,12},{5,13},{6,14},{7,15},{8,0},{9,1},... | collective-permute-start | bytes 884744 | tf_op jit(solution)/shard_map/ppermute | solution.py:54
  70.3 9.5 %collective-permute-start.25 = (bf16[576,256]{1,0:T(8,128)(2,1)S(1)}, bf16[576,256]{1,0:T(8,128)(2,1)S(1)}, u32[]{:S(2)}, u32[]{:S(2)}) collective-permute-start(bf16[576,256]{1,0:T(8,128)(2,1)S(1)} %add_convert_fusion.3), channel_id=1, source_target_pairs={{0,1},{1,2},{2,3},{3,4},{4,5},{5,6},{6,7},{7,0},{8,9},{9,10},{10,1... | collective-permute-start | bytes 884744 | tf_op jit(solution)/shard_map/ppermute | solution.py:46
  79.9 8.3 %collective-permute-start.28 = (bf16[576,256]{1,0:T(8,128)(2,1)S(1)}, bf16[576,256]{1,0:T(8,128)(2,1)S(1)}, u32[]{:S(2)}, u32[]{:S(2)}) collective-permute-start(bf16[576,256]{1,0:T(8,128)(2,1)S(1)} %add_convert_fusion.1), channel_id=1, source_target_pairs={{0,1},{1,2},{2,3},{3,4},{4,5},{5,6},{6,7},{7,0},{8,9},{9,10},{10,1... | collective-permute-start | bytes 884744 | tf_op jit(solution)/shard_map/ppermute | solution.py:46
  83.5 8.6 %collective-permute-start.29 = (bf16[576,256]{1,0:T(8,128)(2,1)S(1)}, bf16[576,256]{1,0:T(8,128)(2,1)S(1)}, u32[]{:S(2)}, u32[]{:S(2)}) collective-permute-start(bf16[576,256]{1,0:T(8,128)(2,1)S(1)} %add_convert_fusion), channel_id=1, source_target_pairs={{0,7},{1,0},{2,1},{3,2},{4,3},{5,4},{6,5},{7,6},{8,15},{9,8},{10,9... | collective-permute-start | bytes 884744 | tf_op jit(solution)/shard_map/ppermute | solution.py:50
  92.7 8.5 %collective-permute-start.30 = (f32[32,1280]{1,0:T(8,128)S(1)}, f32[32,1280]{1,0:T(8,128)S(1)}, u32[]{:S(2)}, u32[]{:S(2)}) collective-permute-start(f32[32,1280]{1,0:T(8,128)S(1)} %get-tuple-element.201), channel_id=1, source_target_pairs={{0,16},{16,0},{32,48},{48,32},{64,80},{80,64},{96,112},{112,96},{1... | collective-permute-start | bytes 491528 | tf_op jit(solution)/shard_map/ppermute | solution.py:497
  (20 other events, 119.7 us)

commit v6 on v5

--- a/solution.py
+++ b/solution.py
@@ -58,6 +58,10 @@
     return lax.dot_general(
         left, right, (((left_dim,), (right_dim,)), ((), ())), preferred_element_type=jnp.float32
     )
+
+
+def place():
+    return lax.axis_index("tensor"), 1 - 2 * (lax.axis_index("dp") % 2)
 
 
 def row_of(rank, offset, height, sign):
@@ -134,10 +138,10 @@
     out_ref[tokens:, :] = (down[:low] + down[low:]).astype(jnp.bfloat16)
 
 
-def gate_part_kernel(offsets, rank_ref, *refs):
+def gate_part_kernel(offsets, *refs):
     count = len(offsets)
     blocks, merged_ref, before, total_ref = refs[:count], refs[count], refs[count + 1 : -1], refs[-1]
-    rank, sign = rank_ref[0], rank_ref[1]
+    rank, sign = place()
     height = blocks[0].shape[1]
     for at, offset in enumerate(offsets):
         rows = merged_ref[pl.ds(row_of(rank, offset, height, sign), height), :]
@@ -156,10 +160,10 @@
     count = len(blocks)
     return pl.pallas_call(
         functools.partial(gate_part_kernel, offsets),
-        in_specs=[SMEM] + [VMEM] * (count + 1 + len(before)),
+        in_specs=[VMEM] * (count + 1 + len(before)),
         out_specs=VMEM,
         out_shape=jax.ShapeDtypeStruct((tokens, wide), jnp.float32),
-        input_output_aliases={count + 2: 0} if before else {},
+        input_output_aliases={count + 1: 0} if before else {},
         compiler_params=pltpu.CompilerParams(vmem_limit_bytes=6 * 2**20),
         cost_estimate=pl.CostEstimate(
             flops=2 * tokens * height * wide * count,
@@ -167,12 +171,11 @@
             transcendentals=0,
         ),
         name="gate_part",
-    )(rank, *blocks, merged, *before)
+    )(*blocks, merged, *before)
 
 
 def gate_late_kernel(
     factor,
-    rank_ref,
     late_a,
     late_b,
     late_c,
@@ -192,7 +195,7 @@
     first_b,
     first_c,
 ):
-    rank, sign = rank_ref[0], rank_ref[1]
+    rank, sign = place()
     tokens, height = late_a.shape
     width = hidden_ref.shape[1]
     low = lowrank_up_ref.shape[0]
@@ -240,7 +243,7 @@
     block = jax.ShapeDtypeStruct((tokens + low, height), jnp.bfloat16)
     return pl.pallas_call(
         functools.partial(gate_late_kernel, factor),
-        in_specs=[SMEM] + [VMEM] * 10,
+        in_specs=[VMEM] * 10,
         out_specs=[VMEM] * 8,
         out_shape=[
             jax.ShapeDtypeStruct((tokens, width), jnp.bfloat16),
@@ -259,12 +262,12 @@
             transcendentals=2 * tokens * width,
         ),
         name="gate_late",
-    )(rank, *late, merged, total, square, magnitude, hidden, saved, lowrank_up)
-
-
-def rest_kernel(factor, count, rank_ref, merged_ref, scaled_ref, latent_ref, both_ref, *refs):
+    )(*late, merged, total, square, magnitude, hidden, saved, lowrank_up)
+
+
+def rest_kernel(factor, count, merged_ref, scaled_ref, latent_ref, both_ref, *refs):
     blocks, up_piece_ref, outs = refs[:count], refs[count], refs[count + 1 :]
-    rank, sign = rank_ref[0], rank_ref[1]
+    rank, sign = place()
     height = outs[0].shape[1]
     low, width = up_piece_ref.shape
     for offset, block, out in zip(REST_OUT, blocks, outs):
@@ -282,7 +285,7 @@
     low = latent.shape[1] // 2
     return pl.pallas_call(
         functools.partial(rest_kernel, factor, count),
-        in_specs=[SMEM] + [VMEM] * (4 + count),
+        in_specs=[VMEM] * (4 + count),
         out_specs=[VMEM] * (count + 1),
         out_shape=[jax.ShapeDtypeStruct((low, width), jnp.float32)]
         + [jax.ShapeDtypeStruct((tokens + low, height), jnp.bfloat16)] * count,
@@ -293,14 +296,14 @@
             transcendentals=0,
         ),
         name="rest",
-    )(rank, merged, scaled, latent, both, *blocks)
-
-
-def payload_kernel(factor, tokens, rank_ref, up_ref, magnitude_ref, *refs):
+    )(merged, scaled, latent, both, *blocks)
+
+
+def payload_kernel(factor, tokens, up_ref, magnitude_ref, *refs):
     parts, (kept_ref, sent_ref) = refs[:4], refs[4:]
     low, width = up_ref.shape
     half = low // 2
-    core = rank_ref[2]
+    core = lax.axis_index("dp") % 2
     for out, upper in ((kept_ref, core), (sent_ref, 1 - core)):
         first = upper == 0
         here = pl.ds(pl.multiple_of(tokens + upper * half, half), half)
@@ -319,18 +322,18 @@
     out = jax.ShapeDtypeStruct((low // 2, width + parts[0].shape[1] + LANES), jnp.float32)
     return pl.pallas_call(
         functools.partial(payload_kernel, factor, tokens),
-        in_specs=[SMEM] + [VMEM] * 6,
+        in_specs=[VMEM] * 6,
         out_specs=[VMEM] * 2,
         out_shape=[out] * 2,
         compiler_params=pltpu.CompilerParams(vmem_limit_bytes=6 * 2**20),
         cost_estimate=pl.CostEstimate(flops=2**20, bytes_accessed=2**20, transcendentals=0),
         name="payload",
-    )(rank, up_piece, magnitude_piece, *parts)
-
-
-def finish_kernel(rank_ref, mine_ref, other_ref, up_ref, down_ref, magnitude_ref):
+    )(up_piece, magnitude_piece, *parts)
+
+
+def finish_kernel(mine_ref, other_ref, up_ref, down_ref, magnitude_ref):
     half, width = mine_ref.shape[0], up_ref.shape[1]
-    core = rank_ref[2]
+    core = lax.axis_index("dp") % 2
     for ref, upper in ((mine_ref, core), (other_ref, 1 - core)):
         here = pl.ds(pl.multiple_of(upper * half, half), half)
         up_ref[here, :] = ref[:, :width]
@@ -343,7 +346,7 @@
     half, wide = other.shape
     return pl.pallas_call(
         finish_kernel,
-        in_specs=[SMEM] + [VMEM] * 2,
+        in_specs=[VMEM] * 2,
         out_specs=[VMEM] * 3,
         out_shape=[
             jax.ShapeDtypeStruct((2 * half, width), jnp.float32),
@@ -353,7 +356,7 @@
         compiler_params=pltpu.CompilerParams(vmem_limit_bytes=6 * 2**20),
         cost_estimate=pl.CostEstimate(flops=2**16, bytes_accessed=2**20, transcendentals=0),
         name="finish",
-    )(rank, mine, other)
+    )(mine, other)
 
 
 def f32(array):

time: 120 us -> 119 us (level)
  waiting for transfers between devices: 33.1 us -> 37.4 us
  Pallas kernels: 21.1 us -> 17.2 us
  starting transfers between devices: 57.8 us -> 56 us
    ppermute x10, waiting for transfers between devices: 15.9 us -> 26.9 us  [down_ring(): return lax.ppermute(array, ('dp', 'tensor'), ring_perm(-1))]
    ppermute x10, waiting for transfers between devices: 10 us -> 3.35 us  [up_ring(): return lax.ppermute(array, ('dp', 'tensor'), ring_perm(1))]
    pallas_call x6, Pallas kernels: 16.5 us -> 13.2 us  [the longest x3 4.64 us: gate_part(): pl.pallas_call(functools.partial(gate_part_kernel, offsets), in_specs=[VM...]
    ppermute x10, starting transfers between devices: 26.7 us -> 24.5 us  [up_ring(): return lax.ppermute(array, ('dp', 'tensor'), ring_perm(1))]
  transfers between devices with their start and end apart: 36 -> 36, of which waited for: 15 -> 15; matrix products, arithmetic and copies ran while one was open for 1% -> 1% of each run, Pallas kernels for 13% -> 11%
where the time goes in v6:
time: 119 us; the launch traced here: 118 us
  starting transfers between devices  56 us (47%)
  waiting for transfers between devices  37.4 us (31%)
  Pallas kernels  17.2 us (14%)
  local copies, waits for them, and re-layouts  5.09 us (4%)
  other arithmetic  1.78 us (1%)
    ppermute x10, waiting for transfers between devices, down_ring(): return lax.ppermute(array, ('dp', 'tensor'), ring_perm(-1))  26.9 us
    ppermute x10, starting transfers between devices, up_ring(): return lax.ppermute(array, ('dp', 'tensor'), ring_perm(1))  24.5 us
    ppermute x10, starting transfers between devices, across(): return lax.ppermute(array, 'tensor', xor_perm(RING))  11.2 us
    ppermute x1, starting transfers between devices, per_device(): pieces = kept + lax.ppermute(sent, 'dp', xor_perm(1))  8 us
    unnamed x16, local copies, waits for them, and re-layouts  5.05 us
    pallas_call x3, Pallas kernels, gate_part(): pl.pallas_call(functools.partial(gate_part_kernel, offsets), in_specs=[VM...  4.64 us
    pallas_call x1, Pallas kernels, rest(): pl.pallas_call(functools.partial(rest_kernel, factor, count), in_specs=[V...  4.43 us
    ppermute x3, waiting for transfers between devices, sum_four(): lax.ppermute(sent, axis, xor_perm(at))  4.12 us
  transfers between devices with their start and end apart: 36, of which 15 were waited for; matrix products, arithmetic and copies ran while one was open for 1% of the time, Pallas kernels for 11%

profile of v6, /device:TPU:1, one launch (start us, length us, event | category | flops | bytes accessed | tf_op | source)
XLA Modules:
  0.0 118.5 jit_solution(16225584234043402201)
XLA Ops:
  0.6 2.1 %collective-permute-start.2 = (bf16[512,256]{1,0:T(8,128)(2,1)}, bf16[512,256]{1,0:T(8,128)(2,1)S(1)}, u32[]{:S(2)}, u32[]{:S(2)}) collective-permute-start(bf16[512,256]{1,0:T(8,128)(2,1)} %refs_12_), channel_id=1, source_target_pairs={{0,8},{1,9},{2,10},{3,11},{4,12},{5,13},{6,14},{7,15},{8,0},{9,1},... | collective-permute-start | bytes 786440 | tf_op jit(solution)/shard_map/ppermute | solution.py:54
  4.4 3.9 %collective-permute-start = (bf16[512,256]{1,0:T(8,128)(2,1)}, bf16[512,256]{1,0:T(8,128)(2,1)S(1)}, u32[]{:S(2)}, u32[]{:S(2)}) collective-permute-start(bf16[512,256]{1,0:T(8,128)(2,1)} %refs_12_), channel_id=1, source_target_pairs={{0,1},{1,2},{2,3},{3,4},{4,5},{5,6},{6,7},{7,0},{8,9},{9,10},{10,1... | collective-permute-start | bytes 786440 | tf_op jit(solution)/shard_map/ppermute | solution.py:46
  8.3 3.1 %copy-done = bf16[4096,896]{1,0:T(8,128)(2,1)S(1)} copy-done((bf16[4096,896]{1,0:T(8,128)(2,1)S(1)}, bf16[4096,896]{1,0:T(8,128)(2,1)}, u32[]{:S(2)}) %copy-start) | copy-done | bytes 7340056
  13.9 2.7 %collective-permute-start.3 = (bf16[512,256]{1,0:T(8,128)(2,1)S(1)}, bf16[512,256]{1,0:T(8,128)(2,1)S(1)}, u32[]{:S(2)}, u32[]{:S(2)}) collective-permute-start(bf16[512,256]{1,0:T(8,128)(2,1)S(1)} %collective-permute-done.refs_1_.refs_9_), channel_id=1, source_target_pairs={{0,1},{1,2},{2,3},{3,4},{4,5},{5,6},{6,7},{7,0},{8,9},{9,10},{10,1... | collective-permute-start | bytes 786440 | tf_op jit(solution)/shard_map/ppermute | solution.py:46
  16.9 3.5 %merge_tail.1 = (bf16[4096,1024]{1,0:T(8,128)(2,1)S(1)}, f32[1,896]{1,0:T(1,128)S(1)}) custom-call(bf16[4096,896]{1,0:T(8,128)(2,1)S(1)} %copy-done, bf16[64,4096]{1,0:T(8,128)(2,1)S(1)} %bitcast.3, bf16[64,896]{1,0:T(8,128)(2,1)S(1)} %copy-done.3, bf16[4096,1024]{1,0:T(8,128)(2,1)S(1)} %get-tuple-element.106.head_ref, ...), custom_call_target="tpu_custom_call", output_to_operand_aliasing={{0}: (3, {})} | custom-call | flops 411041792 | bytes 12845056 | tf_op jit(solution)/shard_map/merge_tail/pallas_call | solution.py:110
  20.4 2.8 %collective-permute-start.5 = (bf16[512,256]{1,0:T(8,128)(2,1)S(1)}, bf16[512,256]{1,0:T(8,128)(2,1)S(1)}, u32[]{:S(2)}, u32[]{:S(2)}) collective-permute-start(bf16[512,256]{1,0:T(8,128)(2,1)S(1)} %collective-permute-done.3.refs_4_.refs_6_), channel_id=1, source_target_pairs={{0,1},{1,2},{2,3},{3,4},{4,5},{5,6},{6,7},{7,0},{8,9},{9,10},{10,1... | collective-permute-start | bytes 786440 | tf_op jit(solution)/shard_map/ppermute | solution.py:46
  27.5 3.0 %collective-permute-start.10 = (bf16[512,256]{1,0:T(8,128)(2,1)S(1)}, bf16[512,256]{1,0:T(8,128)(2,1)S(1)}, u32[]{:S(2)}, u32[]{:S(2)}) collective-permute-start(bf16[512,256]{1,0:T(8,128)(2,1)S(1)} %collective-permute-done.5.refs_0_.refs_3_), channel_id=1, source_target_pairs={{0,1},{1,2},{2,3},{3,4},{4,5},{5,6},{6,7},{7,0},{8,9},{9,10},{10,1... | collective-permute-start | bytes 786440 | tf_op jit(solution)/shard_map/ppermute | solution.py:46
  31.8 2.7 %collective-permute-start.8 = (bf16[512,256]{1,0:T(8,128)(2,1)S(1)}, bf16[512,256]{1,0:T(8,128)(2,1)S(1)}, u32[]{:S(2)}, u32[]{:S(2)}) collective-permute-start(bf16[512,256]{1,0:T(8,128)(2,1)S(1)} %collective-permute-done.4.refs_1_.refs_2_), channel_id=1, source_target_pairs={{0,1},{1,2},{2,3},{3,4},{4,5},{5,6},{6,7},{7,0},{8,9},{9,10},{10,1... | collective-permute-start | bytes 786440 | tf_op jit(solution)/shard_map/ppermute | solution.py:46
  35.5 2.2 %collective-permute-start.14 = (bf16[512,256]{1,0:T(8,128)(2,1)S(1)}, bf16[512,256]{1,0:T(8,128)(2,1)S(1)}, u32[]{:S(2)}, u32[]{:S(2)}) collective-permute-start(bf16[512,256]{1,0:T(8,128)(2,1)S(1)} %collective-permute-done.10.refs_3_.refs_0_), channel_id=1, source_target_pairs={{0,8},{1,9},{2,10},{3,11},{4,12},{5,13},{6,14},{7,15},{8,0},{9,1},... | collective-permute-start | bytes 786440 | tf_op jit(solution)/shard_map/ppermute | solution.py:54
  40.1 3.7 %collective-permute-done.13.refs_1_.late_b = bf16[512,256]{1,0:T(8,128)(2,1)S(1)} collective-permute-done((bf16[512,256]{1,0:T(8,128)(2,1)S(1)}, bf16[512,256]{1,0:T(8,128)(2,1)S(1)}, u32[]{:S(2)}, u32[]{:S(2)}) %collective-permute-start.13) | collective-permute-done | bytes 262176 | tf_op jit(solution)/shard_map/ppermute | solution.py:50
  44.6 3.4 %gate_late.1 = (bf16[512,896]{1,0:T(8,128)(2,1)}, bf16[512,896]{1,0:T(8,128)(2,1)S(1)}, bf16[128,512]{1,0:T(8,128)(2,1)S(1)}, bf16[512,128]{1,0:T(8,128)(2,1)S(1...) custom-call(bf16[512,256]{1,0:T(8,128)(2,1)S(1)} %collective-permute, ...), custom_call_target="tpu_custom_call" | custom-call | flops 1879048192 | bytes 8388608 | tf_op jit(solution)/shard_map/gate_late/pallas_call | solution.py:244
  48.0 2.8 %collective-permute-start.17 = (bf16[576,256]{1,0:T(8,128)(2,1)S(1)}, bf16[576,256]{1,0:T(8,128)(2,1)S(1)}, u32[]{:S(2)}, u32[]{:S(2)}) collective-permute-start(bf16[576,256]{1,0:T(8,128)(2,1)S(1)} %get-tuple-element.149), channel_id=1, source_target_pairs={{0,1},{1,2},{2,3},{3,4},{4,5},{5,6},{6,7},{7,0},{8,9},{9,10},{10,1... | collective-permute-start | bytes 884744 | tf_op jit(solution)/shard_map/ppermute | solution.py:46
  50.8 4.4 %rest.1 = (f32[64,896]{1,0:T(8,128)S(1)}, bf16[576,256]{1,0:T(8,128)(2,1)S(1)}, bf16[576,256]{1,0:T(8,128)(2,1)S(1)}, bf16[576,256]{1,0:T(8,128)(2,1)S(1)}, bf16...) custom-call(bf16[4096,1024]{1,0:T(8,128)(2,1)S(1)} %get-tuple-elemen, ...), custom_call_target="tpu_custom_call" | custom-call | flops 3053453312 | bytes 10223616 | tf_op jit(solution)/shard_map/rest/pallas_call | solution.py:286
  55.5 2.7 %collective-permute-start.19 = (bf16[576,256]{1,0:T(8,128)(2,1)S(1)}, bf16[576,256]{1,0:T(8,128)(2,1)S(1)}, u32[]{:S(2)}, u32[]{:S(2)}) collective-permute-start(bf16[576,256]{1,0:T(8,128)(2,1)S(1)} %add_convert_fusion.7), channel_id=1, source_target_pairs={{0,1},{1,2},{2,3},{3,4},{4,5},{5,6},{6,7},{7,0},{8,9},{9,10},{10,1... | collective-permute-start | bytes 884744 | tf_op jit(solution)/shard_map/ppermute | solution.py:46
  60.3 5.2 %collective-permute-done.18 = bf16[576,256]{1,0:T(8,128)(2,1)S(1)} collective-permute-done((bf16[576,256]{1,0:T(8,128)(2,1)S(1)}, bf16[576,256]{1,0:T(8,128)(2,1)S(1)}, u32[]{:S(2)}, u32[]{:S(2)}) %collective-permute-start.18) | collective-permute-done | bytes 294944 | tf_op jit(solution)/shard_map/ppermute | solution.py:50
  69.7 5.4 %collective-permute-done.22 = bf16[576,256]{1,0:T(8,128)(2,1)S(1)} collective-permute-done((bf16[576,256]{1,0:T(8,128)(2,1)S(1)}, bf16[576,256]{1,0:T(8,128)(2,1)S(1)}, u32[]{:S(2)}, u32[]{:S(2)}) %collective-permute-start.22) | collective-permute-done | bytes 294944 | tf_op jit(solution)/shard_map/ppermute | solution.py:50
  76.5 2.7 %collective-permute-start.28 = (bf16[576,256]{1,0:T(8,128)(2,1)S(1)}, bf16[576,256]{1,0:T(8,128)(2,1)S(1)}, u32[]{:S(2)}, u32[]{:S(2)}) collective-permute-start(bf16[576,256]{1,0:T(8,128)(2,1)S(1)} %add_convert_fusion.1), channel_id=1, source_target_pairs={{0,1},{1,2},{2,3},{3,4},{4,5},{5,6},{6,7},{7,0},{8,9},{9,10},{10,1... | collective-permute-start | bytes 884744 | tf_op jit(solution)/shard_map/ppermute | solution.py:46
  79.1 2.9 %collective-permute-done.26 = bf16[576,256]{1,0:T(8,128)(2,1)S(1)} collective-permute-done((bf16[576,256]{1,0:T(8,128)(2,1)S(1)}, bf16[576,256]{1,0:T(8,128)(2,1)S(1)}, u32[]{:S(2)}, u32[]{:S(2)}) %collective-permute-start.26) | collective-permute-done | bytes 294944 | tf_op jit(solution)/shard_map/ppermute | solution.py:50
  83.1 8.1 %collective-permute-done.29.refs_3_ = bf16[576,256]{1,0:T(8,128)(2,1)S(1)} collective-permute-done((bf16[576,256]{1,0:T(8,128)(2,1)S(1)}, bf16[576,256]{1,0:T(8,128)(2,1)S(1)}, u32[]{:S(2)}, u32[]{:S(2)}) %collective-permute-start.29) | collective-permute-done | bytes 294944 | tf_op jit(solution)/shard_map/ppermute | solution.py:50
  91.3 8.0 %collective-permute-start.30 = (f32[32,1280]{1,0:T(8,128)S(1)}, f32[32,1280]{1,0:T(8,128)S(1)}, u32[]{:S(2)}, u32[]{:S(2)}) collective-permute-start(f32[32,1280]{1,0:T(8,128)S(1)} %get-tuple-element.197), channel_id=1, source_target_pairs={{0,16},{16,0},{32,48},{48,32},{64,80},{80,64},{96,112},{112,96},{1... | collective-permute-start | bytes 491528 | tf_op jit(solution)/shard_map/ppermute | solution.py:500
  100.4 2.8 %collective-permute-start.33 = (bf16[32,1280]{1,0:T(8,128)(2,1)S(1)}, bf16[32,1280]{1,0:T(8,128)(2,1)S(1)}, u32[]{:S(2)}, u32[]{:S(2)}) collective-permute-start(bf16[32,1280]{1,0:T(8,128)(2,1)S(1)} %maximum_maximum_fusion), channel_id=1, source_target_pairs={{0,96},{16,112},{32,64},{48,80},{64,32},{80,48},{96,0},{112,16},{1... | collective-permute-start | bytes 245768 | tf_op jit(solution)/shard_map/ppermute | solution.py:376
  103.9 2.5 %collective-permute-done.33 = bf16[32,1280]{1,0:T(8,128)(2,1)S(1)} collective-permute-done((bf16[32,1280]{1,0:T(8,128)(2,1)S(1)}, bf16[32,1280]{1,0:T(8,128)(2,1)S(1)}, u32[]{:S(2)}, u32[]{:S(2)}) %collective-permute-start.33) | collective-permute-done | bytes 81952 | tf_op jit(solution)/shard_map/ppermute | solution.py:376
  108.1 3.3 %collective-permute-start.34 = (bf16[32,1280]{1,0:T(8,128)(2,1)S(1)}, bf16[32,1280]{1,0:T(8,128)(2,1)S(1)}, u32[]{:S(2)}, u32[]{:S(2)}) collective-permute-start(bf16[32,1280]{1,0:T(8,128)(2,1)S(1)} %maximum_maximum_fusion.1), channel_id=1, source_target_pairs={{0,128},{16,144},{32,160},{48,176},{64,192},{80,208},{96,224},{112... | collective-permute-start | bytes 245768 | tf_op jit(solution)/shard_map/ppermute | solution.py:503
  113.3 3.4 %collective-permute-start.35 = (f32[32,1152]{1,0:T(8,128)S(1)}, f32[32,1152]{1,0:T(8,128)S(1)}, u32[]{:S(2)}, u32[]{:S(2)}) collective-permute-start(f32[32,1152]{1,0:T(8,128)S(1)} %slice.62), channel_id=1, source_target_pairs={{0,16},{16,0},{32,48},{48,32},{64,80},{80,64},{96,112},{112,96},{1... | collective-permute-start | bytes 442376 | tf_op jit(solution)/shard_map/ppermute | solution.py:504
  (96 shorter events, 30.1 us)
Async XLA Ops:
  0.6 13.2 %collective-permute-start.2 = (bf16[512,256]{1,0:T(8,128)(2,1)}, bf16[512,256]{1,0:T(8,128)(2,1)S(1)}, u32[]{:S(2)}, u32[]{:S(2)}) collective-permute-start(bf16[512,256]{1,0:T(8,128)(2,1)} %refs_12_), channel_id=1, source_target_pairs={{0,8},{1,9},{2,10},{3,11},{4,12},{5,13},{6,14},{7,15},{8,0},{9,1},... | collective-permute-start | bytes 786440 | tf_op jit(solution)/shard_map/ppermute | solution.py:54
  2.8 11.1 %collective-permute-start.1 = (bf16[512,256]{1,0:T(8,128)(2,1)}, bf16[512,256]{1,0:T(8,128)(2,1)S(1)}, u32[]{:S(2)}, u32[]{:S(2)}) collective-permute-start(bf16[512,256]{1,0:T(8,128)(2,1)} %refs_12_), channel_id=1, source_target_pairs={{0,7},{1,0},{2,1},{3,2},{4,3},{5,4},{6,5},{7,6},{8,15},{9,8},{10,9... | collective-permute-start | bytes 786440 | tf_op jit(solution)/shard_map/ppermute | solution.py:50
  4.4 9.5 %collective-permute-start = (bf16[512,256]{1,0:T(8,128)(2,1)}, bf16[512,256]{1,0:T(8,128)(2,1)S(1)}, u32[]{:S(2)}, u32[]{:S(2)}) collective-permute-start(bf16[512,256]{1,0:T(8,128)(2,1)} %refs_12_), channel_id=1, source_target_pairs={{0,1},{1,2},{2,3},{3,4},{4,5},{5,6},{6,7},{7,0},{8,9},{9,10},{10,1... | collective-permute-start | bytes 786440 | tf_op jit(solution)/shard_map/ppermute | solution.py:46
  16.6 7.8 %collective-permute-start.6 = (bf16[512,256]{1,0:T(8,128)(2,1)S(1)}, bf16[512,256]{1,0:T(8,128)(2,1)S(1)}, u32[]{:S(2)}, u32[]{:S(2)}) collective-permute-start(bf16[512,256]{1,0:T(8,128)(2,1)S(1)} %collective-permute-done.1.refs_2_.refs_10_), channel_id=1, source_target_pairs={{0,8},{1,9},{2,10},{3,11},{4,12},{5,13},{6,14},{7,15},{8,0},{9,1},... | collective-permute-start | bytes 786440 | tf_op jit(solution)/shard_map/ppermute | solution.py:54
  16.9 8.6 %collective-permute-start.7 = (bf16[512,256]{1,0:T(8,128)(2,1)S(1)}, bf16[512,256]{1,0:T(8,128)(2,1)S(1)}, u32[]{:S(2)}, u32[]{:S(2)}) collective-permute-start(bf16[512,256]{1,0:T(8,128)(2,1)S(1)} %collective-permute-done.1.refs_2_.refs_10_), channel_id=1, source_target_pairs={{0,7},{1,0},{2,1},{3,2},{4,3},{5,4},{6,5},{7,6},{8,15},{9,8},{10,9... | collective-permute-start | bytes 786440 | tf_op jit(solution)/shard_map/ppermute | solution.py:50
  23.2 8.6 %collective-permute-start.4 = (bf16[512,256]{1,0:T(8,128)(2,1)S(1)}, bf16[512,256]{1,0:T(8,128)(2,1)S(1)}, u32[]{:S(2)}, u32[]{:S(2)}) collective-permute-start(bf16[512,256]{1,0:T(8,128)(2,1)S(1)} %collective-permute-done.3.refs_4_.refs_6_), channel_id=1, source_target_pairs={{0,8},{1,9},{2,10},{3,11},{4,12},{5,13},{6,14},{7,15},{8,0},{9,1},... | collective-permute-start | bytes 786440 | tf_op jit(solution)/shard_map/ppermute | solution.py:54
  24.4 7.4 %collective-permute-start.9 = (bf16[512,256]{1,0:T(8,128)(2,1)S(1)}, bf16[512,256]{1,0:T(8,128)(2,1)S(1)}, u32[]{:S(2)}, u32[]{:S(2)}) collective-permute-start(bf16[512,256]{1,0:T(8,128)(2,1)S(1)} %collective-permute-done.6.refs_5_), channel_id=1, source_target_pairs={{0,7},{1,0},{2,1},{3,2},{4,3},{5,4},{6,5},{7,6},{8,15},{9,8},{10,9... | collective-permute-start | bytes 786440 | tf_op jit(solution)/shard_map/ppermute | solution.py:50
  27.5 8.0 %collective-permute-start.10 = (bf16[512,256]{1,0:T(8,128)(2,1)S(1)}, bf16[512,256]{1,0:T(8,128)(2,1)S(1)}, u32[]{:S(2)}, u32[]{:S(2)}) collective-permute-start(bf16[512,256]{1,0:T(8,128)(2,1)S(1)} %collective-permute-done.5.refs_0_.refs_3_), channel_id=1, source_target_pairs={{0,1},{1,2},{2,3},{3,4},{4,5},{5,6},{6,7},{7,0},{8,9},{9,10},{10,1... | collective-permute-start | bytes 786440 | tf_op jit(solution)/shard_map/ppermute | solution.py:46
  31.8 8.3 %collective-permute-start.8 = (bf16[512,256]{1,0:T(8,128)(2,1)S(1)}, bf16[512,256]{1,0:T(8,128)(2,1)S(1)}, u32[]{:S(2)}, u32[]{:S(2)}) collective-permute-start(bf16[512,256]{1,0:T(8,128)(2,1)S(1)} %collective-permute-done.4.refs_1_.refs_2_), channel_id=1, source_target_pairs={{0,1},{1,2},{2,3},{3,4},{4,5},{5,6},{6,7},{7,0},{8,9},{9,10},{10,1... | collective-permute-start | bytes 786440 | tf_op jit(solution)/shard_map/ppermute | solution.py:46
  34.5 9.3 %collective-permute-start.13 = (bf16[512,256]{1,0:T(8,128)(2,1)S(1)}, bf16[512,256]{1,0:T(8,128)(2,1)S(1)}, u32[]{:S(2)}, u32[]{:S(2)}) collective-permute-start(bf16[512,256]{1,0:T(8,128)(2,1)S(1)} %collective-permute-done.9.refs_2_.refs_1_), channel_id=1, source_target_pairs={{0,7},{1,0},{2,1},{3,2},{4,3},{5,4},{6,5},{7,6},{8,15},{9,8},{10,9... | collective-permute-start | bytes 786440 | tf_op jit(solution)/shard_map/ppermute | solution.py:50
  35.5 9.0 %collective-permute-start.14 = (bf16[512,256]{1,0:T(8,128)(2,1)S(1)}, bf16[512,256]{1,0:T(8,128)(2,1)S(1)}, u32[]{:S(2)}, u32[]{:S(2)}) collective-permute-start(bf16[512,256]{1,0:T(8,128)(2,1)S(1)} %collective-permute-done.10.refs_3_.refs_0_), channel_id=1, source_target_pairs={{0,8},{1,9},{2,10},{3,11},{4,12},{5,13},{6,14},{7,15},{8,0},{9,1},... | collective-permute-start | bytes 786440 | tf_op jit(solution)/shard_map/ppermute | solution.py:54
  48.0 7.3 %collective-permute-start.15 = (bf16[576,256]{1,0:T(8,128)(2,1)S(1)}, bf16[576,256]{1,0:T(8,128)(2,1)S(1)}, u32[]{:S(2)}, u32[]{:S(2)}) collective-permute-start(bf16[576,256]{1,0:T(8,128)(2,1)S(1)} %get-tuple-element.128), channel_id=1, source_target_pairs={{0,8},{1,9},{2,10},{3,11},{4,12},{5,13},{6,14},{7,15},{8,0},{9,1},... | collective-permute-start | bytes 884744 | tf_op jit(solution)/shard_map/ppermute | solution.py:54
  48.0 7.3 %collective-permute-start.16 = (bf16[576,256]{1,0:T(8,128)(2,1)S(1)}, bf16[576,256]{1,0:T(8,128)(2,1)S(1)}, u32[]{:S(2)}, u32[]{:S(2)}) collective-permute-start(bf16[576,256]{1,0:T(8,128)(2,1)S(1)} %get-tuple-element.129), channel_id=1, source_target_pairs={{0,7},{1,0},{2,1},{3,2},{4,3},{5,4},{6,5},{7,6},{8,15},{9,8},{10,9... | collective-permute-start | bytes 884744 | tf_op jit(solution)/shard_map/ppermute | solution.py:50
  48.0 7.4 %collective-permute-start.17 = (bf16[576,256]{1,0:T(8,128)(2,1)S(1)}, bf16[576,256]{1,0:T(8,128)(2,1)S(1)}, u32[]{:S(2)}, u32[]{:S(2)}) collective-permute-start(bf16[576,256]{1,0:T(8,128)(2,1)S(1)} %get-tuple-element.149), channel_id=1, source_target_pairs={{0,1},{1,2},{2,3},{3,4},{4,5},{5,6},{6,7},{7,0},{8,9},{9,10},{10,1... | collective-permute-start | bytes 884744 | tf_op jit(solution)/shard_map/ppermute | solution.py:46
  55.3 10.2 %collective-permute-start.18 = (bf16[576,256]{1,0:T(8,128)(2,1)S(1)}, bf16[576,256]{1,0:T(8,128)(2,1)S(1)}, u32[]{:S(2)}, u32[]{:S(2)}) collective-permute-start(bf16[576,256]{1,0:T(8,128)(2,1)S(1)} %add_convert_fusion.8), channel_id=1, source_target_pairs={{0,7},{1,0},{2,1},{3,2},{4,3},{5,4},{6,5},{7,6},{8,15},{9,8},{10,9... | collective-permute-start | bytes 884744 | tf_op jit(solution)/shard_map/ppermute | solution.py:50
  55.5 10.2 %collective-permute-start.19 = (bf16[576,256]{1,0:T(8,128)(2,1)S(1)}, bf16[576,256]{1,0:T(8,128)(2,1)S(1)}, u32[]{:S(2)}, u32[]{:S(2)}) collective-permute-start(bf16[576,256]{1,0:T(8,128)(2,1)S(1)} %add_convert_fusion.7), channel_id=1, source_target_pairs={{0,1},{1,2},{2,3},{3,4},{4,5},{5,6},{6,7},{7,0},{8,9},{9,10},{10,1... | collective-permute-start | bytes 884744 | tf_op jit(solution)/shard_map/ppermute | solution.py:46
  58.3 7.5 %collective-permute-start.20 = (bf16[576,256]{1,0:T(8,128)(2,1)S(1)}, bf16[576,256]{1,0:T(8,128)(2,1)S(1)}, u32[]{:S(2)}, u32[]{:S(2)}) collective-permute-start(bf16[576,256]{1,0:T(8,128)(2,1)S(1)} %add_convert_fusion.6), channel_id=1, source_target_pairs={{0,8},{1,9},{2,10},{3,11},{4,12},{5,13},{6,14},{7,15},{8,0},{9,1},... | collective-permute-start | bytes 884744 | tf_op jit(solution)/shard_map/ppermute | solution.py:54
  59.7 7.5 %collective-permute-start.21 = (bf16[576,256]{1,0:T(8,128)(2,1)S(1)}, bf16[576,256]{1,0:T(8,128)(2,1)S(1)}, u32[]{:S(2)}, u32[]{:S(2)}) collective-permute-start(bf16[576,256]{1,0:T(8,128)(2,1)S(1)} %get-tuple-element.160), channel_id=1, source_target_pairs={{0,1},{1,2},{2,3},{3,4},{4,5},{5,6},{6,7},{7,0},{8,9},{9,10},{10,1... | collective-permute-start | bytes 884744 | tf_op jit(solution)/shard_map/ppermute | solution.py:46
  59.7 16.6 %collective-permute-start.24 = (bf16[576,256]{1,0:T(8,128)(2,1)S(1)}, bf16[576,256]{1,0:T(8,128)(2,1)S(1)}, u32[]{:S(2)}, u32[]{:S(2)}) collective-permute-start(bf16[576,256]{1,0:T(8,128)(2,1)S(1)} %get-tuple-element.168), channel_id=1, source_target_pairs={{0,8},{1,9},{2,10},{3,11},{4,12},{5,13},{6,14},{7,15},{8,0},{9,1},... | collective-permute-start | bytes 884744 | tf_op jit(solution)/shard_map/ppermute | solution.py:54
  65.6 9.5 %collective-permute-start.22 = (bf16[576,256]{1,0:T(8,128)(2,1)S(1)}, bf16[576,256]{1,0:T(8,128)(2,1)S(1)}, u32[]{:S(2)}, u32[]{:S(2)}) collective-permute-start(bf16[576,256]{1,0:T(8,128)(2,1)S(1)} %add_convert_fusion.5), channel_id=1, source_target_pairs={{0,7},{1,0},{2,1},{3,2},{4,3},{5,4},{6,5},{7,6},{8,15},{9,8},{10,9... | collective-permute-start | bytes 884744 | tf_op jit(solution)/shard_map/ppermute | solution.py:50
  67.2 9.2 %collective-permute-start.23 = (bf16[576,256]{1,0:T(8,128)(2,1)S(1)}, bf16[576,256]{1,0:T(8,128)(2,1)S(1)}, u32[]{:S(2)}, u32[]{:S(2)}) collective-permute-start(bf16[576,256]{1,0:T(8,128)(2,1)S(1)} %add_convert_fusion.4), channel_id=1, source_target_pairs={{0,8},{1,9},{2,10},{3,11},{4,12},{5,13},{6,14},{7,15},{8,0},{9,1},... | collective-permute-start | bytes 884744 | tf_op jit(solution)/shard_map/ppermute | solution.py:54
  68.4 7.9 %collective-permute-start.25 = (bf16[576,256]{1,0:T(8,128)(2,1)S(1)}, bf16[576,256]{1,0:T(8,128)(2,1)S(1)}, u32[]{:S(2)}, u32[]{:S(2)}) collective-permute-start(bf16[576,256]{1,0:T(8,128)(2,1)S(1)} %add_convert_fusion.3), channel_id=1, source_target_pairs={{0,1},{1,2},{2,3},{3,4},{4,5},{5,6},{6,7},{7,0},{8,9},{9,10},{10,1... | collective-permute-start | bytes 884744 | tf_op jit(solution)/shard_map/ppermute | solution.py:46
  82.2 9.1 %collective-permute-start.29 = (bf16[576,256]{1,0:T(8,128)(2,1)S(1)}, bf16[576,256]{1,0:T(8,128)(2,1)S(1)}, u32[]{:S(2)}, u32[]{:S(2)}) collective-permute-start(bf16[576,256]{1,0:T(8,128)(2,1)S(1)} %add_convert_fusion), channel_id=1, source_target_pairs={{0,7},{1,0},{2,1},{3,2},{4,3},{5,4},{6,5},{7,6},{8,15},{9,8},{10,9... | collective-permute-start | bytes 884744 | tf_op jit(solution)/shard_map/ppermute | solution.py:50
  91.3 9.0 %collective-permute-start.30 = (f32[32,1280]{1,0:T(8,128)S(1)}, f32[32,1280]{1,0:T(8,128)S(1)}, u32[]{:S(2)}, u32[]{:S(2)}) collective-permute-start(f32[32,1280]{1,0:T(8,128)S(1)} %get-tuple-element.197), channel_id=1, source_target_pairs={{0,16},{16,0},{32,48},{48,32},{64,80},{80,64},{96,112},{112,96},{1... | collective-permute-start | bytes 491528 | tf_op jit(solution)/shard_map/ppermute | solution.py:500
  (20 other events, 120.0 us)
